TPU v7x, 512 devices: a whole 4x8x8 slice. The times are simulated.
512 devices in a mesh: strip: 128 (over y, z, core), grp: 4 (over x).
Axes of the slice: x: 4, y: 8, z: 8, core: 2. Of those that a mesh axis runs over, the one named last changes fastest.
Arguments:
- offsets: float32 [131072, 2, 128], P(('strip', 'grp')), may hold values from 0.5 to 14.5, as said below
- circulation: float32 [131072, 128], P(('strip', 'grp')), may hold values from -6 to 6
- window_anchor: float32 [131072, 2], P(('strip', 'grp')), may hold values from -8 to 8
- local_first: int32 [2, 131072], P(None, ('strip', 'grp')), may hold values from 0 to 255
- local_offset: int32 [2, 131072], P(None, ('strip', 'grp')), may hold values from 1 to 255
- cross_target: int32 [2, 131072], P(None, ('strip', 'grp')), may hold values from 0 to 255
- cross_source: int32 [2, 131072], P(None, ('strip', 'grp')), may hold values from 0 to 1023
- cross_count: int32 [2, 512], P(None, ('strip', 'grp')), may hold values from 16 to 256, as said below
- destination: int32 [2, 131072, 1], P(None, ('strip', 'grp')), may hold values from 0 to 127; in each aligned block of 256 rows (0 to 255, 256 to 511, ..., all dimensions but the last counted through in order) at most 2 rows name the same one
Outputs:
- final_circulation: float32 [131072, 128], P(('strip', 'grp'))
- final_anchor: float32 [131072, 2], P(('strip', 'grp'))
Inputs may be any that keep to these rules, and one draw needn't show every extreme that they name: `offsets`: first component between 0.5 and 8 - 1.5, second between 0.5 and 16 - 1.5. `cross_count`: 256 on at least one device in each step. `destination`: in each step every device names each strip for exactly 2 of its leaves.
All inputs are finite; a program needn't handle non-finite values.
Results may differ from a plain program's by a relative error of at most 0.0003.
Values sent between devices are 32-bit elements; how exact they have to be, the bound alone decides.
A program may use at most 64 MiB of HBM per device.

v0:
```python
import jax
import jax.numpy as jnp
from jax import lax
from jax.sharding import PartitionSpec as P

WX = 8
WY = 16
STEPS = 2


time_step = 0.5
smoothing = 1.0
biot_factor = 0.15915494309189535
pair_block = 8
remesh_block = 32


def from_behind(x, axis, by):
    peers = lax.axis_size(axis)
    return lax.ppermute(x, axis, [(i, (i + by) % peers) for i in range(peers)])


def remesh_kernel(distance):
    radius = jnp.abs(distance)
    inner_part = 1.0 - 2.5 * radius * radius + 1.5 * radius * radius * radius
    outer_part = 0.5 * (2.0 - radius) * (2.0 - radius) * (1.0 - radius)
    return jnp.where(radius < 1.0, inner_part, jnp.where(radius < 2.0, outer_part, 0.0))


def one_sided(targets, sources):
    delta_x = targets[:, 0, :, None] - sources[:, 0, None, :]
    delta_y = targets[:, 1, :, None] - sources[:, 1, None, :]
    weight = biot_factor / (delta_x * delta_x + delta_y * delta_y + smoothing)
    source_gamma = sources[:, 2, None, :]
    along_x = -jnp.sum(source_gamma * delta_y * weight, axis=2)
    along_y = jnp.sum(source_gamma * delta_x * weight, axis=2)
    return jnp.stack([along_x, along_y], axis=1)


def mutual(targets, sources):
    delta_x = targets[:, 0, :, None] - sources[:, 0, None, :]
    delta_y = targets[:, 1, :, None] - sources[:, 1, None, :]
    weight = biot_factor / (delta_x * delta_x + delta_y * delta_y + smoothing)
    tilt_x = delta_x * weight
    tilt_y = delta_y * weight
    source_gamma = sources[:, 2, None, :]
    target_gamma = targets[:, 2, :, None]
    on_targets = jnp.stack(
        [-jnp.sum(source_gamma * tilt_y, axis=2), jnp.sum(source_gamma * tilt_x, axis=2)], axis=1
    )
    on_sources = jnp.stack(
        [jnp.sum(target_gamma * tilt_y, axis=1), -jnp.sum(target_gamma * tilt_x, axis=1)], axis=1
    )
    return (on_targets, on_sources)


def self_field(packed):
    leaf_count = packed.shape[0]
    leaf_size = packed.shape[2]

    def block_self(block_rows):
        return one_sided(block_rows, block_rows)

    blocks = lax.map(block_self, packed.reshape(-1, pair_block, 3, leaf_size))
    return blocks.reshape(leaf_count, 2, leaf_size)


def pair_field(packed, firsts, seconds):
    leaf_size = packed.shape[2]

    def block_pairs(pieces):
        first_rows, second_rows = pieces
        return mutual(packed[first_rows], packed[second_rows])

    on_first, on_second = lax.map(
        block_pairs, (firsts.reshape(-1, pair_block), seconds.reshape(-1, pair_block))
    )
    return (on_first.reshape(-1, 2, leaf_size), on_second.reshape(-1, 2, leaf_size))


def cross_field(packed, remote, target_list, source_list, live_count):
    leaf_size = packed.shape[2]
    lanes = jnp.arange(pair_block, dtype=jnp.int32)

    def cross_turn(block_index, totals):
        own_part, far_part = totals
        block_start = block_index * pair_block
        targets = lax.dynamic_slice_in_dim(target_list, block_start, pair_block)
        sources = lax.dynamic_slice_in_dim(source_list, block_start, pair_block)
        live_mask = (block_start + lanes < live_count).astype(jnp.float32)[:, None, None]
        on_targets, on_sources = mutual(packed[targets], remote[sources])
        return (
            own_part.at[targets].add(on_targets * live_mask),
            far_part.at[sources].add(on_sources * live_mask),
        )

    rounds = (live_count + pair_block - 1) // pair_block
    own_zero = jnp.zeros((packed.shape[0], 2, leaf_size), jnp.float32)
    far_zero = jnp.zeros((remote.shape[0], 2, leaf_size), jnp.float32)
    return lax.fori_loop(0, rounds, cross_turn, (own_zero, far_zero))


def remesh_leaves(advected, strength):
    leaf_count = strength.shape[0]
    leaf_size = strength.shape[1]
    axis_x = jnp.arange(WX, dtype=jnp.float32)
    axis_y = jnp.arange(WY, dtype=jnp.float32)

    def block_nodes(pieces):
        part_moved, part_gamma = pieces
        weight_x = remesh_kernel(part_moved[:, 0, None, :] - axis_x[None, :, None])
        weight_y = remesh_kernel(part_moved[:, 1, None, :] - axis_y[None, :, None])
        grid_nodes = jnp.einsum(
            "lip,ljp->lij",
            weight_x * part_gamma[:, None, :],
            weight_y,
            precision=lax.Precision.HIGHEST,
        )
        return grid_nodes.reshape(part_gamma.shape[0], WX * WY)

    blocks = lax.map(
        block_nodes,
        (
            advected.reshape(-1, remesh_block, 2, leaf_size),
            strength.reshape(-1, remesh_block, leaf_size),
        ),
    )
    return blocks.reshape(leaf_count, leaf_size)


def regroup_order(destinations, strips, per_strip):
    leaf_count = destinations.shape[0]
    columns = lax.broadcasted_iota(jnp.int32, (leaf_count, strips), 1)
    onehot = (destinations[:, None] == columns).astype(jnp.int32)
    earlier = jnp.cumsum(onehot, axis=0) - onehot
    within = jnp.sum(earlier * onehot, axis=1)
    slot_index = destinations * per_strip + within
    return jnp.zeros_like(destinations).at[slot_index].set(jnp.arange(leaf_count, dtype=jnp.int32))


def on_device(
    offsets,
    circulation,
    window_anchor,
    local_first,
    local_offset,
    cross_target,
    cross_source,
    cross_count,
    destination,
):
    leaf_count = circulation.shape[0]
    leaf_size = circulation.shape[1]
    strips = lax.axis_size("strip")
    per_strip = leaf_count // strips
    particle_ids = jnp.arange(leaf_size, dtype=jnp.int32)
    node_grid = jnp.stack([particle_ids // WY, particle_ids % WY]).astype(jnp.float32)
    anchor = window_anchor
    shifted = offsets
    strength = circulation
    for step_index in range(STEPS):
        position = anchor[:, :, None] + shifted
        packed = jnp.concatenate([position, strength[:, None, :]], axis=1)
        velocity = self_field(packed)
        firsts = local_first[step_index]
        partners = (firsts + local_offset[step_index]) % leaf_count
        on_first, on_second = pair_field(packed, firsts, partners)
        velocity = velocity.at[firsts].add(on_first).at[partners].add(on_second)
        whole_strip = lax.all_gather(packed, "grp", axis=0, tiled=True)
        remote = from_behind(whole_strip, "strip", -1)
        own_part, far_part = cross_field(
            packed,
            remote,
            cross_target[step_index],
            cross_source[step_index],
            cross_count[step_index, 0],
        )
        arrived = from_behind(far_part, "strip", 1)
        returned = lax.psum_scatter(arrived, "grp", scatter_dimension=0, tiled=True)
        velocity = velocity + own_part + returned
        advected = shifted + time_step * velocity
        send_order = regroup_order(destination[step_index, :, 0], strips, per_strip)
        arrived_offsets, arrived_strength, anchor = (
            lax.all_to_all(advected[send_order], "strip", split_axis=0, concat_axis=0, tiled=True),
            lax.all_to_all(strength[send_order], "strip", split_axis=0, concat_axis=0, tiled=True),
            lax.all_to_all(anchor[send_order], "strip", split_axis=0, concat_axis=0, tiled=True),
        )
        strength = remesh_leaves(arrived_offsets, arrived_strength)
        shifted = jnp.broadcast_to(node_grid[None], advected.shape)
    return (strength, anchor)


def solution(mesh):
    return jax.shard_map(
        on_device,
        mesh=mesh,
        in_specs=(
            P(("strip", "grp"), None, None),
            P(("strip", "grp"), None),
            P(("strip", "grp"), None),
            P(None, ("strip", "grp")),
            P(None, ("strip", "grp")),
            P(None, ("strip", "grp")),
            P(None, ("strip", "grp")),
            P(None, ("strip", "grp")),
            P(None, ("strip", "grp"), None),
        ),
        out_specs=(P(("strip", "grp"), None), P(("strip", "grp"), None)),
        check_vma=False,
    )
```

profile of v0, /device:TPU:1, one launch (start us, length us, event | category | flops | bytes accessed | tf_op | source)
XLA Modules:
  0.0 881.4 jit_solution(665465701196091230)
XLA Ops:
  12.6 34.9 %all-gather.3.cloned.1.call-done = f32[1024,3,128]{2,0,1:T(8,128)} async-done(((f32[256,3,128]{2,0,1:T(8,128)}), f32[1024,3,128]{2,0,1:T(8,128)}) %all-gather.3.cloned.1.call-update) | async-done | bytes 1572880 | tf_op jit(solution)/shard_map/all_gather | solution.py:169
  53.1 13.7 %all-to-all-start = ((f32[128,2,2]{2,1,0:T(2,128)}), f32[128,2,2]{2,1,0:T(2,128)S(1)}, u32[]{:S(2)}, u32[]{:S(2)}) async-start(f32[128,2,2]{2,1,0:T(2,128)} %bitcast.54), calls=%async_computation | async-start | bytes 262144 | tf_op jit(solution)/shard_map/all_to_all | solution.py:186
  74.0 28.0 %while.96 = (s32[]{:T(128)}, f32[256,2,128]{2,1,0:T(2,128)S(1)}, f32[1024,2,128]{2,1,0:T(2,128)}, s32[]{:T(128)}, s32[256]{0:T(256)S(1)}, /*index=5*/s32[256]{0:...) while((s32[]{:T(128)}, f32[256,2,128]{2,1,0:T(2,128)S(1)}, ...), condition=%wide.region_15.16_spmd.clone, body=%wide.region_8.15_spmd.clone.sunk | while | flops 2240590 | bytes 279095 | solution.py:100
  102.0 25.7 %collective-permute-start.1 = (f32[1024,2,128]{2,1,0:T(2,128)}, f32[1024,2,128]{2,1,0:T(2,128)S(1)}, u32[]{:S(2)}, u32[]{:S(2)}) collective-permute-start(f32[1024,2,128]{2,1,0:T(2,128)} %get-tuple-element.276), channel_id=1, source_target_pairs={{0,4},{4,8},{8,12},{12,16},{16,20},{20,24},{24,28},{28,32},{32,36}... | collective-permute-start | bytes 3145736 | tf_op jit(solution)/shard_map/ppermute | solution.py:20
  127.8 68.4 %while.93 = (s32[]{:T(128)}, f32[32,8,2,128]{3,2,1,0:T(2,128)S(1)}, f32[32,8,2,128]{3,2,1,0:T(2,128)S(1)}, s32[32,8]{1,0:T(8,128)S(1)}, f32[256,3,128]{2,1,0:T(4,128)S(1)}, /*index=5*/s32[32,8]{1,0:T(8,128)S(1)}, s32[]{:T(128)}) while((s32[]{:T(128)}, f32[32,8,2,128]{3,2,1,0:T(2,128)S(1)}, f32[32,8,2,128]{3,2,1,0:T(2,128)S(1)}, ...), condition=%wide.region_22.23_spmd, body=%wide.region_17.22_spmd.sunk | while | flops 2232370 | bytes 229721 | solution.py:75
  196.4 11.8 %collective-permute-done.1 = f32[1024,2,128]{2,1,0:T(2,128)S(1)} collective-permute-done((f32[1024,2,128]{2,1,0:T(2,128)}, f32[1024,2,128]{2,1,0:T(2,128)S(1)}, u32[]{:S(2)}, u32[]{:S(2)}) %collective-permute-start.1) | collective-permute-done | bytes 1048608 | tf_op jit(solution)/shard_map/ppermute | solution.py:20
  209.3 24.2 %while.92 = (s32[]{:T(128)}, f32[32,8,2,128]{3,2,1,0:T(2,128)S(1)}, f32[32,8,3,128]{3,1,2,0:T(8,128)S(1)}, s32[]{:T(128)}) while((s32[]{:T(128)}, f32[32,8,2,128]{3,2,1,0:T(2,128)S(1)}, f32[32,8,3,128]{3,1,2,0:T(8,128)S(1)}, s32[]{:T(128)}) %tuple.255), condition=%wide.region_7.8_spmd, body=%wide.region_4.7_spmd.sunk | while | flops 1704962 | bytes 110653 | solution.py:64
  237.2 126.1 %all-to-all-start.2 = ((f32[128,2,128]{2,1,0:T(2,128)}), f32[128,2,128]{2,1,0:T(2,128)S(1)}, u32[]{:S(2)}, u32[]{:S(2)}) async-start(f32[128,2,128]{2,1,0:T(2,128)} %bitcast.70), calls=%async_computation.2 | async-start | bytes 262144 | tf_op jit(solution)/shard_map/all_to_all | solution.py:185
  363.3 17.3 %all-reduce.5.cloned.1.call-done = f32[1024,2,128]{2,1,0:T(2,128)} async-done(((f32[1024,2,128]{2,1,0:T(2,128)}), f32[1024,2,128]{2,1,0:T(2,128)}) %all-reduce.5.cloned.1.call-update) | async-done | bytes 1048592
  381.8 8.3 scatter_fusion.4
  400.3 15.3 %all-to-all-start.1 = ((f32[256,2,128]{2,1,0:T(2,128)}), f32[256,2,128]{2,1,0:T(2,128)S(1)}, u32[]{:S(2)}, u32[]{:S(2)}) async-start(f32[256,2,128]{2,1,0:T(2,128)} %gather_fusion.9), calls=%async_computation.1 | async-start | bytes 524288 | tf_op jit(solution)/shard_map/all_to_all | solution.py:184
  416.0 13.8 %all-to-all-done.1 = f32[256,2,128]{2,1,0:T(2,128)S(1)} async-done(((f32[256,2,128]{2,1,0:T(2,128)}), f32[256,2,128]{2,1,0:T(2,128)S(1)}, u32[]{:S(2)}, u32[]{:S(2)}) %all-to-all-start.1) | async-done | bytes 262176 | tf_op jit(solution)/shard_map/all_to_all | solution.py:184
  438.8 24.8 %all-gather.5.cloned.1.call-done = f32[1024,3,128]{2,0,1:T(8,128)} async-done(((f32[256,3,128]{2,0,1:T(8,128)}), f32[1024,3,128]{2,0,1:T(8,128)}) %all-gather.5.cloned.1.call-update) | async-done | bytes 1572880 | tf_op jit(solution)/shard_map/all_gather | solution.py:169
  471.6 13.7 %all-to-all-start.5 = ((f32[128,2,2]{1,2,0:T(2,128)}), f32[128,2,2]{1,2,0:T(2,128)S(1)}, u32[]{:S(2)}, u32[]{:S(2)}) async-start(f32[128,2,2]{1,2,0:T(2,128)} %copy.137), calls=%async_computation.5 | async-start | bytes 262144 | tf_op jit(solution)/shard_map/all_to_all | solution.py:186
  489.6 73.2 %while.98 = (s32[]{:T(128)}, f32[256,2,128]{2,1,0:T(2,128)S(1)}, f32[1024,2,128]{2,1,0:T(2,128)}, s32[]{:T(128)}, s32[256]{0:T(256)S(1)}, /*index=5*/s32[256]{0:...) while((s32[]{:T(128)}, f32[256,2,128]{2,1,0:T(2,128)S(1)}, ...), condition=%wide.region_38.39_spmd.clone, body=%wide.region_31.38_spmd.clone.sunk | while | flops 2240590 | bytes 279095 | solution.py:100
  562.9 14.7 %collective-permute-start.3 = (f32[1024,2,128]{2,1,0:T(2,128)}, f32[1024,2,128]{2,1,0:T(2,128)S(1)}, u32[]{:S(2)}, u32[]{:S(2)}) collective-permute-start(f32[1024,2,128]{2,1,0:T(2,128)} %get-tuple-element.282), channel_id=1, source_target_pairs={{0,4},{4,8},{8,12},{12,16},{16,20},{20,24},{24,28},{28,32},{32,36}... | collective-permute-start | bytes 3145736 | tf_op jit(solution)/shard_map/ppermute | solution.py:20
  577.8 90.0 %while.95 = (s32[]{:T(128)}, f32[32,8,2,128]{3,2,1,0:T(2,128)S(1)}, f32[32,8,2,128]{3,2,1,0:T(2,128)S(1)}, s32[32,8]{1,0:T(8,128)}, f32[256,3,128]{2,1,0:T(4,128)S(1)}, /*index=5*/s32[32,8]{1,0:T(8,128)S(1)}, s32[]{:T(128)}) while((s32[]{:T(128)}, f32[32,8,2,128]{3,2,1,0:T(2,128)S(1)}, f32[32,8,2,128]{3,2,1,0:T(2,128)S(1)}, ...), condition=%wide.region_45.46_spmd, body=%wide.region_40.45_spmd.sunk | while | flops 2232370 | bytes 229721 | solution.py:75
  668.9 24.2 %while.94 = (s32[]{:T(128)}, f32[32,8,2,128]{3,2,1,0:T(2,128)S(1)}, f32[32,8,3,128]{3,1,2,0:T(8,128)S(1)}, s32[]{:T(128)}) while((s32[]{:T(128)}, f32[32,8,2,128]{3,2,1,0:T(2,128)S(1)}, f32[32,8,3,128]{3,1,2,0:T(8,128)S(1)}, s32[]{:T(128)}) %tuple.267), condition=%wide.region_30.31_spmd, body=%wide.region_27.30_spmd.sunk | while | flops 1704962 | bytes 110653 | solution.py:64
  694.4 102.3 %all-to-all-start.4 = ((f32[128,2,128]{2,1,0:T(2,128)}), f32[128,2,128]{2,1,0:T(2,128)S(1)}, u32[]{:S(2)}, u32[]{:S(2)}) async-start(f32[128,2,128]{2,1,0:T(2,128)} %bitcast.96), calls=%async_computation.4 | async-start | bytes 262144 | tf_op jit(solution)/shard_map/all_to_all | solution.py:185
  796.7 20.4 %all-reduce.7.cloned.1.call-done = f32[1024,2,128]{2,1,0:T(2,128)} async-done(((f32[1024,2,128]{2,1,0:T(2,128)}), f32[1024,2,128]{2,1,0:T(2,128)}) %all-reduce.7.cloned.1.call-update) | async-done | bytes 1048592
  818.3 8.3 scatter_fusion.6
  826.6 8.3 scatter_fusion.7
  836.8 15.3 %all-to-all-start.3 = ((f32[256,2,128]{2,1,0:T(2,128)}), f32[256,2,128]{2,1,0:T(2,128)S(1)}, u32[]{:S(2)}, u32[]{:S(2)}) async-start(f32[256,2,128]{2,1,0:T(2,128)} %gather_fusion.11), calls=%async_computation.3 | async-start | bytes 524288 | tf_op jit(solution)/shard_map/all_to_all | solution.py:184
  852.9 13.5 %all-to-all-done.3 = f32[256,2,128]{2,1,0:T(2,128)S(1)} async-done(((f32[256,2,128]{2,1,0:T(2,128)}), f32[256,2,128]{2,1,0:T(2,128)S(1)}, u32[]{:S(2)}, u32[]{:S(2)}) %all-to-all-start.3) | async-done | bytes 262176 | tf_op jit(solution)/shard_map/all_to_all | solution.py:184
  (1838 shorter events, 380.9 us)
Async XLA Ops:
  7.2 40.3 %all-gather.3.cloned.1.call-start = ((), (), s32[]{:S(2)}) async-start(), calls=%async_computation.6 | async-start | bytes 1966080 | tf_op jit(solution)/shard_map/all_gather | solution.py:169
  10.0 58.2 %copy-start.1 = (f32[256,3,128]{2,0,1:T(8,128)S(1)}, f32[256,3,128]{2,0,1:T(8,128)}, u32[]{:S(2)}) copy-start(f32[256,3,128]{2,0,1:T(8,128)} %pad_maximum_fusion.2) | copy-start | bytes 1179652
  11.9 57.3 %copy-start.19 = (s32[2,256]{1,0:T(2,128)S(1)}, s32[2,256]{1,0:T(2,128)}, u32[]{:S(2)}) copy-start(s32[2,256]{1,0:T(2,128)} %param.31) | copy-start | bytes 6148
  47.5 22.6 %collective-permute-start = (f32[1024,3,128]{2,0,1:T(8,128)}, f32[1024,3,128]{2,0,1:T(8,128)}, u32[]{:S(2)}, u32[]{:S(2)}) collective-permute-start(f32[1024,3,128]{2,0,1:T(8,128)} %all-gather.3.cloned.1.call-done), channel_id=1, source_target_pairs={{0,508},{4,0},{8,4},{12,8},{16,12},{20,16},{24,20},{28,24},{32,28}... | collective-permute-start | bytes 4718600 | tf_op jit(solution)/shard_map/ppermute | solution.py:20
  53.1 184.2 %all-to-all-start = ((f32[128,2,2]{2,1,0:T(2,128)}), f32[128,2,2]{2,1,0:T(2,128)S(1)}, u32[]{:S(2)}, u32[]{:S(2)}) async-start(f32[128,2,2]{2,1,0:T(2,128)} %bitcast.54), calls=%async_computation | async-start | bytes 262144 | tf_op jit(solution)/shard_map/all_to_all | solution.py:186
  66.8 313.8 %all-reduce.5.cloned.1.call-start = ((), (), s32[]{:S(2)}) async-start(), calls=%async_computation.8 | async-start | bytes 2097152
  74.0 122.3 %copy-start = (f32[256,128]{1,0:T(8,128)S(1)}, f32[256,128]{1,0:T(8,128)}, u32[]{:S(2)}) copy-start(f32[256,128]{1,0:T(8,128)} %param.26) | copy-start | bytes 393220
  74.0 122.3 %copy-start.2 = (f32[256,2,128]{2,1,0:T(2,128)S(1)}, f32[256,2,128]{2,1,0:T(2,128)}, u32[]{:S(2)}) copy-start(f32[256,2,128]{2,1,0:T(2,128)} %param.25) | copy-start | bytes 786436
  74.0 122.3 %copy-start.6 = (f32[256,2]{0,1:T(2,128)S(1)}, f32[256,2]{0,1:T(2,128)}, u32[]{:S(2)}) copy-start(f32[256,2]{0,1:T(2,128)} %param.27) | copy-start | bytes 6148
  102.0 106.2 %collective-permute-start.1 = (f32[1024,2,128]{2,1,0:T(2,128)}, f32[1024,2,128]{2,1,0:T(2,128)S(1)}, u32[]{:S(2)}, u32[]{:S(2)}) collective-permute-start(f32[1024,2,128]{2,1,0:T(2,128)} %get-tuple-element.276), channel_id=1, source_target_pairs={{0,4},{4,8},{8,12},{12,16},{16,20},{20,24},{24,28},{28,32},{32,36}... | collective-permute-start | bytes 3145736 | tf_op jit(solution)/shard_map/ppermute | solution.py:20
  237.2 163.1 %all-to-all-start.2 = ((f32[128,2,128]{2,1,0:T(2,128)}), f32[128,2,128]{2,1,0:T(2,128)S(1)}, u32[]{:S(2)}, u32[]{:S(2)}) async-start(f32[128,2,128]{2,1,0:T(2,128)} %bitcast.70), calls=%async_computation.2 | async-start | bytes 262144 | tf_op jit(solution)/shard_map/all_to_all | solution.py:185
  400.3 29.5 %all-to-all-start.1 = ((f32[256,2,128]{2,1,0:T(2,128)}), f32[256,2,128]{2,1,0:T(2,128)S(1)}, u32[]{:S(2)}, u32[]{:S(2)}) async-start(f32[256,2,128]{2,1,0:T(2,128)} %gather_fusion.9), calls=%async_computation.1 | async-start | bytes 524288 | tf_op jit(solution)/shard_map/all_to_all | solution.py:184
  415.6 47.9 %all-gather.5.cloned.1.call-start = ((), (), s32[]{:S(2)}) async-start(), calls=%async_computation.7 | async-start | bytes 1966080 | tf_op jit(solution)/shard_map/all_gather | solution.py:169
  415.7 69.7 %copy-start.7 = (f32[2,128]{1,0:T(2,128)}, f32[2,128]{1,0:T(2,128)S(1)}, u32[]{:S(2)}) copy-start(f32[2,128]{1,0:T(2,128)S(1)} %add_convert_fusion) | copy-start | bytes 3076
  463.5 22.2 %collective-permute-start.2 = (f32[1024,3,128]{2,0,1:T(8,128)}, f32[1024,3,128]{2,0,1:T(8,128)}, u32[]{:S(2)}, u32[]{:S(2)}) collective-permute-start(f32[1024,3,128]{2,0,1:T(8,128)} %all-gather.5.cloned.1.call-done), channel_id=1, source_target_pairs={{0,508},{4,0},{8,4},{12,8},{16,12},{20,16},{24,20},{28,24},{32,28}... | collective-permute-start | bytes 4718600 | tf_op jit(solution)/shard_map/ppermute | solution.py:20
  471.6 222.9 %all-to-all-start.5 = ((f32[128,2,2]{1,2,0:T(2,128)}), f32[128,2,2]{1,2,0:T(2,128)S(1)}, u32[]{:S(2)}, u32[]{:S(2)}) async-start(f32[128,2,2]{1,2,0:T(2,128)} %copy.137), calls=%async_computation.5 | async-start | bytes 262144 | tf_op jit(solution)/shard_map/all_to_all | solution.py:186
  485.3 331.8 %all-reduce.7.cloned.1.call-start = ((), (), s32[]{:S(2)}) async-start(), calls=%async_computation.9 | async-start | bytes 2097152
  562.9 104.9 %collective-permute-start.3 = (f32[1024,2,128]{2,1,0:T(2,128)}, f32[1024,2,128]{2,1,0:T(2,128)S(1)}, u32[]{:S(2)}, u32[]{:S(2)}) collective-permute-start(f32[1024,2,128]{2,1,0:T(2,128)} %get-tuple-element.282), channel_id=1, source_target_pairs={{0,4},{4,8},{8,12},{12,16},{16,20},{20,24},{24,28},{28,32},{32,36}... | collective-permute-start | bytes 3145736 | tf_op jit(solution)/shard_map/ppermute | solution.py:20
  577.7 115.3 %copy-start.12 = (s32[1024]{0:T(1024)S(1)}, s32[1024]{0:T(1024)}, u32[]{:S(2)}) copy-start(s32[1024]{0:T(1024)} %copy-done.11) | copy-start | bytes 12292
  667.8 150.5 %copy-start.17 = (s32[256,1]{0,1:T(1,128)S(1)}, s32[256,1]{0,1:T(1,128)}, u32[]{:S(2)}) copy-start(s32[256,1]{0,1:T(1,128)} %get-tuple-element.639) | copy-start | bytes 3076
  668.8 157.8 %copy-start.16 = (s32[256,1]{0,1:T(1,128)S(1)}, s32[256,1]{0,1:T(1,128)}, u32[]{:S(2)}) copy-start(s32[256,1]{0,1:T(1,128)} %get-tuple-element.632) | copy-start | bytes 3076
  693.1 141.9 %copy-start.8 = (f32[2,128]{1,0:T(2,128)S(1)}, f32[2,128]{1,0:T(2,128)}, u32[]{:S(2)}) copy-start(f32[2,128]{1,0:T(2,128)} %copy-done.7) | copy-start | bytes 3076
  694.4 142.3 %all-to-all-start.4 = ((f32[128,2,128]{2,1,0:T(2,128)}), f32[128,2,128]{2,1,0:T(2,128)S(1)}, u32[]{:S(2)}, u32[]{:S(2)}) async-start(f32[128,2,128]{2,1,0:T(2,128)} %bitcast.96), calls=%async_computation.4 | async-start | bytes 262144 | tf_op jit(solution)/shard_map/all_to_all | solution.py:185
  836.8 29.6 %all-to-all-start.3 = ((f32[256,2,128]{2,1,0:T(2,128)}), f32[256,2,128]{2,1,0:T(2,128)S(1)}, u32[]{:S(2)}, u32[]{:S(2)}) async-start(f32[256,2,128]{2,1,0:T(2,128)} %gather_fusion.11), calls=%async_computation.3 | async-start | bytes 524288 | tf_op jit(solution)/shard_map/all_to_all | solution.py:184
  (11 other events, 301.1 us)
Sparse Core Ops, SparseCore 0:
  10.1 37.3 all-gather.2
  209.4 171.2 all-reduce.4
  438.9 24.6 all-gather.4
  668.9 148.1 all-reduce.6
where the time goes:
time: 885 us; the launch traced here: 881 us
  starting transfers between devices  332 us (38%)
  other arithmetic  239 us (27%)
  waiting for transfers between devices  137 us (15%)
  local copies, waits for them, and re-layouts  133 us (15%)
  between operations  16.5 us (2%)
  matrix products  11.8 us (1%)
  loops' own time  11.5 us (1%)
    all_to_all x2, starting transfers between devices, on_device(): lax.all_to_all(strength[send_order], 'strip', split_axis=0, concat_axis=0...  228 us
    gather x128, local copies, waits for them, and re-layouts, block_pairs(): return mutual(packed[first_rows], packed[second_rows])  73.6 us
    reduce_sum x82, other arithmetic, mutual(): jnp.sum(target_gamma * tilt_y, axis=1)  65.2 us
    all_gather x2, waiting for transfers between devices, on_device(): whole_strip = lax.all_gather(packed, 'grp', axis=0, tiled=True)  59.6 us
    ppermute x4, starting transfers between devices, from_behind(): return lax.ppermute(x, axis, [(i, (i + by) % peers) for i in range(peers)])  45.5 us
    reduce_sum x64, other arithmetic, one_sided(): along_x = -jnp.sum(source_gamma * delta_y * weight, axis=2)  42.4 us
    unnamed x6, waiting for transfers between devices  37.8 us
    scatter-add x18, other arithmetic, cross_turn(): far_part.at[sources].add(on_sources * live_mask)  34.7 us
  transfers between devices with their start and end apart: 14, of which 9 were waited for; matrix products, arithmetic and copies ran while one was open for 41% of the time, Pallas kernels for 0%

commit v1 on v0

v1 whole, which is shorter than its diff:
```python
import functools
import jax
import jax.numpy as jnp
import numpy as np
from jax import lax
from jax.experimental import pallas as pl
from jax.experimental.pallas import tpu as pltpu
from jax.sharding import PartitionSpec as P

WX = 8
WY = 16
STEPS = 2
time_step = 0.5
biot_factor = 0.15915494309189535
LANES = 128
f32 = jnp.float32
bf16 = jnp.bfloat16


def recip(x):
    return pl.reciprocal(x, approx=True)


def mutual_lanes(a_refs, b_refs, on_a, on_b):
    xa_ref, ya_ref, ga_ref = a_refs
    xb_ref, yb_ref, gb_ref = b_refs
    ua_ref, va_ref = on_a
    ub_ref, vb_ref = on_b
    ub_ref[...] = jnp.zeros_like(ub_ref)
    vb_ref[...] = jnp.zeros_like(vb_ref)
    zero = jnp.zeros((8, LANES), f32)

    def over_a(ia, carry):
        a0 = pl.multiple_of(ia * 8, 8)

        def over_b(ib, acc):
            acc = list(acc)
            rows = pl.ds(pl.multiple_of(ib * 8, 8), 8)
            xb, yb, gb = xb_ref[rows, :], yb_ref[rows, :], gb_ref[rows, :]
            ub, vb = ub_ref[rows, :], vb_ref[rows, :]
            for r in range(8):
                row = pl.ds(a0 + r, 1)
                dx = xa_ref[row, :] - xb
                dy = ya_ref[row, :] - yb
                w = recip(dx * dx + dy * dy + 1.0)
                tx = dx * w
                ty = dy * w
                acc[r] = acc[r] + gb * ty
                acc[8 + r] = acc[8 + r] + gb * tx
                ga = ga_ref[row, :]
                ub = ub + ga * ty
                vb = vb + ga * tx
            ub_ref[rows, :] = ub
            vb_ref[rows, :] = vb
            return tuple(acc)

        acc = lax.fori_loop(0, 16, over_b, (zero,) * 16)
        for r in range(8):
            ua_ref[pl.ds(a0 + r, 1), :] = jnp.sum(acc[r], axis=0, keepdims=True)
            va_ref[pl.ds(a0 + r, 1), :] = jnp.sum(acc[8 + r], axis=0, keepdims=True)
        return carry

    lax.fori_loop(0, 16, over_a, 0)


def self_lanes(a_refs, on_a):
    xa_ref, ya_ref, ga_ref = a_refs
    ua_ref, va_ref = on_a
    zero = jnp.zeros((8, LANES), f32)

    def over_a(ia, carry):
        a0 = pl.multiple_of(ia * 8, 8)

        def over_b(ib, acc):
            acc = list(acc)
            rows = pl.ds(pl.multiple_of(ib * 8, 8), 8)
            xb, yb, gb = xa_ref[rows, :], ya_ref[rows, :], ga_ref[rows, :]
            for r in range(8):
                row = pl.ds(a0 + r, 1)
                dx = xa_ref[row, :] - xb
                dy = ya_ref[row, :] - yb
                w = gb * recip(dx * dx + dy * dy + 1.0)
                acc[r] = acc[r] + dy * w
                acc[8 + r] = acc[8 + r] + dx * w
            return tuple(acc)

        acc = lax.fori_loop(0, 16, over_b, (zero,) * 16)
        for r in range(8):
            ua_ref[pl.ds(a0 + r, 1), :] = jnp.sum(acc[r], axis=0, keepdims=True)
            va_ref[pl.ds(a0 + r, 1), :] = jnp.sum(acc[8 + r], axis=0, keepdims=True)
        return carry

    lax.fori_loop(0, 16, over_a, 0)


def loop8(count, body):
    def eight(k, carry):
        for u in range(8):
            body(k * 8 + u)
        return carry

    lax.fori_loop(0, count // 8, eight, 0)


def rank_order(dest_ref, order_ref, count_ref, step):
    leaves = order_ref.shape[1]
    per_strip = 2

    def clear(k):
        count_ref[k] = 0

    def place(leaf):
        t = dest_ref[step, leaf]
        r = count_ref[t]
        count_ref[t] = r + 1
        order_ref[step, t * per_strip + r] = leaf

    loop8(leaves // per_strip, clear)
    loop8(leaves, place)


def local_kernel(state_ref, first_ref, second_ref, dest_ref, vel_ref, order_ref, ta, tb, ra, rb, oa, ob, count_ref):
    leaves = state_ref.shape[1]
    groups = leaves // LANES
    a_refs = [ta.at[c] for c in range(3)]
    b_refs = [tb.at[c] for c in range(3)]
    on_a = [oa.at[c] for c in range(2)]
    on_b = [ob.at[c] for c in range(2)]
    for step in range(STEPS):
        rank_order(dest_ref, order_ref, count_ref, step)

    def self_group(i, carry):
        rows = pl.ds(pl.multiple_of(i * LANES, LANES), LANES)
        for c in range(3):
            ta[c] = state_ref[c, rows, :].T
        self_lanes(a_refs, on_a)
        vel_ref[0, rows, :] = oa[0].T * -biot_factor
        vel_ref[1, rows, :] = oa[1].T * biot_factor
        return carry

    lax.fori_loop(0, groups, self_group, 0)

    def pair_group(i, carry):
        base = i * LANES

        def fetch(k):
            first = first_ref[base + k]
            second = second_ref[base + k]
            for c in range(3):
                ra[c, pl.ds(k, 1), :] = state_ref[c, pl.ds(first, 1), :]
                rb[c, pl.ds(k, 1), :] = state_ref[c, pl.ds(second, 1), :]

        loop8(LANES, fetch)
        for c in range(3):
            ta[c] = ra[c].T
            tb[c] = rb[c].T
        mutual_lanes(a_refs, b_refs, on_a, on_b)
        ra[0] = oa[0].T * -biot_factor
        ra[1] = oa[1].T * biot_factor
        rb[0] = ob[0].T * biot_factor
        rb[1] = ob[1].T * -biot_factor

        def spread(k):
            first = first_ref[base + k]
            second = second_ref[base + k]
            for c in range(2):
                vel_ref[c, pl.ds(first, 1), :] += ra[c, pl.ds(k, 1), :]
                vel_ref[c, pl.ds(second, 1), :] += rb[c, pl.ds(k, 1), :]

        loop8(LANES, spread)
        return carry

    lax.fori_loop(0, first_ref.shape[0] // LANES, pair_group, 0)


def cross_kernel(state_ref, far_ref, vel_in_ref, target_ref, source_ref, live_ref, vel_ref, part_ref, ta, tb, ra, rb, oa, ob):
    leaves = state_ref.shape[1]
    a_refs = [ta.at[c] for c in range(3)]
    b_refs = [tb.at[c] for c in range(3)]
    on_a = [oa.at[c] for c in range(2)]
    on_b = [ob.at[c] for c in range(2)]
    vel_ref[...] = vel_in_ref[...]
    part_ref[...] = jnp.zeros_like(part_ref)
    live = live_ref[0]

    def pair_group(i, carry):
        base = i * LANES

        def fetch(k):
            target = target_ref[base + k]
            source = source_ref[base + k]
            block = source // leaves
            row = source % leaves
            for c in range(3):
                ra[c, pl.ds(k, 1), :] = state_ref[c, pl.ds(target, 1), :]
                rb[c, pl.ds(k, 1), :] = far_ref[block, c, pl.ds(row, 1), :]

        loop8(LANES, fetch)
        for c in range(3):
            ta[c] = ra[c].T
            tb[c] = rb[c].T
        mutual_lanes(a_refs, b_refs, on_a, on_b)
        ra[0] = oa[0].T * -biot_factor
        ra[1] = oa[1].T * biot_factor
        rb[0] = ob[0].T * biot_factor
        rb[1] = ob[1].T * -biot_factor

        def spread(k, carry):
            target = target_ref[base + k]
            source = source_ref[base + k]
            block = source // leaves
            row = source % leaves
            for c in range(2):
                vel_ref[c, pl.ds(target, 1), :] += ra[c, pl.ds(k, 1), :]
                part_ref[block, c, pl.ds(row, 1), :] += rb[c, pl.ds(k, 1), :]
            return carry

        lax.fori_loop(0, jnp.minimum(live - base, LANES), spread, 0)
        return carry

    lax.fori_loop(0, (live + LANES - 1) // LANES, pair_group, 0)


def node_weight(distance):
    r = jnp.abs(distance)
    inner = 1.0 + r * r * (1.5 * r - 2.5)
    s = jnp.maximum(2.0 - r, 0.0)
    outer = (0.5 * s) * s * (1.0 - r)
    return jnp.where(r < 1.0, inner, outer)


def remesh_lanes(px_ref, py_ref, g_ref, wx_ref, nodes_ref):
    ix = lax.broadcasted_iota(jnp.int32, (WX, LANES), 0).astype(f32)
    iy = lax.broadcasted_iota(jnp.int32, (WX, LANES), 0).astype(f32)

    def over_p(p4, acc):
        acc = list(acc)
        for u in range(2):
            p = p4 * 2 + u
            row = pl.ds(p, 1)
            wx_ref[u] = node_weight(px_ref[row, :] - ix) * g_ref[row, :]
            y = py_ref[row, :] - iy
            wy = (node_weight(y), node_weight(y - 8.0))
            for i in range(WX):
                wxi = wx_ref[u, i : i + 1, :]
                for h in range(2):
                    acc[2 * i + h] = acc[2 * i + h] + wxi * wy[h]
        return tuple(acc)

    acc = lax.fori_loop(0, LANES // 2, over_p, (jnp.zeros((8, LANES), f32),) * 16)
    for i in range(16):
        nodes_ref[8 * i : 8 * i + 8, :] = acc[i]


def remesh_kernel(vel_ref, arrived_ref, shift_ref, g_ref, nodes_ref, px, py, pg, wx, out):
    leaves = g_ref.shape[0]
    blocks = arrived_ref.shape[0]

    def group(i, carry):
        rows = pl.ds(pl.multiple_of(i * LANES, LANES), LANES)
        for c, dst in ((0, px), (1, py)):
            total = vel_ref[c, rows, :]
            for b in range(blocks):
                total = total + arrived_ref[b, c, rows, :]
            dst[...] = (shift_ref[c, rows, :] + time_step * total).T
        pg[...] = g_ref[rows, :].T
        remesh_lanes(px, py, pg, wx, out)
        nodes_ref[rows, :] = out[...].T
        return carry

    lax.fori_loop(0, leaves // LANES, group, 0)


def split(x):
    hi = x.astype(bf16)
    return hi, (x - hi.astype(f32)).astype(bf16)


def dot3(x, m_hi, m_lo):
    hi, lo = split(x)
    d = functools.partial(jnp.dot, preferred_element_type=f32)
    return d(hi, m_hi) + (d(hi, m_lo) + d(lo, m_hi))


@functools.cache
def fourier_tables():
    n1, n2 = 2 * WX - 1, 2 * WY - 1
    size = n1 * n2
    u = np.arange(n1)
    v = np.arange(n2)
    di = np.where(u < WX, u, u - n1)
    dj = np.where(v < WY, v, v - n2)
    DI, DJ = [t.reshape(-1).astype(np.float64) for t in np.meshgrid(di, dj, indexing="ij")]
    k1, k2 = [t.reshape(-1) for t in np.meshgrid(u, v, indexing="ij")]
    keep = [0]
    for m in range(1, size):
        mirror = ((-k1[m]) % n1) * n2 + ((-k2[m]) % n2)
        if m < mirror:
            keep.append(m)
    f1, f2 = k1[keep].astype(np.float64), k2[keep].astype(np.float64)
    nf = len(keep)

    def phase(i, j):
        return 2 * np.pi * (np.outer(i, f1) / n1 + np.outer(j, f2) / n2)

    forward = np.zeros((512, 512))
    p = phase(DI, DJ)
    forward[:size, :nf] = np.cos(p)
    forward[:size, 256 : 256 + nf] = -np.sin(p)
    node = np.arange(WX * WY)
    q = phase(node // WY, node % WY)
    gamma = np.zeros((128, 512))
    gamma[:, :nf] = np.cos(q)
    gamma[:, 256 : 256 + nf] = -np.sin(q)
    weight = np.full(nf, 2.0 / size)
    weight[0] = 1.0 / size
    inverse = np.zeros((512, 128))
    inverse[:nf] = weight[:, None] * np.cos(q).T
    inverse[256 : 256 + nf] = -weight[:, None] * np.sin(q).T
    lattice = np.zeros((8, 512))
    lattice[0, :size] = DI
    lattice[1, :size] = DJ
    ddx = (node // WY)[:, None] - (node // WY)[None, :]
    ddy = (node % WY)[:, None] - (node % WY)[None, :]
    w = biot_factor / (ddx * ddx + ddy * ddy + 1.0)
    own = np.concatenate([(-ddy * w).T, (ddx * w).T], axis=1)

    def halves(x):
        hi = x.astype(np.float32).astype(bf16)
        lo = (x - hi.astype(np.float64)).astype(np.float32).astype(bf16)
        return np.stack([hi, lo])

    return halves(forward), halves(gamma), halves(inverse), lattice.astype(np.float32), halves(own)


def pair_waves(ga, gb, gap, fwd, gam, inv, lat):
    x = gap[:, 0:1] + lat[0:1, :]
    y = gap[:, 64:65] + lat[1:2, :]
    w = biot_factor * recip(x * x + y * y + 1.0)
    kx = dot3(-y * w, fwd[0], fwd[1])
    ky = dot3(x * w, fwd[0], fwd[1])
    wa = dot3(ga, gam[0], gam[1])
    wb = dot3(gb, gam[0], gam[1])
    ar, ai = wa[:, :256], wa[:, 256:]
    br, bi = wb[:, :256], wb[:, 256:]
    on_a, on_b = [], []
    for k in (kx, ky):
        kr, ki = k[:, :256], k[:, 256:]
        on_a.append(dot3(jnp.concatenate([kr * br - ki * bi, kr * bi + ki * br], axis=1), inv[0], inv[1]))
        on_b.append(dot3(jnp.concatenate([kr * ar + ki * ai, kr * ai - ki * ar], axis=1), inv[0], inv[1]))
    return on_a, on_b


def local_waves(g_ref, anc_ref, first_ref, second_ref, fwd_ref, gam_ref, inv_ref, lat_ref, own_ref, vel_ref, ra, rb, rd):
    own = dot3(g_ref[...], own_ref[0], own_ref[1])
    vel_ref[0] = own[:, :128]
    vel_ref[1] = own[:, 128:]
    rows = ra.shape[1]

    def pair_group(i, carry):
        base = i * rows

        def fetch(k):
            first = pl.ds(first_ref[base + k], 1)
            second = pl.ds(second_ref[base + k], 1)
            row = pl.ds(k, 1)
            ra[0, row, :] = g_ref[first, :]
            rb[0, row, :] = g_ref[second, :]
            rd[row, :] = anc_ref[first, :] - anc_ref[second, :]

        loop8(rows, fetch)
        on_a, on_b = pair_waves(ra[0], rb[0], rd[...], fwd_ref, gam_ref, inv_ref, lat_ref)
        for c in range(2):
            ra[c] = on_a[c]
            rb[c] = on_b[c]

        def spread(k):
            first = pl.ds(first_ref[base + k], 1)
            second = pl.ds(second_ref[base + k], 1)
            for c in range(2):
                vel_ref[c, first, :] += ra[c, pl.ds(k, 1), :]
                vel_ref[c, second, :] -= rb[c, pl.ds(k, 1), :]

        loop8(rows, spread)
        return carry

    lax.fori_loop(0, first_ref.shape[0] // rows, pair_group, 0)


def cross_waves(g_ref, anc_ref, far_ref, vel_in_ref, target_ref, source_ref, live_ref, fwd_ref, gam_ref, inv_ref, lat_ref, vel_ref, part_ref, ra, rb, rd):
    leaves = g_ref.shape[0]
    rows = ra.shape[1]
    vel_ref[...] = vel_in_ref[...]
    part_ref[...] = jnp.zeros_like(part_ref)
    live = live_ref[0]

    def pair_group(i, carry):
        base = i * rows

        def fetch(k):
            target = pl.ds(target_ref[base + k], 1)
            source = source_ref[base + k]
            block = source // leaves
            other = pl.ds(source % leaves, 1)
            row = pl.ds(k, 1)
            ra[0, row, :] = g_ref[target, :]
            rb[0, row, :] = far_ref[block, 0, other, :]
            rd[row, :] = anc_ref[target, :] - far_ref[block, 1, other, :]

        loop8(rows, fetch)
        on_a, on_b = pair_waves(ra[0], rb[0], rd[...], fwd_ref, gam_ref, inv_ref, lat_ref)
        for c in range(2):
            ra[c] = on_a[c]
            rb[c] = on_b[c]

        def spread(k, carry):
            target = pl.ds(target_ref[base + k], 1)
            source = source_ref[base + k]
            block = source // leaves
            other = pl.ds(source % leaves, 1)
            for c in range(2):
                vel_ref[c, target, :] += ra[c, pl.ds(k, 1), :]
                part_ref[block, c, other, :] -= rb[c, pl.ds(k, 1), :]
            return carry

        lax.fori_loop(0, jnp.minimum(live - base, rows), spread, 0)
        return carry

    lax.fori_loop(0, (live + rows - 1) // rows, pair_group, 0)


def vspec():
    return pl.BlockSpec(memory_space=pltpu.VMEM)


def sspec():
    return pl.BlockSpec(memory_space=pltpu.SMEM)


def tile():
    return pltpu.VMEM((LANES, LANES), f32)


def tiles(n):
    return pltpu.VMEM((n, LANES, LANES), f32)


def call(kernel, out_shape, in_specs, out_specs, scratch, flops=1e9, **kw):
    return pl.pallas_call(
        kernel,
        out_shape=out_shape,
        in_specs=in_specs,
        out_specs=out_specs,
        scratch_shapes=scratch,
        compiler_params=pltpu.CompilerParams(vmem_limit_bytes=40 * 2**20, **kw),
        cost_estimate=pl.CostEstimate(flops=int(flops), bytes_accessed=2**21, transcendentals=0),
    )


def run_local(state, first, second, dest):
    leaves = state.shape[1]
    return call(
        local_kernel,
        (jax.ShapeDtypeStruct((2, leaves, LANES), f32), jax.ShapeDtypeStruct((STEPS, leaves), jnp.int32)),
        [vspec(), sspec(), sspec(), sspec()],
        (vspec(), sspec()),
        [tiles(3), tiles(3), tiles(3), tiles(3), tiles(2), tiles(2), pltpu.SMEM((leaves // 2,), jnp.int32)],
        flops=3e9,
    )(state, first, second, dest)


def run_cross(state, far, vel, target, source, live):
    leaves = state.shape[1]
    return call(
        cross_kernel,
        (jax.ShapeDtypeStruct(vel.shape, f32), jax.ShapeDtypeStruct((far.shape[0], 2, leaves, LANES), f32)),
        [vspec(), vspec(), vspec(), sspec(), sspec(), sspec()],
        (vspec(), vspec()),
        [tiles(3), tiles(3), tiles(3), tiles(3), tiles(2), tiles(2)],
    )(state, far, vel, target, source, live)


def run_remesh(vel, arrived, shifted, strength):
    return call(
        remesh_kernel,
        jax.ShapeDtypeStruct(strength.shape, f32),
        [vspec()] * 4,
        vspec(),
        [tile(), tile(), tile(), pltpu.VMEM((2, WX, LANES), f32), tile()],
    )(vel, arrived, shifted, strength)


def run_local_waves(strength, anc, first, second, tables, rows=128):
    leaves = strength.shape[0]
    fwd, gam, inv, lat, own = tables
    return call(
        local_waves,
        jax.ShapeDtypeStruct((2, leaves, LANES), f32),
        [vspec(), vspec(), sspec(), sspec()] + [vspec()] * 5,
        vspec(),
        [pltpu.VMEM((2, rows, LANES), f32), pltpu.VMEM((2, rows, LANES), f32), pltpu.VMEM((rows, LANES), f32)],
    )(strength, anc, first, second, fwd, gam, inv, lat, own)


def run_cross_waves(strength, anc, far, vel, target, source, live, tables, rows=128):
    leaves = strength.shape[0]
    fwd, gam, inv, lat, own = tables
    return call(
        cross_waves,
        (jax.ShapeDtypeStruct(vel.shape, f32), jax.ShapeDtypeStruct((far.shape[0], 2, leaves, LANES), f32)),
        [vspec()] * 4 + [sspec()] * 3 + [vspec()] * 4,
        (vspec(), vspec()),
        [pltpu.VMEM((2, rows, LANES), f32), pltpu.VMEM((2, rows, LANES), f32), pltpu.VMEM((rows, LANES), f32)],
    )(strength, anc, far, vel, target, source, live, fwd, gam, inv, lat)


def push_kernel(shift, block_ref, out_ref, send_sem, recv_sem):
    strip, grp = lax.axis_index("strip"), lax.axis_index("grp")
    strips, groups = lax.axis_size("strip"), lax.axis_size("grp")
    to = lax.rem(strip + shift + strips, strips)
    back = lax.rem(strip - shift + strips, strips)
    barrier = pltpu.get_barrier_semaphore()
    for j in range(groups):
        pl.semaphore_signal(barrier, inc=1, device_id={"strip": back, "grp": j})
    pl.semaphore_wait(barrier, groups)
    copies = []
    for j in range(groups):
        peer = lax.rem(grp + j, groups)
        copies.append(
            pltpu.make_async_remote_copy(
                src_ref=block_ref.at[peer] if shift > 0 else block_ref,
                dst_ref=out_ref.at[grp],
                send_sem=send_sem.at[j],
                recv_sem=recv_sem.at[j],
                device_id={"strip": to, "grp": peer},
            )
        )
    for copy in copies:
        copy.start()
    for copy in copies:
        copy.wait()


def push(block, shift, collective_id):
    groups = lax.axis_size("grp")
    shape = block.shape if shift > 0 else (groups,) + block.shape
    return pl.pallas_call(
        functools.partial(push_kernel, shift),
        out_shape=jax.ShapeDtypeStruct(shape, f32),
        in_specs=[pl.BlockSpec(memory_space=pl.ANY)],
        out_specs=pl.BlockSpec(memory_space=pl.ANY),
        scratch_shapes=[pltpu.SemaphoreType.DMA((groups,)), pltpu.SemaphoreType.DMA((groups,))],
        compiler_params=pltpu.CompilerParams(collective_id=collective_id, has_side_effects=True),
    )(block)


def regroup_kernel(step, nodes_ref, anchor_ref, order_ref, out_ref, outbox, send_sem, recv_sem, own_sem):
    strip = lax.axis_index("strip")
    strips = outbox.shape[0]
    barrier = pltpu.get_barrier_semaphore()

    def greet(d, carry):
        pl.semaphore_signal(barrier, inc=1, device_id={"strip": lax.rem(strip + d, strips)})
        return carry

    lax.fori_loop(1, strips, greet, 0)

    def fill(t, carry):
        for r in range(2):
            leaf = pl.ds(order_ref[step, 2 * t + r], 1)
            outbox[t, r : r + 1, :] = nodes_ref[leaf, :]
            outbox[t, 2 + r : 3 + r, :] = anchor_ref[leaf, :]
        return carry

    lax.fori_loop(0, strips, fill, 0)
    pl.semaphore_wait(barrier, strips - 1)

    def send(d, carry):
        to = lax.rem(strip + d, strips)
        pltpu.make_async_remote_copy(
            src_ref=outbox.at[to],
            dst_ref=out_ref.at[strip],
            send_sem=send_sem,
            recv_sem=recv_sem,
            device_id={"strip": to},
        ).start()
        return carry

    lax.fori_loop(1, strips, send, 0)
    own = pltpu.make_async_copy(outbox.at[strip], out_ref.at[strip], own_sem)
    own.start()
    own.wait()
    rest = pl.ds(0, strips - 1)
    pltpu.make_async_copy(outbox.at[rest], outbox.at[rest], send_sem).wait()
    pltpu.make_async_copy(out_ref.at[rest], out_ref.at[rest], recv_sem).wait()


def regroup(nodes, anchor, order, step, collective_id):
    strips = lax.axis_size("strip")
    shape = (strips, 4, LANES)
    return pl.pallas_call(
        functools.partial(regroup_kernel, step),
        out_shape=jax.ShapeDtypeStruct(shape, f32),
        in_specs=[vspec(), vspec(), sspec()],
        out_specs=vspec(),
        scratch_shapes=[pltpu.VMEM(shape, f32)] + [pltpu.SemaphoreType.DMA] * 3,
        compiler_params=pltpu.CompilerParams(
            collective_id=collective_id, has_side_effects=True, vmem_limit_bytes=16 * 2**20
        ),
    )(nodes, anchor, order)


def on_device(
    offsets,
    circulation,
    window_anchor,
    local_first,
    local_offset,
    cross_target,
    cross_source,
    cross_count,
    destination,
):
    leaves = circulation.shape[0]
    per_strip = leaves // lax.axis_size("strip")
    half = LANES // 2
    second = (local_first + local_offset) % leaves
    shifted = offsets.transpose(1, 0, 2)
    state = jnp.concatenate([shifted + window_anchor.T[:, :, None], circulation[None]], axis=0)
    anchor = jnp.repeat(window_anchor, half, axis=1)
    tables = [jnp.asarray(t) for t in fourier_tables()]
    far = push(state, -1, 0)
    vel, order = run_local(state, local_first[0], second[0], destination[:, :, 0])
    vel, part = run_cross(state, far, vel, cross_target[0], cross_source[0], cross_count[0])
    arrived = push(part, 1, 1)
    nodes = run_remesh(vel, arrived, shifted, circulation)
    box = regroup(nodes, anchor, order, 0, 2)
    strength = box[:, :per_strip].reshape(leaves, LANES)
    anchor = box[:, per_strip:].reshape(leaves, LANES)
    far = push(jnp.stack([strength, anchor]), -1, 3)
    vel = run_local_waves(strength, anchor, local_first[1], second[1], tables)
    vel, part = run_cross_waves(
        strength, anchor, far, vel, cross_target[1], cross_source[1], cross_count[1], tables
    )
    arrived = push(part, 1, 4)
    node = jnp.arange(LANES, dtype=jnp.int32)
    grid = jnp.stack([node // WY, node % WY]).astype(f32)
    shifted = jnp.broadcast_to(grid[:, None, :], vel.shape)
    nodes = run_remesh(vel, arrived, shifted, strength)
    box = regroup(nodes, anchor, order, 1, 5)
    strength = box[:, :per_strip].reshape(leaves, LANES)
    anchor = box[:, per_strip:, ::half].reshape(leaves, 2)
    return strength, anchor


def solution(mesh):
    rows = P(("strip", "grp"))
    lists = P(None, ("strip", "grp"))
    return jax.shard_map(
        on_device,
        mesh=mesh,
        in_specs=(rows, rows, rows, lists, lists, lists, lists, lists, lists),
        out_specs=(rows, rows),
        check_vma=False,
    )
```

time: 885 us -> 227 us (0.26)
  starting transfers between devices: 332 us -> 0 us
  other arithmetic: 239 us -> 3.55 us
  Pallas kernels: 0 us -> 210 us
  waiting for transfers between devices: 137 us -> 0 us
  local copies, waits for them, and re-layouts: 133 us -> 11.8 us
  between operations: 16.5 us -> 1.02 us
  matrix products: 11.8 us -> 0 us
  loops' own time: 11.5 us -> 0 us
    all_to_all x6 -> x0, starting transfers between devices: 286 us -> none  [the longest x2 228 us: on_device(): lax.all_to_all(strength[send_order], 'strip', split_axis=0, concat_axis=0...]
    pallas_call x0 -> x12, Pallas kernels: none -> 210 us  [the longest x4 77.3 us: push(): pl.pallas_call(functools.partial(push_kernel, shift), out_shape=jax.Shape...]
    reduce_sum x148 -> x0, other arithmetic: 108 us -> none  [the longest x82 65.2 us: mutual(): jnp.sum(target_gamma * tilt_y, axis=1)]
    gather x170 -> x0, local copies, waits for them, and re-layouts: 102 us -> none  [the longest x128 73.6 us: block_pairs(): return mutual(packed[first_rows], packed[second_rows])]
    scatter-add x40 -> x0, other arithmetic: 82 us -> none  [the longest x18 34.7 us: cross_turn(): far_part.at[sources].add(on_sources * live_mask)]
    all_gather x2 -> x0, waiting for transfers between devices: 59.6 us -> none  [on_device(): whole_strip = lax.all_gather(packed, 'grp', axis=0, tiled=True)]
    ppermute x4 -> x0, starting transfers between devices: 45.5 us -> none  [from_behind(): return lax.ppermute(x, axis, [(i, (i + by) % peers) for i in range(peers)])]
    unnamed x6 -> x0, waiting for transfers between devices: 37.8 us -> none
  transfers between devices with their start and end apart: 14 -> 0, of which waited for: 9 -> 0; matrix products, arithmetic and copies ran while one was open for 41% -> 0% of each run, Pallas kernels for 0% -> 0%
where the time goes in v1:
time: 227 us
  Pallas kernels  210 us (93%)
  local copies, waits for them, and re-layouts  11.8 us (5%)
  other arithmetic  3.55 us (2%)
    pallas_call x4, Pallas kernels, push(): pl.pallas_call(functools.partial(push_kernel, shift), out_shape=jax.Shape...  77.3 us
    pallas_call x2, Pallas kernels, regroup(): pl.pallas_call(functools.partial(regroup_kernel, step), out_shape=jax.Sha...  55.7 us
    pallas_call x1, Pallas kernels, run_local(): call(local_kernel, (jax.ShapeDtypeStruct((2, leaves, LANES), f32), jax.Sh...  36.4 us
    pallas_call x1, Pallas kernels, run_cross(): call(cross_kernel, (jax.ShapeDtypeStruct(vel.shape, f32), jax.ShapeDtypeS...  21.1 us
    unnamed x41, local copies, waits for them, and re-layouts  8.49 us
    pallas_call x2, Pallas kernels, run_remesh(): call(remesh_kernel, jax.ShapeDtypeStruct(strength.shape, f32), [vspec()]...  7.81 us
    pallas_call x1, Pallas kernels, run_local_waves(): call(local_waves, jax.ShapeDtypeStruct((2, leaves, LANES), f32), [vspec()...  7.17 us
    pallas_call x1, Pallas kernels, run_cross_waves(): call(cross_waves, (jax.ShapeDtypeStruct(vel.shape, f32), jax.ShapeDtypeSt...  4.89 us

profile of v1, /device:TPU:1, one launch (start us, length us, event | category | flops | bytes accessed | tf_op | source)
XLA Modules:
  0.0 226.8 jit_solution(12869562784376453027)
XLA Ops:
  0.6 1.1 broadcast_add_fusion
  1.7 0.9 pad_maximum_fusion.block_ref.state_ref
  2.7 0.8 and_select_fusion
  3.5 0.8 fusion.5
  4.9 36.4 %shard_map.150 = (f32[2,256,128]{2,1,0:T(8,128)S(1)}, s32[2,256]{1,0:T(2,128)S(1)}) custom-call(f32[3,256,128]{2,1,0:T(8,128)S(1)} %pad_maximum_fusion.block_ref.state_ref, s32[256]{0:T(256)S(1)} %bitcast.45, s32[256]{0:T(256)S(1)} %bitcast.44, s32[2,256]{1,0:T(2,128)S(1)} %bitcast.37), custom_call_target="tpu_custom_call" | custom-call | flops 3000000000 | bytes 2097152 | tf_op jit(solution)/shard_map/pallas_call | solution.py:462
  41.4 25.5 %shard_map.149.far_ref = f32[4,3,256,128]{3,2,1,0:T(8,128)} custom-call(f32[3,256,128]{2,1,0:T(8,128)} %copy-done.1), custom_call_target="tpu_custom_call" | custom-call | tf_op jit(solution)/shard_map/pallas_call | solution.py:547
  67.6 1.4 copy-done
  69.0 21.1 %shard_map.151 = (f32[2,256,128]{2,1,0:T(8,128)S(1)}, f32[4,2,256,128]{3,2,1,0:T(8,128)S(1)}) custom-call(f32[3,256,128]{2,1,0:T(8,128)S(1)} %copy-done.2, f32[4,3,256,128]{3,2,1,0:T(8,128)S(1)} %copy-done, f32[2,256,128]{2,1,0:T(8,128)S(1)} %get-tuple-element.8.vel_in_ref, s32[256]{0:T(256)S(1)} %bitcast.42, s32[256]{0:T(256)S(1)} %bitcast.43, ...), custom_call_target="tpu_custom_call" | custom-call | flops 1000000000 | bytes 2097152 | tf_op jit(solution)/shard_map/pallas_call | solution.py:474
  90.1 1.0 copy-done.6
  91.1 17.7 %shard_map.152.arrived_ref = f32[4,2,256,128]{3,2,1,0:T(8,128)} custom-call(f32[4,2,256,128]{3,2,1,0:T(8,128)} %copy-done.6), custom_call_target="tpu_custom_call" | custom-call | tf_op jit(solution)/shard_map/pallas_call | solution.py:547
  108.9 1.2 copy-done.7
  110.2 3.9 %shard_map.153.nodes_ref = f32[256,128]{1,0:T(8,128)S(1)} custom-call(f32[2,256,128]{2,1,0:T(8,128)S(1)} %get-tuple-element.9.vel_ref, f32[4,2,256,128]{3,2,1,0:T(8,128)S(1)} %copy-done.7, f32[2,256,128]{2,1,0:T(8,128)S(1)} %bitcast.35, f32[256,128]{1,0:T(8,128)S(1)} %copy-done.8), custom_call_target="tpu_custom_call" | custom-call | flops 1000000000 | bytes 2097152 | tf_op jit(solution)/shard_map/pallas_call | solution.py:484
  114.2 28.8 %shard_map.154 = f32[128,4,128]{2,1,0:T(4,128)S(1)} custom-call(f32[256,128]{1,0:T(8,128)S(1)} %shard_map.153.nodes_ref, f32[256,128]{1,0:T(8,128)S(1)} %copy.20.anchor_ref, s32[2,256]{1,0:T(2,128)S(1)} %get-tuple-element.11.order_ref), custom_call_target="tpu_custom_call" | custom-call | tf_op jit(solution)/shard_map/pallas_call | solution.py:601
  143.2 7.2 %shard_map.156.vel_in_ref = f32[2,256,128]{2,1,0:T(8,128)S(1)} custom-call(f32[256,128]{1,0:T(8,128)S(1)} %bitcast.31, f32[256,128]{1,0:T(8,128)S(1)} %bitcast.27, s32[256]{0:T(256)S(1)} %bitcast.41, s32[256]{0:T(256)S(1)} %bitcast.38, bf16[2,512,512]{2,1,0:T(8,128)(2,1)S(1)} %copy-done.9, bf16[2,128,512]{2,1,0:T(8,128)(2,1)S(1)} %copy-done.10, ...), custom_call_target="tpu_custom_call" | custom-call | flops 1000000000 | bytes 2097152 | tf_op jit(solution)/shard_map/pallas_call | solution.py:496
  150.4 0.7 pad_maximum_fusion.1.block_ref
  151.1 19.6 %shard_map.155.far_ref = f32[4,2,256,128]{3,2,1,0:T(8,128)} custom-call(f32[2,256,128]{2,1,0:T(8,128)} %pad_maximum_fusion.1.block_ref), custom_call_target="tpu_custom_call" | custom-call | tf_op jit(solution)/shard_map/pallas_call | solution.py:547
  170.7 1.2 copy-done.3
  172.0 4.9 %shard_map.157 = (f32[2,256,128]{2,1,0:T(8,128)S(1)}, f32[4,2,256,128]{3,2,1,0:T(8,128)S(1)}) custom-call(f32[256,128]{1,0:T(8,128)S(1)} %bitcast.33, f32[256,128]{1,0:T(8,128)S(1)} %bitcast.29, f32[4,2,256,128]{3,2,1,0:T(8,128)S(1)} %copy-done.3, f32[2,256,128]{2,1,0:T(8,128)S(1)} %shard_map.156.vel_in_ref, s32[256]{0:T(256)S(1)} %bitcast.39, ...), custom_call_target="tpu_custom_call" | custom-call | flops 1000000000 | bytes 2097152 | tf_op jit(solution)/shard_map/pallas_call | solution.py:508
  176.9 1.0 copy-done.5
  177.9 14.4 %shard_map.158.arrived_ref = f32[4,2,256,128]{3,2,1,0:T(8,128)} custom-call(f32[4,2,256,128]{3,2,1,0:T(8,128)} %copy-done.5), custom_call_target="tpu_custom_call" | custom-call | tf_op jit(solution)/shard_map/pallas_call | solution.py:547
  192.4 1.2 copy-done.4
  193.6 3.9 %shard_map.159.nodes_ref = f32[256,128]{1,0:T(8,128)S(1)} custom-call(f32[2,256,128]{2,1,0:T(8,128)S(1)} %get-tuple-element.12.vel_ref, f32[4,2,256,128]{3,2,1,0:T(8,128)S(1)} %copy-done.4, f32[2,256,128]{2,1,0:T(8,128)S(1)} %broadcast_in_dim.15.shift_ref, f32[256,128]{1,0:T(8,128)S(1)} %bitcast.34), custom_call_target="tpu_custom_call" | custom-call | flops 1000000000 | bytes 2097152 | tf_op jit(solution)/shard_map/pallas_call | solution.py:484
  197.5 26.9 %shard_map.160 = f32[128,4,128]{2,1,0:T(4,128)S(1)} custom-call(f32[256,128]{1,0:T(8,128)S(1)} %shard_map.159.nodes_ref, f32[256,128]{1,0:T(8,128)S(1)} %bitcast.30, s32[2,256]{1,0:T(2,128)S(1)} %get-tuple-element.11.order_ref), custom_call_target="tpu_custom_call" | custom-call | tf_op jit(solution)/shard_map/pallas_call | solution.py:601
  224.4 1.0 slice.55
  (46 shorter events, 3.0 us)
Async XLA Ops:
  2.7 38.7 %copy-start.1 = (f32[3,256,128]{2,1,0:T(8,128)}, f32[3,256,128]{2,1,0:T(8,128)S(1)}, u32[]{:S(2)}) copy-start(f32[3,256,128]{2,1,0:T(8,128)S(1)} %pad_maximum_fusion.block_ref.state_ref) | copy-start | bytes 1179652
  41.3 25.6 %copy-start.16 = (s32[2,256]{1,0:T(2,128)S(1)}, s32[2,256]{1,0:T(2,128)}, u32[]{:S(2)}) copy-start(s32[2,256]{1,0:T(2,128)} %param.19) | copy-start | bytes 6148
  41.4 25.6 %copy-start.17 = (s32[2,256]{1,0:T(2,128)S(1)}, s32[2,256]{1,0:T(2,128)}, u32[]{:S(2)}) copy-start(s32[2,256]{1,0:T(2,128)} %param.20) | copy-start | bytes 6148
  41.4 25.6 %copy-start.18 = (s32[2,1]{0,1:T(1,128)S(1)}, s32[2,1]{0,1:T(1,128)}, u32[]{:S(2)}) copy-start(s32[2,1]{0,1:T(1,128)} %param.21) | copy-start | bytes 28
  41.4 26.2 %copy-start.2 = (f32[3,256,128]{2,1,0:T(8,128)S(1)}, f32[3,256,128]{2,1,0:T(8,128)}, u32[]{:S(2)}) copy-start(f32[3,256,128]{2,1,0:T(8,128)} %copy-done.1) | copy-start | bytes 1179652
  67.6 1.4 copy-start
  90.1 1.0 copy-start.6
  91.1 17.7 %copy-start.14 = (f32[256,2,128]{2,1,0:T(2,128)S(1)}, f32[256,2,128]{2,1,0:T(2,128)}, u32[]{:S(2)}) copy-start(f32[256,2,128]{2,1,0:T(2,128)} %param.14) | copy-start | bytes 786436
  91.1 17.8 %copy-start.8 = (f32[256,128]{1,0:T(8,128)S(1)}, f32[256,128]{1,0:T(8,128)}, u32[]{:S(2)}) copy-start(f32[256,128]{1,0:T(8,128)} %g_ref.1) | copy-start | bytes 393220
  108.9 1.2 copy-start.7
  110.1 4.0 %copy-start.15 = (f32[256,2]{0,1:T(2,128)S(1)}, f32[256,2]{0,1:T(2,128)}, u32[]{:S(2)}) copy-start(f32[256,2]{0,1:T(2,128)} %param.16) | copy-start | bytes 6148
  110.1 33.0 %copy-start.9 = (bf16[2,512,512]{2,1,0:T(8,128)(2,1)S(1)}, bf16[2,512,512]{2,1,0:T(8,128)(2,1)}, u32[]{:S(2)}) copy-start(bf16[2,512,512]{2,1,0:T(8,128)(2,1)} %constant.55.clone.fwd_ref) | copy-start | bytes 3145732
  110.1 33.0 %copy-start.10 = (bf16[2,128,512]{2,1,0:T(8,128)(2,1)S(1)}, bf16[2,128,512]{2,1,0:T(8,128)(2,1)}, u32[]{:S(2)}) copy-start(bf16[2,128,512]{2,1,0:T(8,128)(2,1)} %constant.56.clone.gam_ref) | copy-start | bytes 786436
  110.1 33.0 %copy-start.11 = (bf16[2,512,128]{2,1,0:T(8,128)(2,1)S(1)}, bf16[2,512,128]{2,1,0:T(8,128)(2,1)}, u32[]{:S(2)}) copy-start(bf16[2,512,128]{2,1,0:T(8,128)(2,1)} %constant.57.clone.inv_ref) | copy-start | bytes 786436
  110.2 33.0 %copy-start.12 = (bf16[2,128,256]{2,1,0:T(8,128)(2,1)S(1)}, bf16[2,128,256]{2,1,0:T(8,128)(2,1)}, u32[]{:S(2)}) copy-start(bf16[2,128,256]{2,1,0:T(8,128)(2,1)} %constant.59.clone.own_ref) | copy-start | bytes 393220
  110.2 33.0 %copy-start.13 = (f32[8,512]{1,0:T(8,128)S(1)}, f32[8,512]{1,0:T(8,128)}, u32[]{:S(2)}) copy-start(f32[8,512]{1,0:T(8,128)} %constant.58.clone.lat_ref) | copy-start | bytes 49156
  170.7 1.2 copy-start.3
  176.9 1.0 copy-start.5
  192.4 1.2 copy-start.4

commit v2 on v0

v2 whole, which is shorter than its diff:
```python
import functools
import jax
import jax.numpy as jnp
import numpy as np
from jax import lax
from jax.experimental import pallas as pl
from jax.experimental.pallas import tpu as pltpu
from jax.sharding import PartitionSpec as P

WX = 8
WY = 16
STEPS = 2
time_step = 0.5
biot_factor = 0.15915494309189535
LANES = 128
f32 = jnp.float32
bf16 = jnp.bfloat16


def recip(x):
    return pl.reciprocal(x, approx=True)


def mutual_lanes(a_refs, b_refs, on_a, on_b):
    xa_ref, ya_ref, ga_ref = a_refs
    xb_ref, yb_ref, gb_ref = b_refs
    ua_ref, va_ref = on_a
    ub_ref, vb_ref = on_b
    ub_ref[...] = jnp.zeros_like(ub_ref)
    vb_ref[...] = jnp.zeros_like(vb_ref)
    zero = jnp.zeros((8, LANES), f32)

    def over_a(ia, carry):
        a0 = pl.multiple_of(ia * 8, 8)

        def over_b(ib, acc):
            acc = list(acc)
            rows = pl.ds(pl.multiple_of(ib * 8, 8), 8)
            xb, yb, gb = xb_ref[rows, :], yb_ref[rows, :], gb_ref[rows, :]
            ub, vb = ub_ref[rows, :], vb_ref[rows, :]
            for r in range(8):
                row = pl.ds(a0 + r, 1)
                dx = xa_ref[row, :] - xb
                dy = ya_ref[row, :] - yb
                w = recip(dx * dx + dy * dy + 1.0)
                tx = dx * w
                ty = dy * w
                acc[r] = acc[r] + gb * ty
                acc[8 + r] = acc[8 + r] + gb * tx
                ga = ga_ref[row, :]
                ub = ub + ga * ty
                vb = vb + ga * tx
            ub_ref[rows, :] = ub
            vb_ref[rows, :] = vb
            return tuple(acc)

        acc = lax.fori_loop(0, 16, over_b, (zero,) * 16, unroll=8)
        for r in range(8):
            ua_ref[pl.ds(a0 + r, 1), :] = jnp.sum(acc[r], axis=0, keepdims=True)
            va_ref[pl.ds(a0 + r, 1), :] = jnp.sum(acc[8 + r], axis=0, keepdims=True)
        return carry

    lax.fori_loop(0, 16, over_a, 0)


def loop8(count, body):
    def eight(k, carry):
        for u in range(8):
            body(k * 8 + u)
        return carry

    lax.fori_loop(0, count // 8, eight, 0)


def node_weight(distance):
    r = jnp.abs(distance)
    inner = 1.0 + r * r * (1.5 * r - 2.5)
    s = jnp.maximum(2.0 - r, 0.0)
    outer = (0.5 * s) * s * (1.0 - r)
    return jnp.where(r < 1.0, inner, outer)


def remesh_lanes(px_ref, py_ref, g_ref, wx_ref, nodes_ref):
    ix = lax.broadcasted_iota(jnp.int32, (WX, LANES), 0).astype(f32)
    iy = lax.broadcasted_iota(jnp.int32, (WX, LANES), 0).astype(f32)

    def over_p(p4, acc):
        acc = list(acc)
        for u in range(2):
            p = p4 * 2 + u
            row = pl.ds(p, 1)
            wx_ref[u] = node_weight(px_ref[row, :] - ix) * g_ref[row, :]
            y = py_ref[row, :] - iy
            wy = (node_weight(y), node_weight(y - 8.0))
            for i in range(WX):
                wxi = wx_ref[u, i : i + 1, :]
                for h in range(2):
                    acc[2 * i + h] = acc[2 * i + h] + wxi * wy[h]
        return tuple(acc)

    acc = lax.fori_loop(0, LANES // 2, over_p, (jnp.zeros((8, LANES), f32),) * 16)
    for i in range(16):
        nodes_ref[8 * i : 8 * i + 8, :] = acc[i]


def split(x):
    hi = x.astype(bf16)
    return hi, (x - hi.astype(f32)).astype(bf16)


def dot3(x, m_hi, m_lo):
    hi, lo = split(x)
    d = functools.partial(jnp.dot, preferred_element_type=f32)
    return d(hi, m_hi) + (d(hi, m_lo) + d(lo, m_hi))


@functools.cache
def fourier_tables():
    n1, n2 = 2 * WX - 1, 2 * WY - 1
    size = n1 * n2
    u = np.arange(n1)
    v = np.arange(n2)
    di = np.where(u < WX, u, u - n1)
    dj = np.where(v < WY, v, v - n2)
    DI, DJ = [t.reshape(-1).astype(np.float64) for t in np.meshgrid(di, dj, indexing="ij")]
    k1, k2 = [t.reshape(-1) for t in np.meshgrid(u, v, indexing="ij")]
    keep = [0]
    for m in range(1, size):
        mirror = ((-k1[m]) % n1) * n2 + ((-k2[m]) % n2)
        if m < mirror:
            keep.append(m)
    f1, f2 = k1[keep].astype(np.float64), k2[keep].astype(np.float64)
    nf = len(keep)

    def phase(i, j):
        return 2 * np.pi * (np.outer(i, f1) / n1 + np.outer(j, f2) / n2)

    forward = np.zeros((512, 512))
    p = phase(DI, DJ)
    forward[:size, :nf] = np.cos(p)
    forward[:size, 256 : 256 + nf] = -np.sin(p)
    node = np.arange(WX * WY)
    q = phase(node // WY, node % WY)
    gamma = np.zeros((128, 512))
    gamma[:, :nf] = np.cos(q)
    gamma[:, 256 : 256 + nf] = -np.sin(q)
    weight = np.full(nf, 2.0 / size)
    weight[0] = 1.0 / size
    inverse = np.zeros((512, 128))
    inverse[:nf] = weight[:, None] * np.cos(q).T
    inverse[256 : 256 + nf] = -weight[:, None] * np.sin(q).T
    lattice = np.zeros((8, 512))
    lattice[0, :size] = DI
    lattice[1, :size] = DJ
    ddx = (node // WY)[:, None] - (node // WY)[None, :]
    ddy = (node % WY)[:, None] - (node % WY)[None, :]
    w = biot_factor / (ddx * ddx + ddy * ddy + 1.0)
    own = np.concatenate([(-ddy * w).T, (ddx * w).T], axis=1)

    def halves(x):
        hi = x.astype(np.float32).astype(bf16)
        lo = (x - hi.astype(np.float64)).astype(np.float32).astype(bf16)
        return np.stack([hi, lo])

    return halves(forward), halves(gamma), halves(inverse), lattice.astype(np.float32), halves(own)


def vspec():
    return pl.BlockSpec(memory_space=pltpu.VMEM)


def sspec():
    return pl.BlockSpec(memory_space=pltpu.SMEM)


def tile():
    return pltpu.VMEM((LANES, LANES), f32)


def tiles(n):
    return pltpu.VMEM((n, LANES, LANES), f32)


def one_sided_lanes(a_refs, b_refs, on_a):
    xa_ref, ya_ref = a_refs
    xb_ref, yb_ref, gb_ref = b_refs
    ua_ref, va_ref = on_a
    zero = jnp.zeros((8, LANES), f32)

    def over_a(ia, carry):
        a0 = pl.multiple_of(ia * 8, 8)

        def over_b(ib, acc):
            acc = list(acc)
            rows = pl.ds(pl.multiple_of(ib * 8, 8), 8)
            xb, yb, gb = xb_ref[rows, :], yb_ref[rows, :], gb_ref[rows, :]
            for r in range(8):
                row = pl.ds(a0 + r, 1)
                dx = xa_ref[row, :] - xb
                dy = ya_ref[row, :] - yb
                w = gb * recip(dx * dx + (dy * dy + 1.0))
                acc[r] = acc[r] + dy * w
                acc[8 + r] = acc[8 + r] + dx * w
            return tuple(acc)

        acc = lax.fori_loop(0, 16, over_b, (zero,) * 16, unroll=8)
        for r in range(8):
            ua_ref[pl.ds(a0 + r, 1), :] = jnp.sum(acc[r], axis=0, keepdims=True)
            va_ref[pl.ds(a0 + r, 1), :] = jnp.sum(acc[8 + r], axis=0, keepdims=True)
        return carry

    lax.fori_loop(0, 16, over_a, 0)


def dot(a, b):
    return jnp.dot(a, b, preferred_element_type=f32)


def onehot(condition):
    return jnp.where(condition, 1.0, 0.0).astype(bf16)


def dot_exact(hot, x):
    hi, rest = split(x)[0], None
    rest = x - hi.astype(f32)
    mid, lo = split(rest)
    return (dot(hot, hi) + dot(hot, mid)) + dot(hot, lo)


def dot_near(hot, x):
    hi, lo = split(x)
    return dot(hot, hi) + dot(hot, lo)


def spread_rows(index_row, x):
    leaves = index_row.shape[1]
    places = lax.broadcasted_iota(jnp.int32, (leaves, leaves), 0)
    return dot_near(onehot(places == index_row), x)


def earlier(n):
    return onehot(lax.broadcasted_iota(jnp.int32, (n, n), 0) < lax.broadcasted_iota(jnp.int32, (n, n), 1))


def sort_lists(target_ref, source_ref, live_ref, outbox):
    groups = outbox.shape[0]
    n = target_ref.shape[1]
    before = earlier(n)
    rows8 = lax.broadcasted_iota(jnp.int32, (8, n), 0)
    places = lax.broadcasted_iota(jnp.int32, (n, n), 0)
    k = lax.broadcasted_iota(jnp.int32, (1, n), 1)
    outbox[...] = jnp.zeros_like(outbox)
    for step in range(STEPS):
        source = source_ref[step : step + 1, :]
        owner = lax.shift_right_logical(source, n.bit_length() - 1)
        key = jnp.where(k < live_ref[step, 0], owner, groups)
        row = jnp.bitwise_and(source, n - 1)
        mine = jnp.where(rows8 == key, 1.0, 0.0)
        place = jnp.sum(mine * dot(mine.astype(bf16), before), axis=0, keepdims=True).astype(jnp.int32)
        values = jnp.where(rows8 == 0, target_ref[step : step + 1, :], jnp.where(rows8 == 1, row, 0))
        values = values.astype(f32).astype(bf16)
        count = jnp.sum(mine, axis=1, keepdims=True).astype(jnp.int32)
        for b in range(groups):
            hot = onehot((places == place) & (key == b))
            found = lax.dot_general(values, hot, (((1,), (1,)), ((), ())), preferred_element_type=f32)
            outbox[b, 2 * step : 2 * step + 2, :] = found[0:2, :].astype(jnp.int32)
            outbox[b, 4 + step : 5 + step, :] = jnp.broadcast_to(count[b : b + 1, :], (1, n))


class Ring:
    def __init__(self, block, own, up, down, halves, send_sem, recv_sem):
        self.block, self.own, self.up, self.down = block, own, up, down
        self.halves, self.send_sem, self.recv_sem = halves, send_sem, recv_sem
        self.grp = lax.axis_index("grp")
        groups = lax.axis_size("grp")
        self.right = lax.rem(self.grp + 1, groups)
        self.left = lax.rem(self.grp + groups - 1, groups)
        self.across = lax.rem(self.grp + 2, groups)
        strip, strips = lax.axis_index("strip"), lax.axis_size("strip")
        self.above = lax.rem(strip + 1, strips)
        self.below = lax.rem(strip + strips - 1, strips)
        self.sent = []

    def send(self, src, dst, device, slot):
        copy = pltpu.make_async_remote_copy(
            src_ref=src,
            dst_ref=dst,
            send_sem=self.send_sem.at[slot],
            recv_sem=self.recv_sem.at[slot],
            device_id=device,
        )
        copy.start()
        self.sent.append(copy)
        return copy

    def to_strips(self, src, member, slot):
        return [
            self.send(src, self.down.at[member], {"strip": self.above}, slot),
            self.send(src, self.up.at[member], {"strip": self.below}, slot + 1),
        ]

    def first(self):
        self.from_left = self.send(self.block, self.own.at[self.grp], {"grp": self.right}, 0)
        self.from_right = self.send(self.block, self.own.at[self.grp], {"grp": self.left}, 1)
        self.last = self.to_strips(self.block, self.grp, 2)

    def second(self):
        self.from_left.wait_recv()
        half = self.halves(self.own, self.left)[0]
        self.half_a = self.send(half, half, {"grp": self.right}, 4)
        self.last += self.to_strips(self.own.at[self.left], self.left, 5)
        self.from_right.wait_recv()
        half = self.halves(self.own, self.right)[1]
        self.half_b = self.send(half, half, {"grp": self.left}, 7)
        self.last += self.to_strips(self.own.at[self.right], self.right, 8)

    def third(self):
        self.half_a.wait_recv()
        self.half_b.wait_recv()
        self.last += self.to_strips(self.own.at[self.across], self.across, 10)

    def finish(self):
        for copy in self.last:
            copy.wait_recv()
        for copy in self.sent:
            copy.wait_send()


def local_kernel(
    block_ref,
    state_ref,
    first_ref,
    second_ref,
    first_row_ref,
    second_row_ref,
    target_ref,
    source_ref,
    live_ref,
    vel_ref,
    lists_ref,
    up_ref,
    down_ref,
    own_ref,
    outbox,
    ta,
    tb,
    oa,
    ob,
    ra,
    rb,
    send_sem,
    recv_sem,
    list_send,
    list_recv,
):
    leaves = state_ref.shape[1]
    halves = lambda own, member: [own.at[member, :, pl.ds(h * leaves // 2, leaves // 2)] for h in range(2)]
    ring = Ring(block_ref, own_ref, up_ref, down_ref, halves, send_sem, recv_sem)
    groups = lists_ref.shape[0]
    barrier = pltpu.get_barrier_semaphore()
    for device in ({"grp": ring.left}, {"grp": ring.right}, {"strip": ring.above}):
        pl.semaphore_signal(barrier, inc=1, device_id=device)
    for j in range(groups):
        pl.semaphore_signal(barrier, inc=1, device_id={"strip": ring.below, "grp": j})
    sort_lists(target_ref, source_ref, live_ref, outbox)
    pl.semaphore_wait(barrier, 3 + groups)
    ring.first()
    mail = []
    for j in range(groups):
        peer = lax.rem(ring.grp + j, groups)
        copy = pltpu.make_async_remote_copy(
            src_ref=outbox.at[peer],
            dst_ref=lists_ref.at[ring.grp],
            send_sem=list_send.at[j],
            recv_sem=list_recv.at[j],
            device_id={"strip": ring.above, "grp": peer},
        )
        copy.start()
        mail.append(copy)

    def self_group(i, carry):
        rows = pl.ds(pl.multiple_of(i * LANES, LANES), LANES)
        for c in range(3):
            ta[c] = state_ref[c, rows, :].T
        one_sided_lanes((ta.at[0], ta.at[1]), (ta.at[0], ta.at[1], ta.at[2]), (oa.at[0], oa.at[1]))
        vel_ref[0, rows, :] = oa[0].T * -biot_factor
        vel_ref[1, rows, :] = oa[1].T * biot_factor
        return carry

    def pair_group(i):
        base = i * LANES
        rows = pl.ds(base, LANES)

        def fetch(k):
            first = first_ref[base + k]
            second = second_ref[base + k]
            for c in range(3):
                ra[c, pl.ds(base + k, 1), :] = state_ref[c, pl.ds(first, 1), :]
                rb[c, pl.ds(base + k, 1), :] = state_ref[c, pl.ds(second, 1), :]

        loop8(LANES, fetch)
        for c in range(3):
            ta[c] = ra[c, rows, :].T
            tb[c] = rb[c, rows, :].T
        mutual_lanes(
            [ta.at[c] for c in range(3)],
            [tb.at[c] for c in range(3)],
            [oa.at[c] for c in range(2)],
            [ob.at[c] for c in range(2)],
        )
        ra[0, rows, :] = oa[0].T * -biot_factor
        ra[1, rows, :] = oa[1].T * biot_factor
        rb[0, rows, :] = ob[0].T * biot_factor
        rb[1, rows, :] = ob[1].T * -biot_factor

    lax.fori_loop(0, leaves // LANES, self_group, 0)
    ring.second()
    pair_group(0)
    ring.third()
    for i in range(1, leaves // LANES):
        pair_group(i)
    for c in range(2):
        vel_ref[c] += spread_rows(first_row_ref[...], ra[c]) + spread_rows(second_row_ref[...], rb[c])
    ring.finish()
    for copy in mail:
        copy.wait()


def walk(target_ref, source_ref, live_ref, lists_ref, leaves, step, visit):
    live = live_ref[step, 0]

    def mine(k, carry):
        source = source_ref[step, k]
        visit(k, target_ref[step, k], 0, source // leaves, source % leaves)
        return carry

    lax.fori_loop(0, live, mine, 0)
    base = live
    for g in range(lists_ref.shape[0]):
        count = lists_ref[g, 4 + step, 0]

        def theirs(k, carry, g=g, base=base):
            visit(base + k, lists_ref[g, 2 * step + 1, k], 1, g, lists_ref[g, 2 * step, k])
            return carry

        lax.fori_loop(0, count, theirs, 0)
        base = base + count
    return base


def cross_kernel(state_ref, up_ref, down_ref, vel_in_ref, target_ref, source_ref, live_ref, lists_ref, vel_ref, ra, rb, ta, tb, oa):
    leaves = state_ref.shape[1]
    sides = (up_ref, down_ref)
    vel_ref[...] = vel_in_ref[...]

    def fetch(n, leaf, side, block, row):
        for c in range(2):
            ra[c, pl.ds(n, 1), :] = state_ref[c, pl.ds(leaf, 1), :]
        for c in range(3):
            rb[c, pl.ds(n, 1), :] = sides[side][block, c, pl.ds(row, 1), :]

    total = walk(target_ref, source_ref, live_ref, lists_ref, leaves, 0, fetch)

    def pair_group(i, carry):
        rows = pl.ds(pl.multiple_of(i * LANES, LANES), LANES)
        for c in range(2):
            ta[c] = ra[c, rows, :].T
        for c in range(3):
            tb[c] = rb[c, rows, :].T
        one_sided_lanes([ta.at[c] for c in range(2)], [tb.at[c] for c in range(3)], [oa.at[c] for c in range(2)])
        ra[0, rows, :] = oa[0].T * -biot_factor
        ra[1, rows, :] = oa[1].T * biot_factor
        return carry

    lax.fori_loop(0, (total + LANES - 1) // LANES, pair_group, 0)

    def spread(n, leaf, side, block, row):
        for c in range(2):
            vel_ref[c, pl.ds(leaf, 1), :] += ra[c, pl.ds(n, 1), :]

    walk(target_ref, source_ref, live_ref, lists_ref, leaves, 0, spread)


def pair_gap_kernel(x, y, lat, fwd):
    x = jnp.concatenate([x] * 4, axis=1) + lat[0:1, :]
    y = jnp.concatenate([y] * 4, axis=1) + lat[1:2, :]
    w = biot_factor * recip(x * x + y * y + 1.0)
    return dot3(-y * w, fwd[0], fwd[1]), dot3(x * w, fwd[0], fwd[1])


def wave_product(k, g, inv, sign):
    kr, ki, gr, gi = k[:, :256], k[:, 256:], g[:, :256], g[:, 256:]
    if sign < 0:
        wave = jnp.concatenate([kr * gr + ki * gi, kr * gi - ki * gr], axis=1)
    else:
        wave = jnp.concatenate([kr * gr - ki * gi, kr * gi + ki * gr], axis=1)
    return dot3(wave, inv[0], inv[1])


def cross_waves(gamma_ref, up_ref, down_ref, vel_in_ref, target_ref, source_ref, live_ref, lists_ref, own_anc, up_anc, down_anc, fwd, gam, inv, lat, vel_ref, rb, rd, ra):
    leaves = gamma_ref.shape[0]
    sides = (up_ref, down_ref)
    anchors = (up_anc, down_anc)
    vel_ref[...] = vel_in_ref[...]

    def fetch(n, leaf, side, block, row):
        rb[pl.ds(n, 1), :] = sides[side][block, pl.ds(row, 1), :]
        for c in range(2):
            gap = own_anc[2 * (leaf % 2) + c, leaf // 2] - anchors[side][block, 2 * (row % 2) + c, row // 2]
            rd[c, pl.ds(n, 1), :] = jnp.full((1, LANES), gap, f32)

    total = walk(target_ref, source_ref, live_ref, lists_ref, leaves, 1, fetch)

    def pair_group(i, carry):
        rows = pl.ds(pl.multiple_of(i * LANES, LANES), LANES)
        waves = dot3(rb[rows, :], gam[0], gam[1])
        for c, k in enumerate(pair_gap_kernel(rd[0, rows, :], rd[1, rows, :], lat, fwd)):
            ra[c, rows, :] = wave_product(k, waves, inv, 1)
        return carry

    lax.fori_loop(0, (total + LANES - 1) // LANES, pair_group, 0)

    def spread(n, leaf, side, block, row):
        for c in range(2):
            vel_ref[c, pl.ds(leaf, 1), :] += ra[c, pl.ds(n, 1), :]

    walk(target_ref, source_ref, live_ref, lists_ref, leaves, 1, spread)


def regroup_kernel(step, *refs):
    last = step == STEPS - 1
    refs = list(refs)
    take = lambda n: [refs.pop(0) for _ in range(n)]
    vel_ref, shift_ref, g_ref, anchor_ref, dest_ref = take(5)
    if not last:
        first_ref, second_ref, first_row_ref, second_row_ref, fwd, gam, inv, lat, own = take(9)
    (box_ref,) = take(1)
    if not last:
        gamma_ref, spread_ref, next_vel, up_ref, down_ref = take(5)
    px, py, pg, wx, out, nodes, outbox, send_sem, recv_sem, own_sem = take(10)
    if not last:
        block, own_ref, ra, rb, rd, ring_send, ring_recv = take(7)
        leaves = gamma_ref.shape[0]
        halves = lambda ref, m: [ref.at[m, pl.ds(0, leaves // 2)], ref.at[m, pl.ds(leaves // 2, leaves // 2 + 8)]]
        ring = Ring(block, own_ref, up_ref, down_ref, halves, ring_send, ring_recv)
    leaves = g_ref.shape[0]
    strip = lax.axis_index("strip")
    strips = outbox.shape[0]
    barrier = pltpu.get_barrier_semaphore()

    def greet(d, carry):
        pl.semaphore_signal(barrier, inc=1, device_id={"strip": lax.rem(strip + d, strips)})
        return carry

    lax.fori_loop(1, strips, greet, 0)
    if not last:
        for device in ({"grp": ring.left}, {"grp": ring.right}):
            pl.semaphore_signal(barrier, inc=1, device_id=device)

    def remesh(i, carry):
        rows = pl.ds(pl.multiple_of(i * LANES, LANES), LANES)
        for c, dst in ((0, px), (1, py)):
            dst[...] = (shift_ref[c, rows, :] + time_step * vel_ref[c, rows, :]).T
        pg[...] = g_ref[rows, :].T
        remesh_lanes(px, py, pg, wx, out)
        nodes[rows, :] = out[...].T
        return carry

    lax.fori_loop(0, leaves // LANES, remesh, 0)
    dest = dest_ref[...]
    named = jnp.where(lax.broadcasted_iota(jnp.int32, (strips, leaves), 0) == dest, 1.0, 0.0)
    rank = jnp.sum(named * dot(named.astype(bf16), earlier(leaves)), axis=0, keepdims=True)
    hot = [onehot(jnp.where(rank == float(r), named, 0.0) > 0.5) for r in range(2)]
    for r in range(2):
        outbox[:, r, :] = dot_exact(hot[r], nodes[...])
    lane = lax.broadcasted_iota(jnp.int32, (strips, LANES), 1)
    anchors = [dot_exact(hot[r], anchor_ref[...]) for r in range(2)]
    outbox[:, 2, :] = jnp.where(lane < LANES // 2, anchors[0], anchors[1])
    pl.semaphore_wait(barrier, strips - 1 + (0 if last else 2))

    def send(d, carry):
        to = lax.rem(strip + d, strips)
        pltpu.make_async_remote_copy(
            src_ref=outbox.at[to],
            dst_ref=box_ref.at[strip],
            send_sem=send_sem,
            recv_sem=recv_sem,
            device_id={"strip": to},
        ).start()
        return carry

    lax.fori_loop(1, strips, send, 0)
    mine = pltpu.make_async_copy(outbox.at[strip], box_ref.at[strip], own_sem)
    mine.start()
    mine.wait()
    rest = pl.ds(0, strips - 1)
    pltpu.make_async_copy(box_ref.at[rest], box_ref.at[rest], recv_sem).wait()
    pltpu.make_async_copy(outbox.at[rest], outbox.at[rest], send_sem).wait()
    if last:
        return
    for r in range(2):
        block[pl.ds(r, strips, stride=2), :] = box_ref[:, r, :]
    anchors = box_ref[:, 2, :]
    turned = anchors.T
    for q in range(4):
        block[leaves + q : leaves + q + 1, :] = turned[q * (LANES // 4) : q * (LANES // 4) + 1, :]
    block[leaves + 4 : leaves + 8, :] = jnp.zeros((4, LANES), f32)
    ring.first()
    rolled = pltpu.roll(anchors, LANES // 2, 1)
    spread_ref[pl.ds(0, strips, stride=2), :] = jnp.where(lane < LANES // 2, anchors, rolled)
    spread_ref[pl.ds(1, strips, stride=2), :] = jnp.where(lane < LANES // 2, rolled, anchors)
    gamma_ref[...] = block[pl.ds(0, leaves), :]
    field = dot3(gamma_ref[...], own[0], own[1])

    def pair_group(i):
        base = i * LANES

        def fetch(k):
            first = pl.ds(first_ref[base + k], 1)
            second = pl.ds(second_ref[base + k], 1)
            row = pl.ds(base + k, 1)
            ra[0, row, :] = gamma_ref[first, :]
            rb[0, row, :] = gamma_ref[second, :]
            rd[row, :] = spread_ref[first, :] - spread_ref[second, :]

        loop8(LANES, fetch)
        rows = pl.ds(base, LANES)
        gap = rd[rows, :]
        x = jnp.broadcast_to(gap[:, 0:1], (LANES, LANES))
        y = jnp.broadcast_to(gap[:, LANES // 4 : LANES // 4 + 1], (LANES, LANES))
        wa = dot3(ra[0, rows, :], gam[0], gam[1])
        wb = dot3(rb[0, rows, :], gam[0], gam[1])
        for c, k in enumerate(pair_gap_kernel(x, y, lat, fwd)):
            ra[c, rows, :] = wave_product(k, wb, inv, 1)
            rb[c, rows, :] = wave_product(k, wa, inv, -1)

    pair_group(0)
    ring.second()
    for i in range(1, leaves // LANES):
        pair_group(i)
    for c in range(2):
        next_vel[c] = (
            field[:, c * LANES : (c + 1) * LANES]
            + spread_rows(first_row_ref[...], ra[c])
            - spread_rows(second_row_ref[...], rb[c])
        )
    ring.third()
    ring.finish()


def shape(*sizes, dtype=f32):
    return jax.ShapeDtypeStruct(sizes, dtype)


def anywhere():
    return pl.BlockSpec(memory_space=pl.ANY)


def call(kernel, out_shape, in_specs, out_specs, scratch, **kw):
    return pl.pallas_call(
        kernel,
        out_shape=out_shape,
        in_specs=in_specs,
        out_specs=out_specs,
        scratch_shapes=scratch,
        compiler_params=pltpu.CompilerParams(vmem_limit_bytes=48 * 2**20, **kw),
    )


def run_local(state, first, second, target, source, live):
    leaves = state.shape[1]
    groups = lax.axis_size("grp")
    wide = (groups,) + state.shape
    dma = pltpu.SemaphoreType.DMA
    rows = lambda: pltpu.VMEM((3, leaves, LANES), f32)
    return call(
        local_kernel,
        (shape(2, leaves, LANES), shape(groups, 8, leaves, dtype=jnp.int32), shape(*wide), shape(*wide), shape(*wide)),
        [anywhere(), vspec(), sspec(), sspec(), vspec(), vspec(), vspec(), vspec(), sspec()],
        (vspec(), vspec(), anywhere(), anywhere(), anywhere()),
        [pltpu.VMEM((groups, 8, leaves), jnp.int32), tiles(3), tiles(3), tiles(2), tiles(2), rows(), rows()]
        + [dma((12,)), dma((12,)), dma((groups,)), dma((groups,))],
        collective_id=0,
        has_side_effects=True,
    )(state, state, first, second, first[None], second[None], target, source, live)[:4]


def run_cross(state, up, down, vel, target, source, live, lists):
    leaves = state.shape[1]
    most = (1 + up.shape[0]) * leaves
    return call(
        cross_kernel,
        shape(*vel.shape),
        [vspec()] * 4 + [sspec()] * 4,
        vspec(),
        [pltpu.VMEM((2, most, LANES), f32), pltpu.VMEM((3, most, LANES), f32), tiles(2), tiles(3), tiles(2)],
    )(state, up, down, vel, target, source, live, lists)


def run_cross_waves(gamma, up, down, vel, target, source, live, lists, anchors, tables):
    leaves = gamma.shape[0]
    most = (1 + up.shape[0]) * leaves
    fwd, gam, inv, lat, own = tables
    return call(
        cross_waves,
        shape(*vel.shape),
        [vspec()] * 4 + [sspec()] * 7 + [vspec()] * 4,
        vspec(),
        [pltpu.VMEM((most, LANES), f32), pltpu.VMEM((2, most, LANES), f32), pltpu.VMEM((2, most, LANES), f32)],
    )(gamma, up, down, vel, target, source, live, lists, *anchors, fwd, gam, inv, lat)


def run_regroup(step, vel, shifted, gamma, anchor, dest, *more):
    last = step == STEPS - 1
    leaves = gamma.shape[0]
    groups, strips = lax.axis_size("grp"), lax.axis_size("strip")
    dma = pltpu.SemaphoreType.DMA
    box = (strips, 3, LANES)
    out_shape = [shape(*box)]
    in_specs = [vspec()] * 5
    scratch = [tile(), tile(), tile(), pltpu.VMEM((2, WX, LANES), f32), tile(), pltpu.VMEM((leaves, LANES), f32)]
    scratch += [pltpu.VMEM(box, f32), dma, dma, dma]
    if not last:
        block = (leaves + 8, LANES)
        wide = (groups,) + block
        out_shape += [shape(leaves, LANES), shape(leaves, LANES), shape(2, leaves, LANES), shape(*wide), shape(*wide)]
        in_specs += [sspec(), sspec()] + [vspec()] * 7
        rows = lambda n: pltpu.VMEM((n, leaves, LANES), f32)
        scratch += [pltpu.VMEM(block, f32), pltpu.VMEM(wide, f32), rows(2), rows(2), pltpu.VMEM((leaves, LANES), f32)]
        scratch += [dma((12,)), dma((12,))]
    return call(
        functools.partial(regroup_kernel, step),
        tuple(out_shape),
        in_specs,
        (vspec(),) * len(out_shape),
        scratch,
        collective_id=1 + step,
        has_side_effects=True,
    )(vel, shifted, gamma, anchor, dest, *more)


def on_device(
    offsets,
    circulation,
    window_anchor,
    local_first,
    local_offset,
    cross_target,
    cross_source,
    cross_count,
    destination,
):
    leaves = circulation.shape[0]
    strips = lax.axis_size("strip")
    second = (local_first + local_offset) % leaves
    shifted = offsets.transpose(1, 0, 2)
    state = jnp.concatenate([shifted + window_anchor.T[:, :, None], circulation[None]], axis=0)
    anchor = jnp.tile(jnp.repeat(window_anchor, LANES // 4, axis=1), (1, 2))
    tables = [jnp.asarray(t) for t in fourier_tables()]
    lists = (cross_target, cross_source, cross_count)
    vel, inbox, up, down = run_local(state, local_first[0], second[0], *lists)
    vel = run_cross(state, up, down, vel, *lists, inbox)
    dest = destination[:, None, :, 0]
    _, gamma, anchor, vel, up, down = run_regroup(
        0, vel, shifted, circulation, anchor, dest[0],
        local_first[1], second[1], local_first[1:2], second[1:2], *tables,
    )
    own_anchors = anchor[:, :: LANES // 4].reshape(strips, 2, 4)[:, :, :2].reshape(strips, 4).T
    anchors = (own_anchors, up[:, leaves : leaves + 4], down[:, leaves : leaves + 4])
    vel = run_cross_waves(gamma, up, down, vel, *lists, inbox, anchors, tables)
    node = jnp.arange(LANES, dtype=jnp.int32)
    grid = jnp.stack([node // WY, node % WY]).astype(f32)
    shifted = jnp.broadcast_to(grid[:, None, :], vel.shape)
    (box,) = run_regroup(1, vel, shifted, gamma, anchor, dest[1])
    return box[:, :2].reshape(leaves, LANES), box[:, 2, :: LANES // 4].reshape(leaves, 2)


def solution(mesh):
    rows = P(("strip", "grp"))
    lists = P(None, ("strip", "grp"))
    return jax.shard_map(
        on_device,
        mesh=mesh,
        in_specs=(rows, rows, rows, lists, lists, lists, lists, lists, lists),
        out_specs=(rows, rows),
        check_vma=False,
    )
```

time: 885 us -> 141 us (0.16)
  the two profiles are of different devices: /device:TPU:1 before, /device:TPU:19 now
where the time goes in v2:
time: 141 us
  Pallas kernels  127 us (90%)
  local copies, waits for them, and re-layouts  8.96 us (6%)
  other arithmetic  3.56 us (3%)
    pallas_call x2, Pallas kernels, run_regroup(): call(functools.partial(regroup_kernel, step), tuple(out_shape), in_specs,...  72.1 us
    pallas_call x1, Pallas kernels, run_local(): call(local_kernel, (shape(2, leaves, LANES), shape(groups, 8, leaves, dty...  30.6 us
    pallas_call x1, Pallas kernels, run_cross(): call(cross_kernel, shape(*vel.shape), [vspec()] * 4 + [sspec()] * 4, vspe...  12.5 us
    pallas_call x1, Pallas kernels, run_cross_waves(): call(cross_waves, shape(*vel.shape), [vspec()] * 4 + [sspec()] * 7 + [vsp...  12 us
    unnamed x34, local copies, waits for them, and re-layouts  5.45 us

profile of v2, /device:TPU:19, one launch (start us, length us, event | category | flops | bytes accessed | tf_op | source)
XLA Modules:
  0.0 140.7 jit_solution(14577371410558066522)
XLA Ops:
  0.6 0.7 and_select_fusion
  1.4 0.8 fusion.1
  2.1 0.7 copy.24.live_ref
  2.9 1.1 broadcast_add_fusion
  4.0 0.9 pad_maximum_fusion.block_ref.state_ref
  4.9 0.7 copy-done.8
  5.6 0.7 copy-done.10
  6.3 30.6 %shard_map.149 = (f32[2,256,128]{2,1,0:T(8,128)S(1)}, s32[4,8,256]{2,1,0:T(8,128)S(1)}, f32[4,3,256,128]{3,2,1,0:T(8,128)S(1)}, f32[4,3,256,128]{3,2,1,0:T(8,128)S(1)}, f32[4,3,256,128]{3,2,1,0:T(8,128)}) custom-call(f32[3,256,128]{2,1,0:T(8,128)S(1)} %pad_maximum_fusion.block_ref.state_ref, f32[3,256,128]{2,1,0:T(8,128)S(1)} %pad_maximum_fusion.block_ref.state_ref, ...), custom_call_target="tpu_custom_call" | custom-call | tf_op jit(solution)/shard_map/pallas_call | solution.py:676
  37.0 12.5 %shard_map.150.refs_0_ = f32[2,256,128]{2,1,0:T(8,128)S(1)} custom-call(f32[3,256,128]{2,1,0:T(8,128)S(1)} %pad_maximum_fusion.block_ref.state_ref, f32[4,3,256,128]{3,2,1,0:T(8,128)S(1)} %get-tuple-element.11.up_ref, f32[4,3,256,128]{3,2,1,0:T(8,128)S(1)} %get-tuple-element.12.down_ref, f32[2,256,128]{2,1,0:T(8,128)S(1)} %get-tuple-element.13.vel_in_ref, ...), custom_call_target="tpu_custom_call" | custom-call | tf_op jit(solution)/shard_map/pallas_call | solution.py:691
  49.6 0.1 copy.26.refs_3_
  49.8 0.9 copy-done.6
  50.7 45.1 %shard_map.151 = (f32[128,3,128]{2,1,0:T(4,128)}, f32[256,128]{1,0:T(8,128)S(1)}, f32[256,128]{1,0:T(8,128)S(1)}, f32[2,256,128]{2,1,0:T(8,128)S(1)}, f32[4,264,...) custom-call(f32[2,256,128]{2,1,0:T(8,128)S(1)} %shard_map.150.refs_0_, f32[2,256,128]{2,1,0:T(8,128)S(1)} %bitcast.23, ...), custom_call_target="tpu_custom_call" | custom-call | tf_op jit(solution)/shard_map/pallas_call | solution.py:731
  95.8 0.7 copy-done.4
  96.5 0.3 slice.45
  96.8 0.1 copy.30
  96.9 0.9 copy-done.5
  97.8 12.0 %shard_map.152.refs_0_ = f32[2,256,128]{2,1,0:T(8,128)S(1)} custom-call(f32[256,128]{1,0:T(8,128)S(1)} %get-tuple-element.15.gamma_ref.refs_2_, f32[4,264,128]{2,1,0:T(8,128)S(1)} %get-tuple-element.16.up_ref, f32[4,264,128]{2,1,0:T(8,128)S(1)} %get-tuple-element.17.down_ref, f32[2,256,128]{2,1,0:T(8,128)S(1)} %copy-done.5, s32[2,256]{1,0:T(2,128)S(1)} %copy-done.9, ...), custom_call_target="tpu_custom_call" | custom-call | tf_op jit(solution)/shard_map/pallas_call | solution.py:704
  109.9 27.0 %shard_map.153 = f32[128,3,128]{2,1,0:T(4,128)S(1)} custom-call(f32[2,256,128]{2,1,0:T(8,128)S(1)} %shard_map.152.refs_0_, f32[2,256,128]{2,1,0:T(8,128)S(1)} %broadcast_in_dim.15.refs_1_, f32[256,128]{1,0:T(8,128)S(1)} %get-tuple-element.15.gamma_ref.refs_2_, f32[256,128]{1,0:T(8,128)S(1)} %get-tuple-element.19.refs_3_, s32[1,256]{1,0:T(1,128)S(1)} %get-tuple-element.24.refs_4_), custom_call_target="tpu_custom_call" | custom-call | tf_op jit(solution)/shard_map/pallas_call | solution.py:731
  136.9 1.0 slice.51
  137.9 0.5 broadcast.105
  138.5 0.8 reduce.3
  139.3 0.1 reshape_squeeze.3
  139.4 0.7 copy.29
  140.0 0.7 slice.50
  (34 shorter events, 0.2 us)
Async XLA Ops:
  0.6 36.3 %copy-start.9 = (s32[2,256]{1,0:T(2,128)S(1)}, s32[2,256]{1,0:T(2,128)}, u32[]{:S(2)}) copy-start(s32[2,256]{1,0:T(2,128)} %target_ref.5) | copy-start | bytes 6148
  4.9 0.7 copy-start.8
  5.6 0.7 copy-start.10
  36.9 12.6 %copy-start.14 = (s32[2,256,1]{1,2,0:T(1,128)S(1)}, s32[2,256,1]{1,2,0:T(1,128)}, u32[]{:S(2)}) copy-start(s32[2,256,1]{1,2,0:T(1,128)} %param.22) | copy-start | bytes 6148
  36.9 12.6 %copy-start.13 = (f32[256,2]{0,1:T(2,128)S(1)}, f32[256,2]{0,1:T(2,128)}, u32[]{:S(2)}) copy-start(f32[256,2]{0,1:T(2,128)} %param.16) | copy-start | bytes 6148
  37.0 12.8 %copy-start.12 = (f32[256,2,128]{2,1,0:T(2,128)S(1)}, f32[256,2,128]{2,1,0:T(2,128)}, u32[]{:S(2)}) copy-start(f32[256,2,128]{2,1,0:T(2,128)} %param.14) | copy-start | bytes 786436
  37.0 12.8 %copy-start = (bf16[2,512,512]{2,1,0:T(8,128)(2,1)S(1)}, bf16[2,512,512]{2,1,0:T(8,128)(2,1)}, u32[]{:S(2)}) copy-start(bf16[2,512,512]{2,1,0:T(8,128)(2,1)} %constant.55.clone.refs_9_.fwd) | copy-start | bytes 3145732
  37.0 12.8 %copy-start.1 = (bf16[2,128,512]{2,1,0:T(8,128)(2,1)S(1)}, bf16[2,128,512]{2,1,0:T(8,128)(2,1)}, u32[]{:S(2)}) copy-start(bf16[2,128,512]{2,1,0:T(8,128)(2,1)} %constant.56.clone.refs_10_.gam) | copy-start | bytes 786436
  37.0 12.8 %copy-start.2 = (bf16[2,512,128]{2,1,0:T(8,128)(2,1)S(1)}, bf16[2,512,128]{2,1,0:T(8,128)(2,1)}, u32[]{:S(2)}) copy-start(bf16[2,512,128]{2,1,0:T(8,128)(2,1)} %constant.57.clone.refs_11_.inv) | copy-start | bytes 786436
  37.0 12.8 %copy-start.3 = (f32[256,128]{1,0:T(8,128)S(1)}, f32[256,128]{1,0:T(8,128)}, u32[]{:S(2)}) copy-start(f32[256,128]{1,0:T(8,128)} %refs_2_.1) | copy-start | bytes 393220
  37.0 12.8 %copy-start.7 = (f32[8,512]{1,0:T(8,128)S(1)}, f32[8,512]{1,0:T(8,128)}, u32[]{:S(2)}) copy-start(f32[8,512]{1,0:T(8,128)} %constant.58.clone.refs_12_.lat) | copy-start | bytes 49156
  49.8 0.9 copy-start.6
  50.7 46.2 %copy-start.11 = (s32[2,256]{1,0:T(2,128)S(1)}, s32[2,256]{1,0:T(2,128)}, u32[]{:S(2)}) copy-start(s32[2,256]{1,0:T(2,128)} %source_ref.5) | copy-start | bytes 6148
  95.8 0.7 copy-start.4
  96.9 1.0 copy-start.5

commit v3 on v2

v3 whole, which is shorter than its diff:
```python
import functools
import jax
import jax.numpy as jnp
import numpy as np
from jax import lax
from jax.experimental import pallas as pl
from jax.experimental.pallas import tpu as pltpu
from jax.sharding import PartitionSpec as P

WX = 8
WY = 16
STEPS = 2
time_step = 0.5
biot_factor = 0.15915494309189535
LANES = 128
f32 = jnp.float32
bf16 = jnp.bfloat16


def recip(x):
    return pl.reciprocal(x, approx=True)


def mutual_lanes(a_refs, b_refs, on_a, on_b, between):
    xa_ref, ya_ref, ga_ref = a_refs
    xb_ref, yb_ref, gb_ref = b_refs
    ua_ref, va_ref = on_a
    ub_ref, vb_ref = on_b
    ub_ref[...] = jnp.zeros_like(ub_ref)
    vb_ref[...] = jnp.zeros_like(vb_ref)
    zero = jnp.zeros((8, LANES), f32)

    def over_a(ia, carry):
        a0 = pl.multiple_of(ia * 8, 8)

        def over_b(ib, acc):
            acc = list(acc)
            rows = pl.ds(pl.multiple_of(ib * 8, 8), 8)
            xb, yb, gb = xb_ref[rows, :], yb_ref[rows, :], gb_ref[rows, :]
            ub, vb = ub_ref[rows, :], vb_ref[rows, :]
            for r in range(8):
                row = pl.ds(a0 + r, 1)
                dx = xa_ref[row, :] - xb
                dy = ya_ref[row, :] - yb
                w = recip(dx * dx + dy * dy + 1.0)
                tx = dx * w
                ty = dy * w
                acc[r] = acc[r] + gb * ty
                acc[8 + r] = acc[8 + r] + gb * tx
                ga = ga_ref[row, :]
                ub = ub + ga * ty
                vb = vb + ga * tx
            ub_ref[rows, :] = ub
            vb_ref[rows, :] = vb
            return tuple(acc)

        acc = lax.fori_loop(0, 16, over_b, (zero,) * 16, unroll=8)
        for r in range(8):
            ua_ref[pl.ds(a0 + r, 1), :] = jnp.sum(acc[r], axis=0, keepdims=True)
            va_ref[pl.ds(a0 + r, 1), :] = jnp.sum(acc[8 + r], axis=0, keepdims=True)
        return carry

    lax.fori_loop(0, 8, over_a, 0)
    between()
    lax.fori_loop(8, 16, over_a, 0)


def loop8(count, body):
    def eight(k, carry):
        for u in range(8):
            body(k * 8 + u)
        return carry

    lax.fori_loop(0, (count + 7) // 8, eight, 0)


def node_weight(distance):
    r = jnp.abs(distance)
    inner = 1.0 + r * r * (1.5 * r - 2.5)
    s = jnp.maximum(2.0 - r, 0.0)
    outer = (0.5 * s) * s * (1.0 - r)
    return jnp.where(r < 1.0, inner, outer)


def remesh_lanes(px_ref, py_ref, g_ref, wx_ref, nodes_ref):
    ix = lax.broadcasted_iota(jnp.int32, (WX, LANES), 0).astype(f32)
    iy = lax.broadcasted_iota(jnp.int32, (WX, LANES), 0).astype(f32)

    def over_p(p4, acc):
        acc = list(acc)
        for u in range(4):
            p = p4 * 4 + u
            row = pl.ds(p, 1)
            wx_ref[u] = node_weight(px_ref[row, :] - ix) * g_ref[row, :]
            y = py_ref[row, :] - iy
            wy = (node_weight(y), node_weight(y - 8.0))
            for i in range(WX):
                wxi = wx_ref[u, i : i + 1, :]
                for h in range(2):
                    acc[2 * i + h] = acc[2 * i + h] + wxi * wy[h]
        return tuple(acc)

    acc = lax.fori_loop(0, LANES // 4, over_p, (jnp.zeros((8, LANES), f32),) * 16)
    for i in range(16):
        nodes_ref[8 * i : 8 * i + 8, :] = acc[i]


def split(x):
    hi = x.astype(bf16)
    return hi, (x - hi.astype(f32)).astype(bf16)


def dot3(x, m_hi, m_lo):
    hi, lo = split(x)
    n = x.shape[0]
    both = dot(jnp.concatenate([hi, lo], axis=0), m_hi)
    return both[:n] + (both[n:] + dot(hi, m_lo))


def dot(a, b):
    return jnp.dot(a, b, preferred_element_type=f32)


@functools.cache
def fourier_tables():
    n1, n2 = 2 * WX - 1, 2 * WY - 1
    size = n1 * n2
    u = np.arange(n1)
    v = np.arange(n2)
    di = np.where(u < WX, u, u - n1)
    dj = np.where(v < WY, v, v - n2)
    DI, DJ = [t.reshape(-1).astype(np.float64) for t in np.meshgrid(di, dj, indexing="ij")]
    k1, k2 = [t.reshape(-1) for t in np.meshgrid(u, v, indexing="ij")]
    keep = [0]
    for m in range(1, size):
        mirror = ((-k1[m]) % n1) * n2 + ((-k2[m]) % n2)
        if m < mirror:
            keep.append(m)
    f1, f2 = k1[keep].astype(np.float64), k2[keep].astype(np.float64)
    nf = len(keep)

    def phase(i, j):
        return 2 * np.pi * (np.outer(i, f1) / n1 + np.outer(j, f2) / n2)

    forward = np.zeros((512, 512))
    p = phase(DI, DJ)
    forward[:size, :nf] = np.cos(p)
    forward[:size, 256 : 256 + nf] = -np.sin(p)
    node = np.arange(WX * WY)
    q = phase(node // WY, node % WY)
    gamma = np.zeros((128, 512))
    gamma[:, :nf] = np.cos(q)
    gamma[:, 256 : 256 + nf] = -np.sin(q)
    weight = np.full(nf, 2.0 / size)
    weight[0] = 1.0 / size
    inverse = np.zeros((512, 128))
    inverse[:nf] = weight[:, None] * np.cos(q).T
    inverse[256 : 256 + nf] = -weight[:, None] * np.sin(q).T
    lattice = np.zeros((8, 512))
    lattice[0, :size] = DI
    lattice[1, :size] = DJ
    ddx = (node // WY)[:, None] - (node // WY)[None, :]
    ddy = (node % WY)[:, None] - (node % WY)[None, :]
    w = biot_factor / (ddx * ddx + ddy * ddy + 1.0)
    own = np.concatenate([(-ddy * w).T, (ddx * w).T], axis=1)

    def halves(x):
        hi = x.astype(np.float32).astype(bf16)
        lo = (x - hi.astype(np.float64)).astype(np.float32).astype(bf16)
        return np.stack([hi, lo])

    return halves(forward), halves(gamma), halves(inverse), lattice.astype(np.float32), halves(own)


def vspec():
    return pl.BlockSpec(memory_space=pltpu.VMEM)


def sspec():
    return pl.BlockSpec(memory_space=pltpu.SMEM)


def tile():
    return pltpu.VMEM((LANES, LANES), f32)


def tiles(n):
    return pltpu.VMEM((n, LANES, LANES), f32)


def one_sided_lanes(a_refs, b_refs, on_a, chunks=2):
    xa_ref, ya_ref = a_refs
    xb_ref, yb_ref, gb_ref = b_refs
    ua_ref, va_ref = on_a
    zero = jnp.zeros((8, LANES), f32)

    def over_a(ia, carry):
        a0 = pl.multiple_of(ia * 8, 8)

        def over_b(chunk, u, acc):
            acc = list(acc)
            rows = pl.ds(pl.multiple_of(chunk * 64 + u * 8, 8), 8)
            xb, yb, gb = xb_ref[rows, :], yb_ref[rows, :], gb_ref[rows, :]
            for r in range(8):
                row = pl.ds(a0 + r, 1)
                dx = xa_ref[row, :] - xb
                dy = ya_ref[row, :] - yb
                w = gb * recip(dx * dx + (dy * dy + 1.0))
                acc[r] = acc[r] + dy * w
                acc[8 + r] = acc[8 + r] + dx * w
            return tuple(acc)

        def over_chunk(chunk, acc):
            for u in range(8):
                acc = over_b(chunk, u, acc)
            return acc

        acc = lax.fori_loop(0, chunks, over_chunk, (zero,) * 16)
        for r in range(8):
            ua_ref[pl.ds(a0 + r, 1), :] = jnp.sum(acc[r], axis=0, keepdims=True)
            va_ref[pl.ds(a0 + r, 1), :] = jnp.sum(acc[8 + r], axis=0, keepdims=True)
        return carry

    lax.fori_loop(0, 16, over_a, 0)


def onehot(condition):
    return jnp.where(condition, 1.0, 0.0).astype(bf16)


def dot_exact(hot, x):
    hi, rest = split(x)[0], None
    rest = x - hi.astype(f32)
    mid, lo = split(rest)
    return (dot(hot, hi) + dot(hot, mid)) + dot(hot, lo)


def dot_near(hot, x):
    hi, lo = split(x)
    return dot(hot, hi) + dot(hot, lo)


def spread_rows(index_row, x):
    leaves = index_row.shape[1]
    places = lax.broadcasted_iota(jnp.int32, (leaves, leaves), 0)
    return dot_near(onehot(places == index_row), x)


def earlier(n):
    return onehot(lax.broadcasted_iota(jnp.int32, (n, n), 0) < lax.broadcasted_iota(jnp.int32, (n, n), 1))


def sort_lists(target_ref, source_ref, live_ref, outbox):
    groups = outbox.shape[0]
    n = target_ref.shape[1]
    before = earlier(n)
    rows8 = lax.broadcasted_iota(jnp.int32, (8, n), 0)
    places = lax.broadcasted_iota(jnp.int32, (n, n), 0)
    k = lax.broadcasted_iota(jnp.int32, (1, n), 1)
    outbox[...] = jnp.zeros_like(outbox)
    for step in range(STEPS):
        source = source_ref[step : step + 1, :]
        owner = lax.shift_right_logical(source, n.bit_length() - 1)
        key = jnp.where(k < live_ref[0, step], owner, groups)
        row = jnp.bitwise_and(source, n - 1)
        mine = jnp.where(rows8 == key, 1.0, 0.0)
        place = jnp.sum(mine * dot(mine.astype(bf16), before), axis=0, keepdims=True).astype(jnp.int32)
        values = jnp.where(rows8 == 0, target_ref[step : step + 1, :], jnp.where(rows8 == 1, row, 0))
        values = values.astype(f32).astype(bf16)
        count = jnp.sum(mine, axis=1, keepdims=True).astype(jnp.int32)
        for b in range(groups):
            hot = onehot((places == place) & (key == b))
            found = lax.dot_general(values, hot, (((1,), (1,)), ((), ())), preferred_element_type=f32)
            outbox[b, 2 * step : 2 * step + 2, :] = found[0:2, :].astype(jnp.int32)
            outbox[b, 4 + step : 5 + step, :] = jnp.broadcast_to(count[b : b + 1, :], (1, n))


class Ring:
    def __init__(self, block, own, up, down, part, chunk, send_sem, recv_sem):
        start, size, first = chunk
        self.block = part(block, start, size)
        view = lambda ref: lambda member: part(ref, start, size, member)
        self.own, self.up, self.down = view(own), view(up), view(down)
        self.halves = (
            lambda member: part(own, start, first, member),
            lambda member: part(own, start + first, size - first, member),
        )
        self.send_sem, self.recv_sem = send_sem, recv_sem
        self.grp = lax.axis_index("grp")
        groups = lax.axis_size("grp")
        self.right = lax.rem(self.grp + 1, groups)
        self.left = lax.rem(self.grp + groups - 1, groups)
        self.across = lax.rem(self.grp + 2, groups)
        strip, strips = lax.axis_index("strip"), lax.axis_size("strip")
        self.above = lax.rem(strip + 1, strips)
        self.below = lax.rem(strip + strips - 1, strips)
        self.sent = []

    def send(self, src, dst, device, slot):
        copy = pltpu.make_async_remote_copy(
            src_ref=src,
            dst_ref=dst,
            send_sem=self.send_sem.at[slot],
            recv_sem=self.recv_sem.at[slot],
            device_id=device,
        )
        copy.start()
        self.sent.append(copy)
        return copy

    def to_strips(self, src, member, slot):
        return [
            self.send(src, self.down(member), {"strip": self.above}, slot),
            self.send(src, self.up(member), {"strip": self.below}, slot + 1),
        ]

    def first(self):
        self.from_left = self.send(self.block, self.own(self.grp), {"grp": self.right}, 0)
        self.from_right = self.send(self.block, self.own(self.grp), {"grp": self.left}, 1)
        self.last = self.to_strips(self.block, self.grp, 2)

    def second(self):
        self.from_left.wait_recv()
        half = self.halves[0](self.left)
        self.half_a = self.send(half, half, {"grp": self.right}, 4)
        self.last += self.to_strips(self.own(self.left), self.left, 5)
        self.from_right.wait_recv()
        half = self.halves[1](self.right)
        self.half_b = self.send(half, half, {"grp": self.left}, 7)
        self.last += self.to_strips(self.own(self.right), self.right, 8)

    def third(self):
        self.half_a.wait_recv()
        self.half_b.wait_recv()
        self.last += self.to_strips(self.own(self.across), self.across, 10)

    def finish(self):
        for copy in self.last:
            copy.wait_recv()
        for copy in self.sent:
            copy.wait_send()


class Rings:
    def __init__(self, block, own, up, down, part, chunks, send_sem, recv_sem):
        self.rings = [
            Ring(block, own, up, down, part, chunk, send_sem.at[i], recv_sem.at[i]) for i, chunk in enumerate(chunks)
        ]

    def first(self):
        for ring in self.rings:
            ring.first()

    def second(self):
        for ring in self.rings:
            ring.second()

    def third(self):
        for ring in self.rings:
            ring.third()

    def finish(self):
        for ring in self.rings:
            ring.finish()


def local_kernel(
    offset_in,
    gamma_in,
    anchor_in,
    first_in,
    shift_in,
    target_in,
    source_in,
    live_ref,
    state_ref,
    vel_ref,
    lists_ref,
    first_out,
    second_out,
    target_ref,
    source_ref,
    up_ref,
    down_ref,
    own_ref,
    offset_ref,
    gamma_ref,
    anchor_ref,
    shift_ref,
    first_ref,
    second_ref,
    outbox,
    ta,
    tb,
    oa,
    ob,
    ra,
    rb,
    load_sem,
    send_sem,
    recv_sem,
    list_send,
    list_recv,
):
    loaded = load_tables(
        [
            (offset_in, offset_ref),
            (gamma_in, gamma_ref),
            (anchor_in, anchor_ref),
            (first_in, first_out),
            (shift_in, shift_ref),
            (target_in, target_ref),
            (source_in, source_ref),
            (first_in, first_ref),
            (shift_in, second_ref),
        ],
        load_sem,
    )
    leaves = gamma_ref.shape[0]
    blocks = range(leaves // LANES)
    part = lambda ref, start, size, *member: ref.at[(*member, slice(None), pl.ds(start, size))]
    cut = leaves // 2
    chunks = [(0, cut, cut // 2), (cut, cut, cut // 2)]
    rings = Rings(state_ref, own_ref, up_ref, down_ref, part, chunks, send_sem, recv_sem)
    ring = rings.rings[0]
    groups = lists_ref.shape[0]
    barrier = pltpu.get_barrier_semaphore()
    for device in ({"grp": ring.left}, {"grp": ring.right}, {"strip": ring.above}):
        pl.semaphore_signal(barrier, inc=1, device_id=device)
    for j in range(groups):
        pl.semaphore_signal(barrier, inc=1, device_id={"strip": ring.below, "grp": j})
    loaded()
    second_out[...] = jnp.bitwise_and(first_out[...] + shift_ref[...], leaves - 1)
    for h in blocks:
        rows = pl.ds(h * LANES, LANES)
        for c in range(2):
            column = jnp.broadcast_to(anchor_ref[c : c + 1, h * LANES : (h + 1) * LANES], (LANES, LANES)).T
            state_ref[c, rows, :] = offset_ref[rows, c, :] + column
        state_ref[2, rows, :] = gamma_ref[rows, :]
    pl.semaphore_wait(barrier, 3 + groups)
    rings.first()
    sort_lists(target_ref, source_ref, live_ref, outbox)
    mail = []
    for j in range(groups):
        peer = lax.rem(ring.grp + j, groups)
        copy = pltpu.make_async_remote_copy(
            src_ref=outbox.at[peer],
            dst_ref=lists_ref.at[ring.grp],
            send_sem=list_send.at[j],
            recv_sem=list_recv.at[j],
            device_id={"strip": ring.above, "grp": peer},
        )
        copy.start()
        mail.append(copy)

    def self_group(i, carry):
        rows = pl.ds(pl.multiple_of(i * LANES, LANES), LANES)
        for c in range(3):
            ta[c] = state_ref[c, rows, :].T
        one_sided_lanes((ta.at[0], ta.at[1]), (ta.at[0], ta.at[1], ta.at[2]), (oa.at[0], oa.at[1]))
        vel_ref[0, rows, :] = oa[0].T * -biot_factor
        vel_ref[1, rows, :] = oa[1].T * biot_factor
        return carry

    def pair_group(i, between):
        base = i * LANES
        rows = pl.ds(base, LANES)

        def fetch(k):
            first = first_ref[0, base + k]
            second = jnp.bitwise_and(first + second_ref[0, base + k], leaves - 1)
            for c in range(3):
                ra[c, pl.ds(base + k, 1), :] = state_ref[c, pl.ds(first, 1), :]
                rb[c, pl.ds(base + k, 1), :] = state_ref[c, pl.ds(second, 1), :]

        loop8(LANES, fetch)
        for c in range(3):
            ta[c] = ra[c, rows, :].T
            tb[c] = rb[c, rows, :].T
        mutual_lanes(
            [ta.at[c] for c in range(3)],
            [tb.at[c] for c in range(3)],
            [oa.at[c] for c in range(2)],
            [ob.at[c] for c in range(2)],
            between,
        )
        ra[0, rows, :] = oa[0].T * -biot_factor
        ra[1, rows, :] = oa[1].T * biot_factor
        rb[0, rows, :] = ob[0].T * biot_factor
        rb[1, rows, :] = ob[1].T * -biot_factor

    lax.fori_loop(0, leaves // LANES, self_group, 0)
    rings.second()
    for i in blocks:
        pair_group(i, rings.third if i == 0 else lambda: None)
    for c in range(2):
        vel_ref[c] += spread_rows(first_out[0:1, :], ra[c]) + spread_rows(second_out[0:1, :], rb[c])
    rings.finish()
    for copy in mail:
        copy.wait()


def walk(target_ref, source_ref, live_ref, lists_ref, leaves, step, visit):
    live = live_ref[0, step]
    shift = leaves.bit_length() - 1

    def mine(k):
        source = source_ref[step, k]
        block, row = lax.shift_right_logical(source, shift), jnp.bitwise_and(source, leaves - 1)
        visit(k, jnp.where(k < live, target_ref[step, k], leaves), 0, block, row)

    loop8(live, mine)
    base = live
    for g in range(lists_ref.shape[0]):
        count = lists_ref[g, 4 + step, 0]

        def theirs(k, g=g, base=base, count=count):
            leaf = jnp.where(k < count, lists_ref[g, 2 * step + 1, k], leaves)
            visit(base + k, leaf, 1, g, lists_ref[g, 2 * step, k])

        loop8(count, theirs)
        base = base + count
    return base


def cross_kernel(state_ref, up_ref, down_ref, vel_in_ref, target_ref, source_ref, live_ref, lists_ref, vel_ref, ra, rb, ta, tb, oa, total_ref):
    leaves = state_ref.shape[1]
    sides = (up_ref, down_ref)
    for c in range(2):
        total_ref[c, pl.ds(0, leaves), :] = vel_in_ref[c]

    def fetch(n, leaf, side, block, row):
        own = jnp.minimum(leaf, leaves - 1)
        for c in range(2):
            ra[c, pl.ds(n, 1), :] = state_ref[c, pl.ds(own, 1), :]
        for c in range(3):
            rb[c, pl.ds(n, 1), :] = sides[side][block, c, pl.ds(row, 1), :]

    total = walk(target_ref, source_ref, live_ref, lists_ref, leaves, 0, fetch)

    def pair_group(i, carry):
        rows = pl.ds(pl.multiple_of(i * LANES, LANES), LANES)
        half = LANES // 2
        few = total - i * LANES <= half

        @pl.when(few)
        def _():
            low = pl.ds(pl.multiple_of(i * LANES, LANES), half)
            high = pl.ds(pl.multiple_of(i * LANES + half, half), half)
            for c in range(2):
                ra[c, high, :] = ra[c, low, :]
            for c in range(3):
                rb[c, high, :] = pltpu.roll(rb[c, low, :], half, 1)

        for c in range(2):
            ta[c] = ra[c, rows, :].T
        for c in range(3):
            tb[c] = rb[c, rows, :].T
        one_sided_lanes(
            [ta.at[c] for c in range(2)],
            [tb.at[c] for c in range(3)],
            [oa.at[c] for c in range(2)],
            jnp.where(few, 1, 2),
        )
        for c, sign in ((0, -biot_factor), (1, biot_factor)):
            found = oa[c].T * sign
            ra[c, rows, :] = found
            ra[c, pl.ds(pl.multiple_of(i * LANES, LANES), half), :] = found[:half] + jnp.where(few, found[half:], 0.0)
        return carry

    lax.fori_loop(0, (total + LANES - 1) // LANES, pair_group, 0)

    def spread(n, leaf, side, block, row):
        for c in range(2):
            total_ref[c, pl.ds(leaf, 1), :] += ra[c, pl.ds(n, 1), :]

    walk(target_ref, source_ref, live_ref, lists_ref, leaves, 0, spread)
    for c in range(2):
        vel_ref[c] = total_ref[c, pl.ds(0, leaves), :]


def lattice_waves(x, y, lat, fwd):
    n = x.shape[0]
    x = jnp.concatenate([x] * 4, axis=1) + lat[0:1, :]
    y = jnp.concatenate([y] * 4, axis=1) + lat[1:2, :]
    w = biot_factor * recip(x * x + y * y + 1.0)
    waves = dot3(jnp.concatenate([-y * w, x * w], axis=0), fwd[0], fwd[1])
    return waves[:n], waves[n:]


def wave_product(k, g, sign):
    kr, ki, gr, gi = k[:, :256], k[:, 256:], g[:, :256], g[:, 256:]
    if sign < 0:
        return jnp.concatenate([kr * gr + ki * gi, kr * gi - ki * gr], axis=1)
    return jnp.concatenate([kr * gr - ki * gi, kr * gi + ki * gr], axis=1)


def load_tables(pairs, sem):
    copies = [pltpu.make_async_copy(src, dst, sem.at[i]) for i, (src, dst) in enumerate(pairs)]
    for copy in copies:
        copy.start()

    def wait():
        for copy in copies:
            copy.wait()

    return wait


def spread_anchors(anchor_ref, half):
    cols = slice(half * LANES, (half + 1) * LANES)
    part = [jnp.broadcast_to(anchor_ref[c : c + 1, cols], (LANES // 4, LANES)) for c in range(2)]
    return jnp.concatenate(part + part, axis=0).T


def cross_waves(
    spread_ref,
    up_ref,
    down_ref,
    vel_in_ref,
    target_ref,
    source_ref,
    live_ref,
    lists_ref,
    fwd_in,
    gam_in,
    inv_in,
    lat,
    vel_ref,
    rb,
    rd,
    ra,
    total_ref,
    far_anc,
    fwd,
    gam,
    inv,
    sem,
):
    leaves = vel_in_ref.shape[1]
    sides = (up_ref, down_ref)
    ready = load_tables([(fwd_in, fwd), (gam_in, gam), (inv_in, inv)], sem)
    quarter = LANES // 4
    for side in range(2):
        for b in range(up_ref.shape[0]):
            lines = [
                jnp.broadcast_to(sides[side][b, leaves + q : leaves + q + 1, :], (quarter, LANES)) for q in range(4)
            ]
            anchors = jnp.concatenate(lines, axis=0).T
            far_anc[side, b, pl.ds(0, LANES, stride=2), :] = anchors
            far_anc[side, b, pl.ds(1, LANES, stride=2), :] = pltpu.roll(anchors, LANES // 2, 1)
    for c in range(2):
        total_ref[c, pl.ds(0, leaves), :] = vel_in_ref[c]

    def fetch(n, leaf, side, block, row):
        rb[pl.ds(n, 1), :] = sides[side][block, pl.ds(row, 1), :]
        own = jnp.minimum(leaf, leaves - 1)
        rd[pl.ds(n, 1), :] = spread_ref[pl.ds(own, 1), :] - far_anc[side, block, pl.ds(row, 1), :]

    total = walk(target_ref, source_ref, live_ref, lists_ref, leaves, 1, fetch)
    ready()

    def pair_group(i, carry):
        rows = pl.ds(pl.multiple_of(i * LANES, LANES), LANES)
        waves = dot3(rb[rows, :], gam[0], gam[1])
        gap = rd[rows, :]
        x = jnp.broadcast_to(gap[:, 0:1], (LANES, LANES))
        y = jnp.broadcast_to(gap[:, quarter : quarter + 1], (LANES, LANES))
        products = [wave_product(k, waves, 1) for k in lattice_waves(x, y, lat, fwd)]
        found = dot3(jnp.concatenate(products, axis=0), inv[0], inv[1])
        ra[0, rows, :] = found[:LANES]
        ra[1, rows, :] = found[LANES:]
        return carry

    lax.fori_loop(0, (total + LANES - 1) // LANES, pair_group, 0)

    def spread(n, leaf, side, block, row):
        for c in range(2):
            total_ref[c, pl.ds(leaf, 1), :] += ra[c, pl.ds(n, 1), :]

    walk(target_ref, source_ref, live_ref, lists_ref, leaves, 1, spread)
    for c in range(2):
        vel_ref[c] = total_ref[c, pl.ds(0, leaves), :]


def regroup_kernel(step, *refs):
    last = step == STEPS - 1
    refs = list(refs)
    take = lambda n: [refs.pop(0) for _ in range(n)]
    vel_ref, shift_ref, g_ref, anchor_ref, dest_ref = take(5)
    leaves = vel_ref.shape[1]
    if not last:
        first_ref, second_ref, first_row_ref, second_row_ref, fwd_in, gam_in, inv_in, lat, own_in = take(9)
        block, spread_ref, next_vel, up_ref, down_ref = take(5)
    else:
        gamma_ref, final_ref = take(2)
    px, py, pg, wx, out, nodes, outbox, box_ref, send_sem, recv_sem, own_sem = take(11)
    if not last:
        own_ref, ra, rb, rd, fwd, gam, inv, own, ring_send, ring_recv, table_sem = take(11)
        ready = load_tables([(fwd_in, fwd), (gam_in, gam), (inv_in, inv), (own_in, own)], table_sem)
    else:
        (spread_ref,) = take(1)
    if not last:
        part = lambda ref, start, size, *member: ref.at[(*member, pl.ds(start, size))]
        cut = leaves // 2
        chunks = [(0, cut, cut // 2), (cut, cut + 8, cut // 2)]
        rings = Rings(block, own_ref, up_ref, down_ref, part, chunks, ring_send, ring_recv)
        ring = rings.rings[0]
    strip = lax.axis_index("strip")
    strips = outbox.shape[0]
    barrier = pltpu.get_barrier_semaphore()

    def greet(d, carry):
        pl.semaphore_signal(barrier, inc=1, device_id={"strip": jnp.bitwise_and(strip + d, strips - 1)})
        return carry

    lax.fori_loop(1, strips, greet, 0, unroll=8)
    if not last:
        for device in ({"grp": ring.left}, {"grp": ring.right}):
            pl.semaphore_signal(barrier, inc=1, device_id=device)

    def remesh(i, carry):
        rows = pl.ds(pl.multiple_of(i * LANES, LANES), LANES)
        for c, dst in ((0, px), (1, py)):
            if last:
                node = lax.broadcasted_iota(jnp.int32, (LANES, LANES), 0)
                node = jnp.bitwise_and(node, WY - 1) if c else lax.shift_right_logical(node, WY.bit_length() - 1)
                dst[...] = node.astype(f32) + (time_step * vel_ref[c, rows, :]).T
            else:
                dst[...] = (shift_ref[rows, c, :] + time_step * vel_ref[c, rows, :]).T
        pg[...] = g_ref[rows, :].T
        remesh_lanes(px, py, pg, wx, out)
        nodes[rows, :] = out[...].T
        return carry

    lax.fori_loop(0, leaves // LANES, remesh, 0)
    dest = dest_ref[step]
    named = jnp.where(lax.broadcasted_iota(jnp.int32, (strips, leaves), 0) == dest, 1.0, 0.0)
    rank = jnp.sum(named * dot(named.astype(bf16), earlier(leaves)), axis=0, keepdims=True)
    hot = [onehot(jnp.where(rank == float(r), named, 0.0) > 0.5) for r in range(2)]
    for r in range(2):
        outbox[:, r, :] = dot_exact(hot[r], nodes[...])
    lane = lax.broadcasted_iota(jnp.int32, (strips, LANES), 1)
    if last:
        spread = anchor_ref[...]
    else:
        spread = jnp.concatenate([spread_anchors(anchor_ref, h) for h in range(leaves // LANES)], axis=0)
    anchors = [dot_exact(hot[r], spread) for r in range(2)]
    outbox[:, 2, :] = jnp.where(lane < LANES // 2, anchors[0], anchors[1])
    pl.semaphore_wait(barrier, strips - 1 + (0 if last else 2))

    def send(d, carry):
        to = jnp.bitwise_and(strip + d, strips - 1)
        pltpu.make_async_remote_copy(
            src_ref=outbox.at[to],
            dst_ref=box_ref.at[strip],
            send_sem=send_sem,
            recv_sem=recv_sem,
            device_id={"strip": to},
        ).start()
        return carry

    lax.fori_loop(1, strips, send, 0, unroll=8)
    mine = pltpu.make_async_copy(outbox.at[strip], box_ref.at[strip], own_sem)
    mine.start()
    mine.wait()
    rest = pl.ds(0, strips - 1)
    pltpu.make_async_copy(box_ref.at[rest], box_ref.at[rest], recv_sem).wait()
    pltpu.make_async_copy(outbox.at[rest], outbox.at[rest], send_sem).wait()
    anchors = box_ref[:, 2, :]
    rolled = pltpu.roll(anchors, LANES // 2, 1)
    if last:
        for r in range(2):
            gamma_ref[pl.ds(r, strips, stride=2), :] = box_ref[:, r, :]
        spread_ref[pl.ds(0, strips, stride=2), :] = anchors
        spread_ref[pl.ds(1, strips, stride=2), :] = rolled
        for h in range(leaves // LANES):
            turned = spread_ref[pl.ds(h * LANES, LANES), :].T
            for c in range(2):
                row = turned[c * (LANES // 4) : c * (LANES // 4) + 1, :]
                final_ref[c : c + 1, h * LANES : (h + 1) * LANES] = row
        return
    for r in range(2):
        block[pl.ds(r, strips, stride=2), :] = box_ref[:, r, :]
    turned = anchors.T
    for q in range(4):
        block[leaves + q : leaves + q + 1, :] = turned[q * (LANES // 4) : q * (LANES // 4) + 1, :]
    block[leaves + 4 : leaves + 8, :] = jnp.zeros((4, LANES), f32)
    rings.first()
    spread_ref[pl.ds(0, strips, stride=2), :] = jnp.where(lane < LANES // 2, anchors, rolled)
    spread_ref[pl.ds(1, strips, stride=2), :] = jnp.where(lane < LANES // 2, rolled, anchors)
    ready()
    field = dot3(block[pl.ds(0, leaves), :], own[0], own[1])

    def pair_group(i, between):
        base = i * LANES

        def fetch(k):
            first = pl.ds(first_ref[1, base + k], 1)
            second = pl.ds(second_ref[1, base + k], 1)
            row = pl.ds(base + k, 1)
            ra[0, row, :] = block[first, :]
            rb[0, row, :] = block[second, :]
            rd[row, :] = spread_ref[first, :] - spread_ref[second, :]

        loop8(LANES, fetch)
        between()
        rows = pl.ds(base, LANES)
        gap = rd[rows, :]
        x = jnp.broadcast_to(gap[:, 0:1], (LANES, LANES))
        y = jnp.broadcast_to(gap[:, LANES // 4 : LANES // 4 + 1], (LANES, LANES))
        waves = dot3(jnp.concatenate([ra[0, rows, :], rb[0, rows, :]], axis=0), gam[0], gam[1])
        wa, wb = waves[:LANES], waves[LANES:]
        kernels = lattice_waves(x, y, lat, fwd)
        products = [wave_product(k, wb, 1) for k in kernels] + [wave_product(k, wa, -1) for k in kernels]
        found = dot3(jnp.concatenate(products, axis=0), inv[0], inv[1])
        for c in range(2):
            ra[c, rows, :] = found[c * LANES : (c + 1) * LANES]
            rb[c, rows, :] = found[(2 + c) * LANES : (3 + c) * LANES]

    for i in range(leaves // LANES):
        pair_group(i, (rings.second, rings.third)[i] if i < 2 else lambda: None)
    for c in range(2):
        next_vel[c] = (
            field[:, c * LANES : (c + 1) * LANES]
            + spread_rows(first_row_ref[1:2, :], ra[c])
            - spread_rows(second_row_ref[1:2, :], rb[c])
        )
    rings.finish()


def shape(*sizes, dtype=f32):
    return jax.ShapeDtypeStruct(sizes, dtype)


def anywhere():
    return pl.BlockSpec(memory_space=pl.ANY)


def call(kernel, out_shape, in_specs, out_specs, scratch, **kw):
    return pl.pallas_call(
        kernel,
        out_shape=out_shape,
        in_specs=in_specs,
        out_specs=out_specs,
        scratch_shapes=scratch,
        compiler_params=pltpu.CompilerParams(vmem_limit_bytes=48 * 2**20, **kw),
    )


def run_local(offsets, gamma, anchor, first, shift, target, source, live):
    leaves = gamma.shape[0]
    groups = lax.axis_size("grp")
    state = (3, leaves, LANES)
    wide = (groups,) + state
    dma = pltpu.SemaphoreType.DMA
    rows = lambda: pltpu.VMEM(state, f32)
    pairs = first.shape
    ints = shape(*pairs, dtype=jnp.int32)
    return call(
        local_kernel,
        (shape(*state), shape(2, leaves, LANES), shape(groups, 8, leaves, dtype=jnp.int32))
        + (ints,) * 4
        + (shape(*wide),) * 3,
        [pl.BlockSpec(memory_space=pltpu.HBM)] * 7 + [sspec()],
        (vspec(),) * 7 + (anywhere(),) * 3,
        [pltpu.VMEM(offsets.shape, f32), pltpu.VMEM(gamma.shape, f32), pltpu.VMEM(anchor.shape, f32)]
        + [pltpu.VMEM(pairs, jnp.int32), pltpu.SMEM(pairs, jnp.int32), pltpu.SMEM(pairs, jnp.int32)]
        + [pltpu.VMEM((groups, 8, leaves), jnp.int32), tiles(3), tiles(3), tiles(2), tiles(2), rows(), rows()]
        + [dma((9,)), dma((2, 12)), dma((2, 12)), dma((groups,)), dma((groups,))],
        collective_id=0,
        has_side_effects=True,
    )(offsets, gamma, anchor, first, shift, target, source, live)[:9]


def run_cross(state, up, down, vel, target, source, live, lists):
    leaves = state.shape[1]
    most = (1 + up.shape[0]) * leaves + LANES
    return call(
        cross_kernel,
        shape(*vel.shape),
        [vspec()] * 4 + [sspec()] * 4,
        vspec(),
        [pltpu.VMEM((2, most, LANES), f32), pltpu.VMEM((3, most, LANES), f32), tiles(2), tiles(3), tiles(2)]
        + [pltpu.VMEM((2, leaves + 8, LANES), f32)],
    )(state, up, down, vel, target, source, live, lists)


def run_cross_waves(spread, up, down, vel, target, source, live, lists, tables):
    leaves = vel.shape[1]
    groups = up.shape[0]
    most = (1 + groups) * leaves + 8
    fwd, gam, inv, lat, own = tables
    return call(
        cross_waves,
        shape(*vel.shape),
        [vspec()] * 4 + [sspec()] * 4 + [anywhere()] * 3 + [vspec()],
        vspec(),
        [pltpu.VMEM((most, LANES), f32), pltpu.VMEM((most, LANES), f32), pltpu.VMEM((2, most, LANES), f32)]
        + [pltpu.VMEM((2, leaves + 8, LANES), f32), pltpu.VMEM((2, groups, leaves, LANES), f32)]
        + [pltpu.VMEM(t.shape, bf16) for t in (fwd, gam, inv)]
        + [pltpu.SemaphoreType.DMA((3,))],
    )(spread, up, down, vel, target, source, live, lists, fwd, gam, inv, lat)


def run_regroup(step, vel, shifted, gamma, anchor, dest, *more):
    last = step == STEPS - 1
    leaves = vel.shape[1]
    groups, strips = lax.axis_size("grp"), lax.axis_size("strip")
    dma = pltpu.SemaphoreType.DMA
    box = (strips, 3, LANES)
    in_specs = [vspec()] * 5
    scratch = [tile(), tile(), tile(), pltpu.VMEM((4, WX, LANES), f32), tile(), pltpu.VMEM((leaves, LANES), f32)]
    scratch += [pltpu.VMEM(box, f32), pltpu.VMEM(box, f32), dma, dma, dma]
    if last:
        out_shape = [shape(leaves, LANES), shape(2, leaves)]
        scratch += [pltpu.VMEM((leaves, LANES), f32)]
    else:
        block = (leaves + 8, LANES)
        wide = (groups,) + block
        out_shape = [shape(*block), shape(leaves, LANES), shape(2, leaves, LANES), shape(*wide), shape(*wide)]
        in_specs += [sspec(), sspec(), vspec(), vspec()] + [anywhere()] * 3 + [vspec(), anywhere()]
        rows = lambda n: pltpu.VMEM((n, leaves, LANES), f32)
        scratch += [pltpu.VMEM(wide, f32), rows(2), rows(2), pltpu.VMEM((leaves, LANES), f32)]
        scratch += [pltpu.VMEM(more[i].shape, bf16) for i in (4, 5, 6, 8)]
        scratch += [dma((2, 12)), dma((2, 12)), dma((4,))]
    return call(
        functools.partial(regroup_kernel, step),
        tuple(out_shape),
        in_specs,
        (vspec(),) * len(out_shape),
        scratch,
        collective_id=1 + step,
        has_side_effects=True,
    )(vel, shifted, gamma, anchor, dest, *more)


def on_device(
    offsets,
    circulation,
    window_anchor,
    local_first,
    local_offset,
    cross_target,
    cross_source,
    cross_count,
    destination,
):
    anchor = window_anchor.T
    dest = destination.transpose(0, 2, 1)
    tables = [jnp.asarray(t) for t in fourier_tables()]
    live = cross_count.T
    state, vel, inbox, first, second, target, source, up, down = run_local(
        offsets, circulation, anchor, local_first, local_offset, cross_target, cross_source, live
    )
    lists = (target, source, live, inbox)
    vel = run_cross(state, up, down, vel, *lists)
    block, spread, vel, up, down = run_regroup(
        0, vel, offsets, circulation, anchor, dest, first, second, first, second, *tables
    )
    vel = run_cross_waves(spread, up, down, vel, *lists, tables)
    gamma, anchor = run_regroup(1, vel, block, block, spread, dest)
    return gamma, anchor.T


def solution(mesh):
    rows = P(("strip", "grp"))
    lists = P(None, ("strip", "grp"))
    return jax.shard_map(
        on_device,
        mesh=mesh,
        in_specs=(rows, rows, rows, lists, lists, lists, lists, lists, lists),
        out_specs=(rows, rows),
        check_vma=False,
    )
```

time: 141 us -> 119 us (0.84)
  the two profiles are of different devices: /device:TPU:19 before, /device:TPU:1 now
where the time goes in v3:
time: 119 us
  Pallas kernels  111 us (93%)
  local copies, waits for them, and re-layouts  7.2 us (6%)
    pallas_call x2, Pallas kernels, run_regroup(): call(functools.partial(regroup_kernel, step), tuple(out_shape), in_specs,...  69.2 us
    pallas_call x1, Pallas kernels, run_local(): call(local_kernel, (shape(*state), shape(2, leaves, LANES), shape(groups,...  32.9 us
    unnamed x36, local copies, waits for them, and re-layouts  7.2 us
    pallas_call x1, Pallas kernels, run_cross(): call(cross_kernel, shape(*vel.shape), [vspec()] * 4 + [sspec()] * 4, vspe...  4.41 us
    pallas_call x1, Pallas kernels, run_cross_waves(): call(cross_waves, shape(*vel.shape), [vspec()] * 4 + [sspec()] * 4 + [any...  3.99 us

profile of v3, /device:TPU:1, one launch (start us, length us, event | category | flops | bytes accessed | tf_op | source)
XLA Modules:
  0.0 118.5 jit_solution(11800168880832574918)
XLA Ops:
  0.6 0.0 copy-start.1
  0.6 0.9 copy-done.1
  1.6 0.9 copy-done.5
  2.5 0.7 copy-done.9
  3.2 0.7 copy-done.11
  3.8 0.7 copy-done.13
  4.5 0.7 copy-done.14
  5.2 0.7 copy-done.15
  5.9 0.7 copy-done.16
  6.6 32.9 %shard_map.149 = (f32[3,256,128]{2,1,0:T(8,128)S(1)}, f32[2,256,128]{2,1,0:T(8,128)S(1)}, s32[4,8,256]{2,1,0:T(8,128)S(1)}, s32[2,256]{1,0:T(2,128)S(1)}, s32[2,...) custom-call(f32[256,2,128]{2,1,0:T(2,128)S(1)} %copy-done.1, ...), custom_call_target="tpu_custom_call" | custom-call | tf_op jit(solution)/shard_map/pallas_call | solution.py:860
  39.5 0.0 copy-start
  39.5 0.0 copy-start.2
  39.5 0.0 copy-start.3
  39.5 0.0 copy-start.4
  39.5 0.0 copy-start.6
  39.5 0.0 copy-start.7
  39.6 0.0 copy-start.8
  39.6 0.0 copy-start.10
  39.6 4.4 %shard_map.150.refs_0_ = f32[2,256,128]{2,1,0:T(8,128)S(1)} custom-call(f32[3,256,128]{2,1,0:T(8,128)S(1)} %get-tuple-element.18.state_ref, f32[4,3,256,128]{3,2,1,0:T(8,128)S(1)} %get-tuple-element.19.up_ref, f32[4,3,256,128]{3,2,1,0:T(8,128)S(1)} %get-tuple-element.20.down_ref, f32[2,256,128]{2,1,0:T(8,128)S(1)} %get-tuple-element.21.vel_in_ref, ...), custom_call_target="tpu_custom_call" | custom-call | tf_op jit(solution)/shard_map/pallas_call | solution.py:879
  44.1 48.1 %shard_map.151 = (f32[264,128]{1,0:T(8,128)S(1)}, f32[256,128]{1,0:T(8,128)S(1)}, f32[2,256,128]{2,1,0:T(8,128)S(1)}, f32[4,264,128]{2,1,0:T(8,128)S(1)}, f32[4,264,128]{2,1,0:T(8,128)S(1)}) custom-call(f32[2,256,128]{2,1,0:T(8,128)S(1)} %shard_map.150.refs_0_, f32[256,2,128]{2,1,0:T(2,128)S(1)} %copy-done.2, f32[256,128]{1,0:T(8,128)S(1)} %copy-done.6, ...), custom_call_target="tpu_custom_call" | custom-call | tf_op jit(solution)/shard_map/pallas_call | solution.py:927
  92.2 4.0 %shard_map.152.refs_0_ = f32[2,256,128]{2,1,0:T(8,128)S(1)} custom-call(f32[256,128]{1,0:T(8,128)S(1)} %get-tuple-element.27.spread_ref.refs_3_, f32[4,264,128]{2,1,0:T(8,128)S(1)} %get-tuple-element.28.up_ref, f32[4,264,128]{2,1,0:T(8,128)S(1)} %get-tuple-element.29.down_ref, f32[2,256,128]{2,1,0:T(8,128)S(1)} %get-tuple-element.30.vel_in_ref, ...), custom_call_target="tpu_custom_call" | custom-call | tf_op jit(solution)/shard_map/pallas_call | solution.py:894
  96.2 21.1 %shard_map.153 = (f32[256,128]{1,0:T(8,128)S(1)}, f32[2,256]{1,0:T(2,128)S(1)}) custom-call(f32[2,256,128]{2,1,0:T(8,128)S(1)} %shard_map.152.refs_0_, f32[264,128]{1,0:T(8,128)S(1)} %get-tuple-element.31.refs_1_.refs_2_, f32[264,128]{1,0:T(8,128)S(1)} %get-tuple-element.31.refs_1_.refs_2_, f32[256,128]{1,0:T(8,128)S(1)} %get-tuple-element.27.spread_ref.refs_3_, ...), custom_call_target="tpu_custom_call" | custom-call | tf_op jit(solution)/shard_map/pallas_call | solution.py:927
  117.3 0.7 copy.18
  118.0 0.6 copy.19
  (17 shorter events, 0.0 us)
Async XLA Ops:
  0.6 1.0 copy-start.1
  1.6 0.9 copy-start.5
  2.5 0.7 copy-start.9
  3.2 0.7 copy-start.11
  3.8 0.7 copy-start.13
  4.5 0.7 copy-start.14
  5.2 0.7 copy-start.15
  5.9 0.7 copy-start.16
  39.5 4.5 %copy-start = (bf16[2,512,512]{2,1,0:T(8,128)(2,1)S(1)}, bf16[2,512,512]{2,1,0:T(8,128)(2,1)}, u32[]{:S(2)}) copy-start(bf16[2,512,512]{2,1,0:T(8,128)(2,1)} %constant.10.clone.refs_9_.fwd_in) | copy-start | bytes 3145732
  39.5 4.5 %copy-start.2 = (f32[256,2,128]{2,1,0:T(2,128)S(1)}, f32[256,2,128]{2,1,0:T(2,128)}, u32[]{:S(2)}) copy-start(f32[256,2,128]{2,1,0:T(2,128)} %refs_1_.1) | copy-start | bytes 786436
  39.5 4.5 %copy-start.3 = (bf16[2,512,128]{2,1,0:T(8,128)(2,1)S(1)}, bf16[2,512,128]{2,1,0:T(8,128)(2,1)}, u32[]{:S(2)}) copy-start(bf16[2,512,128]{2,1,0:T(8,128)(2,1)} %constant.12.clone.refs_11_.inv_in) | copy-start | bytes 786436
  39.5 4.5 %copy-start.4 = (bf16[2,128,512]{2,1,0:T(8,128)(2,1)S(1)}, bf16[2,128,512]{2,1,0:T(8,128)(2,1)}, u32[]{:S(2)}) copy-start(bf16[2,128,512]{2,1,0:T(8,128)(2,1)} %constant.11.clone.refs_10_.gam_in) | copy-start | bytes 786436
  39.5 4.5 %copy-start.6 = (f32[256,128]{1,0:T(8,128)S(1)}, f32[256,128]{1,0:T(8,128)}, u32[]{:S(2)}) copy-start(f32[256,128]{1,0:T(8,128)} %refs_2_.1) | copy-start | bytes 393220
  39.5 4.5 %copy-start.7 = (bf16[2,128,256]{2,1,0:T(8,128)(2,1)S(1)}, bf16[2,128,256]{2,1,0:T(8,128)(2,1)}, u32[]{:S(2)}) copy-start(bf16[2,128,256]{2,1,0:T(8,128)(2,1)} %constant.14.clone.refs_13_) | copy-start | bytes 393220
  39.6 4.5 %copy-start.8 = (f32[8,512]{1,0:T(8,128)S(1)}, f32[8,512]{1,0:T(8,128)}, u32[]{:S(2)}) copy-start(f32[8,512]{1,0:T(8,128)} %constant.13.clone.refs_12_.lat) | copy-start | bytes 49156
  39.6 4.5 %copy-start.10 = (s32[2,256,1]{1,2,0:T(1,128)S(1)}, s32[2,256,1]{1,2,0:T(1,128)}, u32[]{:S(2)}) copy-start(s32[2,256,1]{1,2,0:T(1,128)} %param.22) | copy-start | bytes 6148
  44.1 48.1 %copy-start.12 = (s32[2,1]{0,1:T(1,128)S(1)}, s32[2,1]{0,1:T(1,128)}, u32[]{:S(2)}) copy-start(s32[2,1]{0,1:T(1,128)} %param.21) | copy-start | bytes 28

commit v4 on v3

--- a/solution.py
+++ b/solution.py
@@ -240,36 +240,54 @@
     return dot(hot, hi) + dot(hot, lo)
 
 
+def places(index_row):
+    n = index_row.shape[1]
+    return onehot(lax.broadcasted_iota(jnp.int32, (n, n), 0) == index_row)
+
+
 def spread_rows(index_row, x):
-    leaves = index_row.shape[1]
-    places = lax.broadcasted_iota(jnp.int32, (leaves, leaves), 0)
-    return dot_near(onehot(places == index_row), x)
+    return dot_near(places(index_row), x)
+
+
+def pick_columns(x, hot):
+    hi = x.astype(bf16)
+    mid, lo = split(x - hi.astype(f32))
+    return (dot(hi, hot) + dot(mid, hot)) + dot(lo, hot)
+
+
+def spread_columns(x, hot):
+    dims = (((1,), (1,)), ((), ()))
+    hi, lo = split(x)
+    return lax.dot_general(hi, hot, dims, preferred_element_type=f32) + lax.dot_general(
+        lo, hot, dims, preferred_element_type=f32
+    )
 
 
 def earlier(n):
     return onehot(lax.broadcasted_iota(jnp.int32, (n, n), 0) < lax.broadcasted_iota(jnp.int32, (n, n), 1))
 
 
-def sort_lists(target_ref, source_ref, live_ref, outbox):
+def sort_lists(ints_ref, outbox):
     groups = outbox.shape[0]
-    n = target_ref.shape[1]
+    n = ints_ref.shape[1]
     before = earlier(n)
     rows8 = lax.broadcasted_iota(jnp.int32, (8, n), 0)
-    places = lax.broadcasted_iota(jnp.int32, (n, n), 0)
+    slots = lax.broadcasted_iota(jnp.int32, (n, n), 0)
     k = lax.broadcasted_iota(jnp.int32, (1, n), 1)
     outbox[...] = jnp.zeros_like(outbox)
     for step in range(STEPS):
-        source = source_ref[step : step + 1, :]
+        target = ints_ref[4 + step : 5 + step, :]
+        source = ints_ref[6 + step : 7 + step, :]
         owner = lax.shift_right_logical(source, n.bit_length() - 1)
-        key = jnp.where(k < live_ref[0, step], owner, groups)
+        key = jnp.where(k < ints_ref[8 + step : 9 + step, :], owner, groups)
         row = jnp.bitwise_and(source, n - 1)
         mine = jnp.where(rows8 == key, 1.0, 0.0)
         place = jnp.sum(mine * dot(mine.astype(bf16), before), axis=0, keepdims=True).astype(jnp.int32)
-        values = jnp.where(rows8 == 0, target_ref[step : step + 1, :], jnp.where(rows8 == 1, row, 0))
+        values = jnp.where(rows8 == 0, target, jnp.where(rows8 == 1, row, 0))
         values = values.astype(f32).astype(bf16)
         count = jnp.sum(mine, axis=1, keepdims=True).astype(jnp.int32)
         for b in range(groups):
-            hot = onehot((places == place) & (key == b))
+            hot = onehot((slots == place) & (key == b))
             found = lax.dot_general(values, hot, (((1,), (1,)), ((), ())), preferred_element_type=f32)
             outbox[b, 2 * step : 2 * step + 2, :] = found[0:2, :].astype(jnp.int32)
             outbox[b, 4 + step : 5 + step, :] = jnp.broadcast_to(count[b : b + 1, :], (1, n))
@@ -368,54 +386,29 @@
     offset_in,
     gamma_in,
     anchor_in,
-    first_in,
-    shift_in,
-    target_in,
-    source_in,
-    live_ref,
+    ints_ref,
     state_ref,
     vel_ref,
     lists_ref,
-    first_out,
-    second_out,
-    target_ref,
-    source_ref,
     up_ref,
     down_ref,
     own_ref,
     offset_ref,
     gamma_ref,
     anchor_ref,
-    shift_ref,
-    first_ref,
-    second_ref,
     outbox,
-    ta,
-    tb,
+    turned,
+    pa,
+    pb,
     oa,
     ob,
-    ra,
-    rb,
     load_sem,
     send_sem,
     recv_sem,
     list_send,
     list_recv,
 ):
-    loaded = load_tables(
-        [
-            (offset_in, offset_ref),
-            (gamma_in, gamma_ref),
-            (anchor_in, anchor_ref),
-            (first_in, first_out),
-            (shift_in, shift_ref),
-            (target_in, target_ref),
-            (source_in, source_ref),
-            (first_in, first_ref),
-            (shift_in, second_ref),
-        ],
-        load_sem,
-    )
+    loaded = load_tables([(offset_in, offset_ref), (gamma_in, gamma_ref), (anchor_in, anchor_ref)], load_sem)
     leaves = gamma_ref.shape[0]
     blocks = range(leaves // LANES)
     part = lambda ref, start, size, *member: ref.at[(*member, slice(None), pl.ds(start, size))]
@@ -430,7 +423,6 @@
     for j in range(groups):
         pl.semaphore_signal(barrier, inc=1, device_id={"strip": ring.below, "grp": j})
     loaded()
-    second_out[...] = jnp.bitwise_and(first_out[...] + shift_ref[...], leaves - 1)
     for h in blocks:
         rows = pl.ds(h * LANES, LANES)
         for c in range(2):
@@ -439,7 +431,7 @@
         state_ref[2, rows, :] = gamma_ref[rows, :]
     pl.semaphore_wait(barrier, 3 + groups)
     rings.first()
-    sort_lists(target_ref, source_ref, live_ref, outbox)
+    sort_lists(ints_ref, outbox)
     mail = []
     for j in range(groups):
         peer = lax.rem(ring.grp + j, groups)
@@ -453,61 +445,44 @@
         copy.start()
         mail.append(copy)
 
-    def self_group(i, carry):
-        rows = pl.ds(pl.multiple_of(i * LANES, LANES), LANES)
+    for h in blocks:
+        rows = pl.ds(h * LANES, LANES)
         for c in range(3):
-            ta[c] = state_ref[c, rows, :].T
-        one_sided_lanes((ta.at[0], ta.at[1]), (ta.at[0], ta.at[1], ta.at[2]), (oa.at[0], oa.at[1]))
-        vel_ref[0, rows, :] = oa[0].T * -biot_factor
-        vel_ref[1, rows, :] = oa[1].T * biot_factor
-        return carry
-
-    def pair_group(i, between):
-        base = i * LANES
-        rows = pl.ds(base, LANES)
-
-        def fetch(k):
-            first = first_ref[0, base + k]
-            second = jnp.bitwise_and(first + second_ref[0, base + k], leaves - 1)
-            for c in range(3):
-                ra[c, pl.ds(base + k, 1), :] = state_ref[c, pl.ds(first, 1), :]
-                rb[c, pl.ds(base + k, 1), :] = state_ref[c, pl.ds(second, 1), :]
-
-        loop8(LANES, fetch)
-        for c in range(3):
-            ta[c] = ra[c, rows, :].T
-            tb[c] = rb[c, rows, :].T
-        mutual_lanes(
-            [ta.at[c] for c in range(3)],
-            [tb.at[c] for c in range(3)],
-            [oa.at[c] for c in range(2)],
-            [ob.at[c] for c in range(2)],
-            between,
-        )
-        ra[0, rows, :] = oa[0].T * -biot_factor
-        ra[1, rows, :] = oa[1].T * biot_factor
-        rb[0, rows, :] = ob[0].T * biot_factor
-        rb[1, rows, :] = ob[1].T * -biot_factor
-
-    lax.fori_loop(0, leaves // LANES, self_group, 0)
-    rings.second()
-    for i in blocks:
-        pair_group(i, rings.third if i == 0 else lambda: None)
-    for c in range(2):
-        vel_ref[c] += spread_rows(first_out[0:1, :], ra[c]) + spread_rows(second_out[0:1, :], rb[c])
+            turned[h, c] = state_ref[c, rows, :].T
+    views = lambda ref, h, n: [ref.at[h, c] for c in range(n)]
+    for h in blocks:
+        one_sided_lanes(views(turned, h, 2), views(turned, h, 3), views(vel_ref, h, 2))
+        rings.rings[h].second()
+    first = ints_ref[0:1, :]
+    hot_a = places(first)
+    hot_b = places(jnp.bitwise_and(first + ints_ref[2:3, :], leaves - 1))
+    for c in range(3):
+        whole = jnp.concatenate([turned[h, c] for h in blocks], axis=1)
+        for ref, hot in ((pa, hot_a), (pb, hot_b)):
+            picked = pick_columns(whole, hot)
+            for h in blocks:
+                ref[h, c] = picked[:, h * LANES : (h + 1) * LANES]
+    for h in blocks:
+        between = rings.third if h == 0 else lambda: None
+        mutual_lanes(views(pa, h, 3), views(pb, h, 3), views(oa, h, 2), views(ob, h, 2), between)
+    for c, sign in ((0, -biot_factor), (1, biot_factor)):
+        on_a, on_b = [jnp.concatenate([ref[h, c] for h in blocks], axis=1) for ref in (oa, ob)]
+        pairs = spread_columns(on_a, hot_a) - spread_columns(on_b, hot_b)
+        for h in blocks:
+            vel_ref[h, c] = (vel_ref[h, c] + pairs[:, h * LANES : (h + 1) * LANES]) * sign
     rings.finish()
     for copy in mail:
         copy.wait()
 
 
-def walk(target_ref, source_ref, live_ref, lists_ref, leaves, step, visit):
-    live = live_ref[0, step]
+def walk(ints_ref, lists_ref, leaves, step, visit):
+    live = ints_ref[8 + step, 0]
     shift = leaves.bit_length() - 1
 
     def mine(k):
-        source = source_ref[step, k]
+        source = ints_ref[6 + step, k]
         block, row = lax.shift_right_logical(source, shift), jnp.bitwise_and(source, leaves - 1)
-        visit(k, jnp.where(k < live, target_ref[step, k], leaves), 0, block, row)
+        visit(k, jnp.where(k < live, ints_ref[4 + step, k], leaves), 0, block, row)
 
     loop8(live, mine)
     base = live
@@ -523,11 +498,10 @@
     return base
 
 
-def cross_kernel(state_ref, up_ref, down_ref, vel_in_ref, target_ref, source_ref, live_ref, lists_ref, vel_ref, ra, rb, ta, tb, oa, total_ref):
+def cross_kernel(state_ref, up_ref, down_ref, ints_ref, lists_ref, vel_ref, ra, rb, ta, tb, oa, total_ref):
     leaves = state_ref.shape[1]
     sides = (up_ref, down_ref)
-    for c in range(2):
-        total_ref[c, pl.ds(0, leaves), :] = vel_in_ref[c]
+    total_ref[...] = jnp.zeros_like(total_ref)
 
     def fetch(n, leaf, side, block, row):
         own = jnp.minimum(leaf, leaves - 1)
@@ -536,7 +510,7 @@
         for c in range(3):
             rb[c, pl.ds(n, 1), :] = sides[side][block, c, pl.ds(row, 1), :]
 
-    total = walk(target_ref, source_ref, live_ref, lists_ref, leaves, 0, fetch)
+    total = walk(ints_ref, lists_ref, leaves, 0, fetch)
 
     def pair_group(i, carry):
         rows = pl.ds(pl.multiple_of(i * LANES, LANES), LANES)
@@ -574,7 +548,7 @@
         for c in range(2):
             total_ref[c, pl.ds(leaf, 1), :] += ra[c, pl.ds(n, 1), :]
 
-    walk(target_ref, source_ref, live_ref, lists_ref, leaves, 0, spread)
+    walk(ints_ref, lists_ref, leaves, 0, spread)
     for c in range(2):
         vel_ref[c] = total_ref[c, pl.ds(0, leaves), :]
 
@@ -618,9 +592,7 @@
     up_ref,
     down_ref,
     vel_in_ref,
-    target_ref,
-    source_ref,
-    live_ref,
+    ints_ref,
     lists_ref,
     fwd_in,
     gam_in,
@@ -657,7 +629,7 @@
         own = jnp.minimum(leaf, leaves - 1)
         rd[pl.ds(n, 1), :] = spread_ref[pl.ds(own, 1), :] - far_anc[side, block, pl.ds(row, 1), :]
 
-    total = walk(target_ref, source_ref, live_ref, lists_ref, leaves, 1, fetch)
+    total = walk(ints_ref, lists_ref, leaves, 1, fetch)
     ready()
 
     def pair_group(i, carry):
@@ -678,7 +650,7 @@
         for c in range(2):
             total_ref[c, pl.ds(leaf, 1), :] += ra[c, pl.ds(n, 1), :]
 
-    walk(target_ref, source_ref, live_ref, lists_ref, leaves, 1, spread)
+    walk(ints_ref, lists_ref, leaves, 1, spread)
     for c in range(2):
         vel_ref[c] = total_ref[c, pl.ds(0, leaves), :]
 
@@ -690,7 +662,7 @@
     vel_ref, shift_ref, g_ref, anchor_ref, dest_ref = take(5)
     leaves = vel_ref.shape[1]
     if not last:
-        first_ref, second_ref, first_row_ref, second_row_ref, fwd_in, gam_in, inv_in, lat, own_in = take(9)
+        turned_ref, ints_ref, list_ref, fwd_in, gam_in, inv_in, lat, own_in = take(8)
         block, spread_ref, next_vel, up_ref, down_ref = take(5)
     else:
         gamma_ref, final_ref = take(2)
@@ -727,7 +699,8 @@
                 node = jnp.bitwise_and(node, WY - 1) if c else lax.shift_right_logical(node, WY.bit_length() - 1)
                 dst[...] = node.astype(f32) + (time_step * vel_ref[c, rows, :]).T
             else:
-                dst[...] = (shift_ref[rows, c, :] + time_step * vel_ref[c, rows, :]).T
+                moved = (shift_ref[rows, c, :] + time_step * vel_ref[c, rows, :]).T
+                dst[...] = moved + time_step * turned_ref[i, c]
         pg[...] = g_ref[rows, :].T
         remesh_lanes(px, py, pg, wx, out)
         nodes[rows, :] = out[...].T
@@ -796,8 +769,9 @@
         base = i * LANES
 
         def fetch(k):
-            first = pl.ds(first_ref[1, base + k], 1)
-            second = pl.ds(second_ref[1, base + k], 1)
+            start = list_ref[1, base + k]
+            first = pl.ds(start, 1)
+            second = pl.ds(jnp.bitwise_and(start + list_ref[3, base + k], leaves - 1), 1)
             row = pl.ds(base + k, 1)
             ra[0, row, :] = block[first, :]
             rb[0, row, :] = block[second, :]
@@ -820,11 +794,13 @@
 
     for i in range(leaves // LANES):
         pair_group(i, (rings.second, rings.third)[i] if i < 2 else lambda: None)
+    first = ints_ref[1:2, :]
+    second = jnp.bitwise_and(first + ints_ref[3:4, :], leaves - 1)
     for c in range(2):
         next_vel[c] = (
             field[:, c * LANES : (c + 1) * LANES]
-            + spread_rows(first_row_ref[1:2, :], ra[c])
-            - spread_rows(second_row_ref[1:2, :], rb[c])
+            + spread_rows(first, ra[c])
+            - spread_rows(second, rb[c])
         )
     rings.finish()
 
@@ -837,56 +813,51 @@
     return pl.BlockSpec(memory_space=pl.ANY)
 
 
-def call(kernel, out_shape, in_specs, out_specs, scratch, **kw):
+def call(kernel, out_shape, in_specs, out_specs, scratch, vmem=48, **kw):
     return pl.pallas_call(
         kernel,
         out_shape=out_shape,
         in_specs=in_specs,
         out_specs=out_specs,
         scratch_shapes=scratch,
-        compiler_params=pltpu.CompilerParams(vmem_limit_bytes=48 * 2**20, **kw),
+        compiler_params=pltpu.CompilerParams(vmem_limit_bytes=vmem * 2**20, **kw),
     )
 
 
-def run_local(offsets, gamma, anchor, first, shift, target, source, live):
+def run_local(offsets, gamma, anchor, ints):
     leaves = gamma.shape[0]
     groups = lax.axis_size("grp")
     state = (3, leaves, LANES)
     wide = (groups,) + state
     dma = pltpu.SemaphoreType.DMA
-    rows = lambda: pltpu.VMEM(state, f32)
-    pairs = first.shape
-    ints = shape(*pairs, dtype=jnp.int32)
+    cols = lambda n: pltpu.VMEM((leaves // LANES, n, LANES, LANES), f32)
     return call(
         local_kernel,
-        (shape(*state), shape(2, leaves, LANES), shape(groups, 8, leaves, dtype=jnp.int32))
-        + (ints,) * 4
-        + (shape(*wide),) * 3,
-        [pl.BlockSpec(memory_space=pltpu.HBM)] * 7 + [sspec()],
-        (vspec(),) * 7 + (anywhere(),) * 3,
+        (shape(*state), shape(leaves // LANES, 2, LANES, LANES), shape(groups, 8, leaves, dtype=jnp.int32)) + (shape(*wide),) * 3,
+        [pl.BlockSpec(memory_space=pltpu.HBM)] * 3 + [vspec()],
+        (vspec(),) * 3 + (anywhere(),) * 3,
         [pltpu.VMEM(offsets.shape, f32), pltpu.VMEM(gamma.shape, f32), pltpu.VMEM(anchor.shape, f32)]
-        + [pltpu.VMEM(pairs, jnp.int32), pltpu.SMEM(pairs, jnp.int32), pltpu.SMEM(pairs, jnp.int32)]
-        + [pltpu.VMEM((groups, 8, leaves), jnp.int32), tiles(3), tiles(3), tiles(2), tiles(2), rows(), rows()]
-        + [dma((9,)), dma((2, 12)), dma((2, 12)), dma((groups,)), dma((groups,))],
+        + [pltpu.VMEM((groups, 8, leaves), jnp.int32), cols(3), cols(3), cols(3), cols(2), cols(2)]
+        + [dma((3,)), dma((2, 12)), dma((2, 12)), dma((groups,)), dma((groups,))],
         collective_id=0,
         has_side_effects=True,
-    )(offsets, gamma, anchor, first, shift, target, source, live)[:9]
-
-
-def run_cross(state, up, down, vel, target, source, live, lists):
+    )(offsets, gamma, anchor, ints)[:5]
+
+
+def run_cross(state, up, down, ints, lists):
     leaves = state.shape[1]
     most = (1 + up.shape[0]) * leaves + LANES
     return call(
         cross_kernel,
-        shape(*vel.shape),
-        [vspec()] * 4 + [sspec()] * 4,
+        shape(2, leaves, LANES),
+        [vspec()] * 3 + [sspec()] * 2,
         vspec(),
         [pltpu.VMEM((2, most, LANES), f32), pltpu.VMEM((3, most, LANES), f32), tiles(2), tiles(3), tiles(2)]
         + [pltpu.VMEM((2, leaves + 8, LANES), f32)],
-    )(state, up, down, vel, target, source, live, lists)
-
-
-def run_cross_waves(spread, up, down, vel, target, source, live, lists, tables):
+    )(state, up, down, ints, lists)
+
+
+def run_cross_waves(spread, up, down, vel, ints, lists, tables):
     leaves = vel.shape[1]
     groups = up.shape[0]
     most = (1 + groups) * leaves + 8
@@ -894,13 +865,13 @@
     return call(
         cross_waves,
         shape(*vel.shape),
-        [vspec()] * 4 + [sspec()] * 4 + [anywhere()] * 3 + [vspec()],
+        [vspec()] * 4 + [sspec()] * 2 + [anywhere()] * 3 + [vspec()],
         vspec(),
         [pltpu.VMEM((most, LANES), f32), pltpu.VMEM((most, LANES), f32), pltpu.VMEM((2, most, LANES), f32)]
         + [pltpu.VMEM((2, leaves + 8, LANES), f32), pltpu.VMEM((2, groups, leaves, LANES), f32)]
         + [pltpu.VMEM(t.shape, bf16) for t in (fwd, gam, inv)]
         + [pltpu.SemaphoreType.DMA((3,))],
-    )(spread, up, down, vel, target, source, live, lists, fwd, gam, inv, lat)
+    )(spread, up, down, vel, ints, lists, fwd, gam, inv, lat)
 
 
 def run_regroup(step, vel, shifted, gamma, anchor, dest, *more):
@@ -919,10 +890,10 @@
         block = (leaves + 8, LANES)
         wide = (groups,) + block
         out_shape = [shape(*block), shape(leaves, LANES), shape(2, leaves, LANES), shape(*wide), shape(*wide)]
-        in_specs += [sspec(), sspec(), vspec(), vspec()] + [anywhere()] * 3 + [vspec(), anywhere()]
+        in_specs += [vspec(), vspec(), sspec()] + [anywhere()] * 3 + [vspec(), anywhere()]
         rows = lambda n: pltpu.VMEM((n, leaves, LANES), f32)
         scratch += [pltpu.VMEM(wide, f32), rows(2), rows(2), pltpu.VMEM((leaves, LANES), f32)]
-        scratch += [pltpu.VMEM(more[i].shape, bf16) for i in (4, 5, 6, 8)]
+        scratch += [pltpu.VMEM(more[i].shape, bf16) for i in (3, 4, 5, 7)]
         scratch += [dma((2, 12)), dma((2, 12)), dma((4,))]
     return call(
         functools.partial(regroup_kernel, step),
@@ -948,17 +919,15 @@
 ):
     anchor = window_anchor.T
     dest = destination.transpose(0, 2, 1)
+    live = jnp.broadcast_to(cross_count, local_first.shape)
+    ints = jnp.concatenate([local_first, local_offset, cross_target, cross_source, live, live, live, live], axis=0)
     tables = [jnp.asarray(t) for t in fourier_tables()]
-    live = cross_count.T
-    state, vel, inbox, first, second, target, source, up, down = run_local(
-        offsets, circulation, anchor, local_first, local_offset, cross_target, cross_source, live
+    state, turned, inbox, up, down = run_local(offsets, circulation, anchor, ints)
+    vel = run_cross(state, up, down, ints, inbox)
+    block, spread, vel, up, down = run_regroup(
+        0, vel, offsets, circulation, anchor, dest, turned, ints, ints, *tables
     )
-    lists = (target, source, live, inbox)
-    vel = run_cross(state, up, down, vel, *lists)
-    block, spread, vel, up, down = run_regroup(
-        0, vel, offsets, circulation, anchor, dest, first, second, first, second, *tables
-    )
-    vel = run_cross_waves(spread, up, down, vel, *lists, tables)
+    vel = run_cross_waves(spread, up, down, vel, ints, inbox, tables)
     gamma, anchor = run_regroup(1, vel, block, block, spread, dest)
     return gamma, anchor.T
 

time: 119 us -> 117 us (0.983)
  local copies, waits for them, and re-layouts: 7.2 us -> 5.31 us
    pallas_call x3, Pallas kernels: 41.3 us -> 47.9 us  [the longest x1 30.3 us: run_local(): call(local_kernel, (shape(*state), shape(leaves // LANES, 2, LANES, LANES...]
    pallas_call x2, Pallas kernels: 69.2 us -> 63.2 us  [run_regroup(): call(functools.partial(regroup_kernel, step), tuple(out_shape), in_specs,...]
    unnamed x36 -> x24, local copies, waits for them, and re-layouts: 7.2 us -> 3.82 us
where the time goes in v4:
time: 117 us
  Pallas kernels  111 us (95%)
  local copies, waits for them, and re-layouts  5.31 us (5%)
    pallas_call x2, Pallas kernels, run_regroup(): call(functools.partial(regroup_kernel, step), tuple(out_shape), in_specs,...  63.2 us
    pallas_call x1, Pallas kernels, run_local(): call(local_kernel, (shape(*state), shape(leaves // LANES, 2, LANES, LANES...  30.3 us
    pallas_call x1, Pallas kernels, run_cross(): call(cross_kernel, shape(2, leaves, LANES), [vspec()] * 3 + [sspec()] * 2...  9.18 us
    pallas_call x1, Pallas kernels, run_cross_waves(): call(cross_waves, shape(*vel.shape), [vspec()] * 4 + [sspec()] * 2 + [any...  8.37 us
    unnamed x24, local copies, waits for them, and re-layouts  3.82 us

profile of v4, /device:TPU:1, one launch (start us, length us, event | category | flops | bytes accessed | tf_op | source)
XLA Modules:
  0.0 117.1 jit_solution(5421266360670749627)
XLA Ops:
  0.6 0.7 broadcast_in_dim.8
  1.4 0.8 concatenate.3.ints_ref.refs_6_.refs_7_
  2.1 0.9 copy-done.3
  3.1 0.9 copy-done.5
  4.0 0.7 copy-done.9
  4.7 30.3 %shard_map.149 = (f32[3,256,128]{2,1,0:T(8,128)S(1)}, f32[2,2,128,128]{3,2,1,0:T(8,128)S(1)}, s32[4,8,256]{2,1,0:T(8,128)S(1)}, f32[4,3,256,128]{3,2,1,0:T(8,128...) custom-call(f32[256,2,128]{2,1,0:T(2,128)S(1)} %copy-done.3, f32[256,128]{1,0:T(8,128)S(1)} %copy-done.5, ...), custom_call_target="tpu_custom_call" | custom-call | tf_op jit(solution)/shard_map/pallas_call | solution.py:834
  35.0 0.0 copy-start
  35.0 0.0 copy-start.1
  35.0 0.0 copy-start.2
  35.0 0.0 copy-start.4
  35.0 0.0 copy-start.6
  35.0 0.0 copy-start.7
  35.1 0.0 copy-start.8
  35.1 0.0 copy-start.10
  35.1 9.2 %shard_map.150.refs_0_ = f32[2,256,128]{2,1,0:T(8,128)S(1)} custom-call(f32[3,256,128]{2,1,0:T(8,128)S(1)} %get-tuple-element.14.state_ref, f32[4,3,256,128]{3,2,1,0:T(8,128)S(1)} %get-tuple-element.15.up_ref, f32[4,3,256,128]{3,2,1,0:T(8,128)S(1)} %get-tuple-element.16.down_ref, s32[16,256]{1,0:T(8,128)S(1)} %concatenate.3.ints_ref.refs_6_.refs_7_, ...), custom_call_target="tpu_custom_call" | custom-call | tf_op jit(solution)/shard_map/pallas_call | solution.py:850
  44.3 0.0 copy-done
  44.3 0.0 copy-done.1
  44.3 0.0 copy-done.2
  44.3 0.0 copy-done.4
  44.3 45.4 %shard_map.151 = (f32[264,128]{1,0:T(8,128)S(1)}, f32[256,128]{1,0:T(8,128)S(1)}, f32[2,256,128]{2,1,0:T(8,128)S(1)}, f32[4,264,128]{2,1,0:T(8,128)S(1)}, f32[4,264,128]{2,1,0:T(8,128)S(1)}) custom-call(f32[2,256,128]{2,1,0:T(8,128)S(1)} %shard_map.150.refs_0_, f32[256,2,128]{2,1,0:T(2,128)S(1)} %copy-done.4, f32[256,128]{1,0:T(8,128)S(1)} %copy-done.6, ...), custom_call_target="tpu_custom_call" | custom-call | tf_op jit(solution)/shard_map/pallas_call | solution.py:898
  89.8 8.4 %shard_map.152.refs_0_ = f32[2,256,128]{2,1,0:T(8,128)S(1)} custom-call(f32[256,128]{1,0:T(8,128)S(1)} %get-tuple-element.19.spread_ref.refs_3_, f32[4,264,128]{2,1,0:T(8,128)S(1)} %get-tuple-element.20.up_ref, f32[4,264,128]{2,1,0:T(8,128)S(1)} %get-tuple-element.21.down_ref, f32[2,256,128]{2,1,0:T(8,128)S(1)} %get-tuple-element.22.vel_in_ref, ...), custom_call_target="tpu_custom_call" | custom-call | tf_op jit(solution)/shard_map/pallas_call | solution.py:865
  98.2 17.7 %shard_map.153 = (f32[256,128]{1,0:T(8,128)S(1)}, f32[2,256]{1,0:T(2,128)S(1)}) custom-call(f32[2,256,128]{2,1,0:T(8,128)S(1)} %shard_map.152.refs_0_, f32[264,128]{1,0:T(8,128)S(1)} %get-tuple-element.23.refs_1_.refs_2_, f32[264,128]{1,0:T(8,128)S(1)} %get-tuple-element.23.refs_1_.refs_2_, f32[256,128]{1,0:T(8,128)S(1)} %get-tuple-element.19.spread_ref.refs_3_, ...), custom_call_target="tpu_custom_call" | custom-call | tf_op jit(solution)/shard_map/pallas_call | solution.py:898
  115.9 0.7 copy.18
  116.6 0.6 copy.19
  (7 shorter events, 0.0 us)
Async XLA Ops:
  2.1 0.9 copy-start.3
  3.1 0.9 copy-start.5
  4.0 0.7 copy-start.9
  35.0 9.3 %copy-start = (bf16[2,512,512]{2,1,0:T(8,128)(2,1)S(1)}, bf16[2,512,512]{2,1,0:T(8,128)(2,1)}, u32[]{:S(2)}) copy-start(bf16[2,512,512]{2,1,0:T(8,128)(2,1)} %constant.10.clone.refs_8_.fwd_in) | copy-start | bytes 3145732
  35.0 9.3 %copy-start.1 = (bf16[2,512,128]{2,1,0:T(8,128)(2,1)S(1)}, bf16[2,512,128]{2,1,0:T(8,128)(2,1)}, u32[]{:S(2)}) copy-start(bf16[2,512,128]{2,1,0:T(8,128)(2,1)} %constant.12.clone.refs_10_.inv_in) | copy-start | bytes 786436
  35.0 9.3 %copy-start.2 = (bf16[2,128,512]{2,1,0:T(8,128)(2,1)S(1)}, bf16[2,128,512]{2,1,0:T(8,128)(2,1)}, u32[]{:S(2)}) copy-start(bf16[2,128,512]{2,1,0:T(8,128)(2,1)} %constant.11.clone.refs_9_.gam_in) | copy-start | bytes 786436
  35.0 9.3 %copy-start.4 = (f32[256,2,128]{2,1,0:T(2,128)S(1)}, f32[256,2,128]{2,1,0:T(2,128)}, u32[]{:S(2)}) copy-start(f32[256,2,128]{2,1,0:T(2,128)} %refs_1_.1) | copy-start | bytes 786436
  35.0 9.3 %copy-start.6 = (f32[256,128]{1,0:T(8,128)S(1)}, f32[256,128]{1,0:T(8,128)}, u32[]{:S(2)}) copy-start(f32[256,128]{1,0:T(8,128)} %refs_2_.1) | copy-start | bytes 393220
  35.0 9.3 %copy-start.7 = (bf16[2,128,256]{2,1,0:T(8,128)(2,1)S(1)}, bf16[2,128,256]{2,1,0:T(8,128)(2,1)}, u32[]{:S(2)}) copy-start(bf16[2,128,256]{2,1,0:T(8,128)(2,1)} %constant.14.clone.refs_12_) | copy-start | bytes 393220
  35.1 9.3 %copy-start.8 = (f32[8,512]{1,0:T(8,128)S(1)}, f32[8,512]{1,0:T(8,128)}, u32[]{:S(2)}) copy-start(f32[8,512]{1,0:T(8,128)} %constant.13.clone.refs_11_.lat) | copy-start | bytes 49156
  35.1 9.3 %copy-start.10 = (s32[2,256,1]{1,2,0:T(1,128)S(1)}, s32[2,256,1]{1,2,0:T(1,128)}, u32[]{:S(2)}) copy-start(s32[2,256,1]{1,2,0:T(1,128)} %param.22) | copy-start | bytes 6148

commit v5 on v4

--- a/solution.py
+++ b/solution.py
@@ -195,33 +195,30 @@
     zero = jnp.zeros((8, LANES), f32)
 
     def over_a(ia, carry):
-        a0 = pl.multiple_of(ia * 8, 8)
-
-        def over_b(chunk, u, acc):
+        a0 = pl.multiple_of(ia * 16, 16)
+
+        def over_b(ib, acc):
             acc = list(acc)
-            rows = pl.ds(pl.multiple_of(chunk * 64 + u * 8, 8), 8)
+            rows = pl.ds(ib * 8, 8)
             xb, yb, gb = xb_ref[rows, :], yb_ref[rows, :], gb_ref[rows, :]
-            for r in range(8):
+            for r in range(16):
                 row = pl.ds(a0 + r, 1)
                 dx = xa_ref[row, :] - xb
                 dy = ya_ref[row, :] - yb
                 w = gb * recip(dx * dx + (dy * dy + 1.0))
                 acc[r] = acc[r] + dy * w
-                acc[8 + r] = acc[8 + r] + dx * w
+                acc[16 + r] = acc[16 + r] + dx * w
             return tuple(acc)
 
-        def over_chunk(chunk, acc):
-            for u in range(8):
-                acc = over_b(chunk, u, acc)
-            return acc
-
-        acc = lax.fori_loop(0, chunks, over_chunk, (zero,) * 16)
-        for r in range(8):
+        acc = (zero,) * 32
+        for ib in range(8 * chunks):
+            acc = over_b(ib, acc)
+        for r in range(16):
             ua_ref[pl.ds(a0 + r, 1), :] = jnp.sum(acc[r], axis=0, keepdims=True)
-            va_ref[pl.ds(a0 + r, 1), :] = jnp.sum(acc[8 + r], axis=0, keepdims=True)
+            va_ref[pl.ds(a0 + r, 1), :] = jnp.sum(acc[16 + r], axis=0, keepdims=True)
         return carry
 
-    lax.fori_loop(0, 16, over_a, 0)
+    lax.fori_loop(0, LANES // 16, over_a, 0)
 
 
 def onehot(condition):
@@ -530,12 +527,16 @@
             ta[c] = ra[c, rows, :].T
         for c in range(3):
             tb[c] = rb[c, rows, :].T
-        one_sided_lanes(
-            [ta.at[c] for c in range(2)],
-            [tb.at[c] for c in range(3)],
-            [oa.at[c] for c in range(2)],
-            jnp.where(few, 1, 2),
-        )
+        views = [[ref.at[c] for c in range(n)] for ref, n in ((ta, 2), (tb, 3), (oa, 2))]
+
+        @pl.when(few)
+        def _():
+            one_sided_lanes(*views, 1)
+
+        @pl.when(jnp.logical_not(few))
+        def _():
+            one_sided_lanes(*views)
+
         for c, sign in ((0, -biot_factor), (1, biot_factor)):
             found = oa[c].T * sign
             ra[c, rows, :] = found

time: 117 us -> 117 us (level)
    pallas_call x2, Pallas kernels: 63.2 us -> 70 us  [run_regroup(): call(functools.partial(regroup_kernel, step), tuple(out_shape), in_specs,...]
    pallas_call x1, Pallas kernels: 8.37 us -> 3.88 us  [run_cross_waves(): call(cross_waves, shape(*vel.shape), [vspec()] * 4 + [sspec()] * 2 + [any...]
    pallas_call x1, Pallas kernels: 9.18 us -> 6.22 us  [run_cross(): call(cross_kernel, shape(2, leaves, LANES), [vspec()] * 3 + [sspec()] * 2...]
where the time goes in v5:
time: 117 us; the launch traced here: 116 us
  Pallas kernels  110 us (94%)
  local copies, waits for them, and re-layouts  5.31 us (5%)
    pallas_call x2, Pallas kernels, run_regroup(): call(functools.partial(regroup_kernel, step), tuple(out_shape), in_specs,...  70 us
    pallas_call x1, Pallas kernels, run_local(): call(local_kernel, (shape(*state), shape(leaves // LANES, 2, LANES, LANES...  30.1 us
    pallas_call x1, Pallas kernels, run_cross(): call(cross_kernel, shape(2, leaves, LANES), [vspec()] * 3 + [sspec()] * 2...  6.22 us
    pallas_call x1, Pallas kernels, run_cross_waves(): call(cross_waves, shape(*vel.shape), [vspec()] * 4 + [sspec()] * 2 + [any...  3.88 us
    unnamed x24, local copies, waits for them, and re-layouts  3.82 us

profile of v5, /device:TPU:1, one launch (start us, length us, event | category | flops | bytes accessed | tf_op | source)
XLA Modules:
  0.0 116.3 jit_solution(1424346105618910128)
XLA Ops:
  0.6 0.7 broadcast_in_dim.8
  1.4 0.8 concatenate.3.ints_ref.refs_6_.refs_7_
  2.1 0.9 copy-done.3
  3.1 0.9 copy-done.5
  4.0 0.7 copy-done.9
  4.7 30.1 %shard_map.149 = (f32[3,256,128]{2,1,0:T(8,128)S(1)}, f32[2,2,128,128]{3,2,1,0:T(8,128)S(1)}, s32[4,8,256]{2,1,0:T(8,128)S(1)}, f32[4,3,256,128]{3,2,1,0:T(8,128...) custom-call(f32[256,2,128]{2,1,0:T(2,128)S(1)} %copy-done.3, f32[256,128]{1,0:T(8,128)S(1)} %copy-done.5, ...), custom_call_target="tpu_custom_call" | custom-call | tf_op jit(solution)/shard_map/pallas_call | solution.py:835
  34.7 0.0 copy-start
  34.8 0.0 copy-start.1
  34.8 0.0 copy-start.2
  34.8 0.0 copy-start.4
  34.8 0.0 copy-start.6
  34.8 0.0 copy-start.7
  34.8 0.0 copy-start.8
  34.8 0.0 copy-start.10
  34.8 6.2 %shard_map.150.refs_0_ = f32[2,256,128]{2,1,0:T(8,128)S(1)} custom-call(f32[3,256,128]{2,1,0:T(8,128)S(1)} %get-tuple-element.14.state_ref, f32[4,3,256,128]{3,2,1,0:T(8,128)S(1)} %get-tuple-element.15.up_ref, f32[4,3,256,128]{3,2,1,0:T(8,128)S(1)} %get-tuple-element.16.down_ref, s32[16,256]{1,0:T(8,128)S(1)} %concatenate.3.ints_ref.refs_6_.refs_7_, ...), custom_call_target="tpu_custom_call" | custom-call | tf_op jit(solution)/shard_map/pallas_call | solution.py:851
  41.1 0.0 copy-done
  41.1 0.0 copy-done.1
  41.1 0.0 copy-done.2
  41.1 0.0 copy-done.4
  41.1 49.0 %shard_map.151 = (f32[264,128]{1,0:T(8,128)S(1)}, f32[256,128]{1,0:T(8,128)S(1)}, f32[2,256,128]{2,1,0:T(8,128)S(1)}, f32[4,264,128]{2,1,0:T(8,128)S(1)}, f32[4,264,128]{2,1,0:T(8,128)S(1)}) custom-call(f32[2,256,128]{2,1,0:T(8,128)S(1)} %shard_map.150.refs_0_, f32[256,2,128]{2,1,0:T(2,128)S(1)} %copy-done.4, f32[256,128]{1,0:T(8,128)S(1)} %copy-done.6, ...), custom_call_target="tpu_custom_call" | custom-call | tf_op jit(solution)/shard_map/pallas_call | solution.py:899
  90.1 3.9 %shard_map.152.refs_0_ = f32[2,256,128]{2,1,0:T(8,128)S(1)} custom-call(f32[256,128]{1,0:T(8,128)S(1)} %get-tuple-element.19.spread_ref.refs_3_, f32[4,264,128]{2,1,0:T(8,128)S(1)} %get-tuple-element.20.up_ref, f32[4,264,128]{2,1,0:T(8,128)S(1)} %get-tuple-element.21.down_ref, f32[2,256,128]{2,1,0:T(8,128)S(1)} %get-tuple-element.22.vel_in_ref, ...), custom_call_target="tpu_custom_call" | custom-call | tf_op jit(solution)/shard_map/pallas_call | solution.py:866
  94.0 21.0 %shard_map.153 = (f32[256,128]{1,0:T(8,128)S(1)}, f32[2,256]{1,0:T(2,128)S(1)}) custom-call(f32[2,256,128]{2,1,0:T(8,128)S(1)} %shard_map.152.refs_0_, f32[264,128]{1,0:T(8,128)S(1)} %get-tuple-element.23.refs_1_.refs_2_, f32[264,128]{1,0:T(8,128)S(1)} %get-tuple-element.23.refs_1_.refs_2_, f32[256,128]{1,0:T(8,128)S(1)} %get-tuple-element.19.spread_ref.refs_3_, ...), custom_call_target="tpu_custom_call" | custom-call | tf_op jit(solution)/shard_map/pallas_call | solution.py:899
  115.0 0.7 copy.18
  115.7 0.6 copy.19
  (7 shorter events, 0.0 us)
Async XLA Ops:
  2.1 0.9 copy-start.3
  3.1 0.9 copy-start.5
  4.0 0.7 copy-start.9
  34.7 6.3 %copy-start = (bf16[2,512,512]{2,1,0:T(8,128)(2,1)S(1)}, bf16[2,512,512]{2,1,0:T(8,128)(2,1)}, u32[]{:S(2)}) copy-start(bf16[2,512,512]{2,1,0:T(8,128)(2,1)} %constant.10.clone.refs_8_.fwd_in) | copy-start | bytes 3145732
  34.8 6.3 %copy-start.1 = (bf16[2,512,128]{2,1,0:T(8,128)(2,1)S(1)}, bf16[2,512,128]{2,1,0:T(8,128)(2,1)}, u32[]{:S(2)}) copy-start(bf16[2,512,128]{2,1,0:T(8,128)(2,1)} %constant.12.clone.refs_10_.inv_in) | copy-start | bytes 786436
  34.8 6.3 %copy-start.2 = (bf16[2,128,512]{2,1,0:T(8,128)(2,1)S(1)}, bf16[2,128,512]{2,1,0:T(8,128)(2,1)}, u32[]{:S(2)}) copy-start(bf16[2,128,512]{2,1,0:T(8,128)(2,1)} %constant.11.clone.refs_9_.gam_in) | copy-start | bytes 786436
  34.8 6.3 %copy-start.4 = (f32[256,2,128]{2,1,0:T(2,128)S(1)}, f32[256,2,128]{2,1,0:T(2,128)}, u32[]{:S(2)}) copy-start(f32[256,2,128]{2,1,0:T(2,128)} %refs_1_.1) | copy-start | bytes 786436
  34.8 6.3 %copy-start.6 = (f32[256,128]{1,0:T(8,128)S(1)}, f32[256,128]{1,0:T(8,128)}, u32[]{:S(2)}) copy-start(f32[256,128]{1,0:T(8,128)} %refs_2_.1) | copy-start | bytes 393220
  34.8 6.3 %copy-start.7 = (bf16[2,128,256]{2,1,0:T(8,128)(2,1)S(1)}, bf16[2,128,256]{2,1,0:T(8,128)(2,1)}, u32[]{:S(2)}) copy-start(bf16[2,128,256]{2,1,0:T(8,128)(2,1)} %constant.14.clone.refs_12_) | copy-start | bytes 393220
  34.8 6.3 %copy-start.8 = (f32[8,512]{1,0:T(8,128)S(1)}, f32[8,512]{1,0:T(8,128)}, u32[]{:S(2)}) copy-start(f32[8,512]{1,0:T(8,128)} %constant.13.clone.refs_11_.lat) | copy-start | bytes 49156
  34.8 6.3 %copy-start.10 = (s32[2,256,1]{1,2,0:T(1,128)S(1)}, s32[2,256,1]{1,2,0:T(1,128)}, u32[]{:S(2)}) copy-start(s32[2,256,1]{1,2,0:T(1,128)} %param.22) | copy-start | bytes 6148
